TPU v7x, 512 devices: a whole 4x4x16 slice. The times are simulated.
512 devices in a mesh: row: 16 (over z_lo, core), col: 32 (over z_hi, y, x).
Axes of the slice: x: 4, y: 4, z: 16 (z_hi: 2, z_lo: 8; z = z_hi * 8 + z_lo), core: 2. Of those that a mesh axis runs over, the one named last changes fastest.
Arguments:
- inverse_anc: bfloat16 [2, 16384, 16384], P(None, 'row', 'col'), may hold values from -6 to 6
- lower_panel: bfloat16 [2, 8, 16, 256, 256], P(None, None, 'row', 'col'), may hold values from -0.125 to 0.125
- diag_inverse: float32 [2, 8, 256, 256], P(None, None, 'row'), may hold values from -6 to 6
- structure: int32 [8, 16], replicated, may hold values from 0 to 63, as said below
Outputs:
- upper_inverse: bfloat16 [2, 8, 256, 16384], P(None, None, 'row', 'col')
- diag_block: float32 [2, 8, 256, 256], P(None, None, 'row')
Inputs may be any that keep to these rules, and one draw needn't show every extreme that they name: Entry r of a supernode's structure is a block from r * 4 to (r + 1) * 4 - 1.
All inputs are finite; a program needn't handle non-finite values.
Results may differ from a plain program's by a relative error of at most 0.0028.
Values may be sent and summed in bfloat16 or wider, within the bound.
No kernel may reach another device: no remote copies, remote signals or barrier semaphores. Data moves between devices by JAX's collectives and lax.ppermute only.
A program may use at most 64 MiB of HBM per device.

v0:
```python
import jax
import jax.numpy as jnp
from jax import lax
from jax.sharding import PartitionSpec as P


def from_root(value, axis, source):
    kept = jnp.where(lax.axis_index(axis) == source, value, 0).astype(value.dtype)
    return lax.psum(kept, axis)


def send_down(own_block, source_entry):
    return from_root(own_block, "row", source_entry)


def row_sums(parts):
    return lax.psum_scatter(parts, "row", scatter_dimension=2, tiled=True)


def shards(inverse_anc, lower_panel, diag_inverse, structure):
    width = lower_panel.shape[4]
    nsup = lower_panel.shape[1]
    band = inverse_anc.shape[1] // width
    col_band = inverse_anc.shape[2] // width
    my_row = lax.axis_index("row")
    my_col = lax.axis_index("col")
    gathered = lax.all_gather(lower_panel, "col", axis=3, tiled=True)
    own_block = gathered[:, :, 0]
    own_slot = jnp.take(structure, my_row, axis=1)
    local_row = own_slot - band * my_row
    row_blocks = inverse_anc.reshape(2, band, width, col_band * width)
    picked_rows = jnp.take(row_blocks, local_row, axis=1)
    source_entry = my_col * col_band // band
    far_slot = jnp.take(structure, source_entry, axis=1)
    present = far_slot // col_band == my_col
    local_col = far_slot - col_band * my_col
    selector = (local_col[:, None] == jnp.arange(col_band, dtype=jnp.int32)[None, :]) & present[
        :, None
    ]
    picked = picked_rows.reshape(2, nsup, width, col_band, width)
    chosen = jnp.sum(picked * selector.astype(jnp.bfloat16)[None, :, None, :, None], axis=3)
    form = "kba,kbc->kac"
    lreal = own_block[0]
    limag = own_block[1]
    real = jnp.einsum(form, lreal, chosen[0], preferred_element_type=jnp.float32)
    real = real - jnp.einsum(form, limag, chosen[1], preferred_element_type=jnp.float32)
    imag = jnp.einsum(form, lreal, chosen[1], preferred_element_type=jnp.float32)
    imag = imag + jnp.einsum(form, limag, chosen[0], preferred_element_type=jnp.float32)
    summed = row_sums(jnp.stack([real, imag]))
    below = send_down(own_block, source_entry)
    upper_block = (-summed).astype(jnp.bfloat16)
    below = below * present.astype(jnp.bfloat16)[None, :, None, None]
    dform = "kac,kcd->kad"
    dreal = jnp.einsum(dform, upper_block[0], below[0], preferred_element_type=jnp.float32)
    dreal = dreal - jnp.einsum(dform, upper_block[1], below[1], preferred_element_type=jnp.float32)
    dimag = jnp.einsum(dform, upper_block[0], below[1], preferred_element_type=jnp.float32)
    dimag = dimag + jnp.einsum(dform, upper_block[1], below[0], preferred_element_type=jnp.float32)
    total = lax.psum(jnp.stack([dreal, dimag]), "col")
    diag_block = diag_inverse - total
    pieces = []
    for column in range(col_band):
        keep = selector[:, column][None, :, None, None]
        pieces.append(jnp.where(keep, upper_block, jnp.zeros_like(upper_block)))
    upper_inverse = jnp.concatenate(pieces, axis=3)
    return (upper_inverse, diag_block)


def solution(mesh):
    placed = (
        P(None, "row", "col"),
        P(None, None, "row", "col", None),
        P(None, None, "row", None),
        P(),
    )
    return jax.shard_map(
        shards,
        mesh=mesh,
        in_specs=placed,
        out_specs=(P(None, None, "row", "col"), P(None, None, "row", None)),
        check_vma=False,
    )
```

profile of v0, /device:TPU:2, one launch (start us, length us, event | category | flops | bytes accessed | tf_op | source)
XLA Modules:
  0.0 1057.3 jit_solution(5500824122528157433)
XLA Ops:
  7.2 0.0 all-gather.2.cloned.1.call-start
  7.2 0.7 all-gather.2.cloned.1.call-update
  7.9 0.0 all-reduce.3.cloned.1.call-start
  8.0 1.0 select_reduce_fusion.1
  9.0 2.8 gather_fusion
  11.8 6.9 gather.10
  18.7 0.1 copy.13
  18.8 137.5 %all-gather.2.cloned.1.call-done = bf16[2,8,1,256,256]{4,3,1,2,0:T(8,128)(2,1)} async-done(((bf16[2,8,1,8,256]{4,3,1,2,0:T(8,128)(2,1)}), bf16[2,8,1,256,256]{4,3,1,2,0:T(8,128)(2,1)}) %all-gather.2.cloned.1.call-update) | async-done | bytes 2097168 | tf_op jit(solution)/shard_map/all_gather | solution.py:27
  156.3 3.0 select_bitcast_fusion
  159.3 0.0 reduce-scatter.2.cloned.1.call-start
  159.4 10.6 %multiply_reduce_fusion = bf16[2,8,256,256]{3,2,0,1:T(8,128)(2,1)S(1)} fusion(bf16[2,8,256,2,256]{4,3,2,0,1:T(2,128)(2,1)} %gather.10, pred[8]{0:T(512)(128)(4,1)S(1)} %get-tuple-element.24, bf16[8,2]{1,0:T(8,128)(2,1)S(1)} %copy.13), kind=kLoop, calls=%fused_computation.3 | loop fusion | flops 5242880 | bytes 6291496 | tf_op jit(solution)/shard_map/reduce_sum | solution.py:41
  170.0 0.5 fusion.2
  170.5 0.5 subtract_bitcast_fusion
  171.0 0.5 fusion.3
  171.5 0.5 add_bitcast_fusion
  172.0 2.2 pad_maximum_fusion
  174.2 5.5 copy.17
  179.7 0.0 reduce-scatter.2.cloned.1.call-update
  179.7 0.0 all-reduce.5.cloned.1.call-start
  179.8 178.9 %all-reduce.3.cloned.1.call-done = bf16[2,8,256,256]{3,2,1,0:T(8,128)(2,1)} async-done(((bf16[2,8,256,256]{3,2,1,0:T(8,128)(2,1)}), bf16[2,8,256,256]{3,2,1,0:T(8,128)(2,1)}) %all-reduce.3.cloned.1.call-update) | async-done | bytes 2097168 | tf_op jit(solution)/shard_map/psum | solution.py:9
  358.7 3.1 broadcast_multiply_fusion
  361.8 113.6 %reduce-scatter.2.cloned.1.call-done = f32[2,8,16,256]{3,1,0,2:T(8,128)} async-done(((f32[2,8,256,256]{3,1,0,2:T(8,128)}), f32[2,8,16,256]{3,1,0,2:T(8,128)}) %reduce-scatter.2.cloned.1.call-update) | async-done | bytes 262160 | tf_op jit(solution)/shard_map/reduce_scatter | solution.py:17
  475.5 1.3 broadcast_select_fusion.2
  476.7 1.5 fusion.4
  478.2 1.5 fusion.5
  479.7 0.3 fusion.1
  480.0 0.3 fusion
  480.2 0.7 pad_maximum_fusion.2
  481.0 0.1 broadcast_select_fusion.1
  481.1 0.7 pad_maximum_fusion.1
  481.8 567.3 %all-reduce.5.cloned.1.call-done = f32[2,8,16,256]{3,2,1,0:T(8,128)} async-done(((f32[2,8,16,256]{3,2,1,0:T(8,128)}), f32[2,8,16,256]{3,2,1,0:T(8,128)}) %all-reduce.5.cloned.1.call-update) | async-done | bytes 262160 | tf_op jit(solution)/shard_map/psum | solution.py:58
  1049.1 1.7 sub.41
  (16 shorter events, 0.1 us)
Async XLA Ops:
  7.2 1.8 copy-start
  7.2 149.1 %all-gather.2.cloned.1.call-start = ((), (), s32[]{:S(2)}) async-start(), calls=%async_computation.1 | async-start | bytes 2162688 | tf_op jit(solution)/shard_map/all_gather | solution.py:27
  7.9 350.8 %all-reduce.3.cloned.1.call-start = ((), (), s32[]{:S(2)}) async-start(), calls=%async_computation.3 | async-start | bytes 4194304 | tf_op jit(solution)/shard_map/psum | solution.py:9
  159.3 316.1 %reduce-scatter.2.cloned.1.call-start = ((), (), s32[]{:S(2)}) async-start(), calls=%async_computation.2 | async-start | bytes 4456448 | tf_op jit(solution)/shard_map/reduce_scatter | solution.py:17
  159.4 10.6 %copy-start.2 = (bf16[2,8,1,256,256]{4,3,1,2,0:T(8,128)(2,1)S(1)}, bf16[2,8,1,256,256]{4,3,1,2,0:T(8,128)(2,1)}, u32[]{:S(2)}) copy-start(bf16[2,8,1,256,256]{4,3,1,2,0:T(8,128)(2,1)} %all-gather.2.cloned.1.call-done) | copy-start | bytes 6291460
  179.7 869.4 %all-reduce.5.cloned.1.call-start = ((), (), s32[]{:S(2)}) async-start(), calls=%async_computation.4 | async-start | bytes 524288 | tf_op jit(solution)/shard_map/psum | solution.py:58
  475.5 4.2 copy-start.1
  479.7 569.4 %copy-start.3 = (f32[2,8,16,256]{3,2,1,0:T(8,128)S(1)}, f32[2,8,16,256]{3,2,1,0:T(8,128)}, u32[]{:S(2)}) copy-start(f32[2,8,16,256]{3,2,1,0:T(8,128)} %param.8) | copy-start | bytes 786436
Sparse Core Ops, SparseCore 0:
  12.1 144.1 all-gather.1
  159.5 199.1 all-reduce.2
  361.6 113.8 reduce-scatter.1
  481.1 567.9 all-reduce.4
where the time goes:
time: 1060 us
  waiting for transfers between devices  998 us (94%)
  other arithmetic  24.5 us (2%)
  local copies, waits for them, and re-layouts  15.3 us (1%)
  between operations  13.9 us (1%)
    psum x1, waiting for transfers between devices, shards(): total = lax.psum(jnp.stack([dreal, dimag]), 'col')  567 us
    psum x1, waiting for transfers between devices, from_root(): return lax.psum(kept, axis)  179 us
    all_gather x1, waiting for transfers between devices, shards(): gathered = lax.all_gather(lower_panel, 'col', axis=3, tiled=True)  137 us
    reduce_scatter x1, waiting for transfers between devices, row_sums(): return lax.psum_scatter(parts, 'row', scatter_dimension=2, tiled=True)  114 us
  transfers between devices with their start and end apart: 4, of which 4 were waited for; matrix products, arithmetic and copies ran while one was open for 3% of the time, Pallas kernels for 0%

commit v1 on v0

v1 whole, which is shorter than its diff:
```python
import functools

import jax
import jax.numpy as jnp
from jax import lax
from jax.experimental import pallas as pl
from jax.experimental.pallas import tpu as pltpu
from jax.sharding import Mesh, PartitionSpec as P

BF = jnp.bfloat16
F32 = jnp.float32
ROW = ("za", "zb", "zc", "core")
COL = ("zh", "y", "xa", "h")
PLANE = ("y", "xa", "h")
VMEM_LIMIT = 48 * 1024 * 1024


def params():
    return pltpu.CompilerParams(vmem_limit_bytes=VMEM_LIMIT)


def whole(count):
    return [pl.BlockSpec(memory_space=pltpu.VMEM)] * count


def block_row(k, st, ids):
    return st[k, ids[0]] - 4 * ids[0]


def block_col(k, st, ids):
    return lax.rem(st[k, ids[1] // 2], 2)


def present(k, st, ids):
    return st[k, ids[1] // 2] // 2 == ids[1]


def pick_kernel(st, ids, block, out):
    out[:, 0] = block[...]


def pick_far_half(inverse_anc, structure, ids):
    def at(k, st, ids):
        half = 1 - lax.rem(ids[1], 2)
        return (0, block_row(k, st, ids), 2 * block_col(k, st, ids) + half)

    return pl.pallas_call(
        pick_kernel,
        grid_spec=pltpu.PrefetchScalarGridSpec(
            num_scalar_prefetch=2,
            grid=(8,),
            in_specs=[pl.BlockSpec((2, 256, 128), at)],
            out_specs=pl.BlockSpec((2, 1, 256, 128), lambda k, st, ids: (0, k, 0, 0)),
        ),
        out_shape=jax.ShapeDtypeStruct((2, 8, 256, 128), BF),
        compiler_params=params(),
    )(structure, ids, inverse_anc)


def merge_kernel(st, ids, block, got, out):
    k = pl.program_id(0)
    mine = present(k, st, ids)

    @pl.when(mine)
    def _():
        out[:, 0] = block[...]

    @pl.when(jnp.logical_not(mine))
    def _():
        out[...] = got[...]


def merge_halves(inverse_anc, got, structure, ids):
    def at(k, st, ids):
        half = lax.rem(ids[1], 2)
        return (0, block_row(k, st, ids), 2 * block_col(k, st, ids) + half)

    slab = pl.BlockSpec((2, 1, 256, 128), lambda k, st, ids: (0, k, 0, 0))
    return pl.pallas_call(
        merge_kernel,
        grid_spec=pltpu.PrefetchScalarGridSpec(
            num_scalar_prefetch=2,
            grid=(8,),
            in_specs=[pl.BlockSpec((2, 256, 128), at), slab],
            out_specs=slab,
        ),
        out_shape=jax.ShapeDtypeStruct((2, 8, 256, 128), BF),
        compiler_params=params(),
    )(structure, ids, inverse_anc, got)


def lanes_kernel(panel, out):
    x = panel[...].astype(F32).reshape(128, 256).astype(BF)
    src = lax.broadcasted_iota(jnp.int32, (256, 256), 0)
    dst = lax.broadcasted_iota(jnp.int32, (256, 256), 1)
    t = src % 16
    core = (src // 16) % 2
    zc = (src // 32) % 2
    zab = src // 64
    place = core * 128 + zc * 64 + zab * 16 + t
    perm = jnp.where(place == dst, 1.0, 0.0).astype(BF)
    y = jnp.dot(x, perm, preferred_element_type=F32)
    for c in range(2):
        half = y[:, 128 * c : 128 * c + 128].reshape(2, 8, 8, 128).astype(BF)
        for z in range(2):
            out[c, z] = half


def split_lanes(panel):
    return pl.pallas_call(
        lanes_kernel,
        in_specs=whole(1),
        out_specs=whole(1)[0],
        out_shape=jax.ShapeDtypeStruct((2, 2, 2, 8, 8, 128), BF),
        compiler_params=params(),
    )(panel)


def product_kernel(ids, panel, own, sib, keep, send):
    core = ids[2]
    upper = ids[3] == 0
    for k in range(8):
        total = None
        for source, blocks in ((core, own), (1 - core, sib)):
            left = []
            for p in range(2):
                part = panel[:, source, :, p, k].astype(F32)
                left.append(jnp.swapaxes(part, 0, 1).reshape(256, 128).astype(BF))
            re = blocks[0, k]
            im = blocks[1, k]
            form = (((0,), (0,)), ((), ()))
            one = lax.dot_general(
                left[0], jnp.concatenate([re, im], axis=1), form, preferred_element_type=F32
            )
            two = lax.dot_general(
                left[1], jnp.concatenate([-im, re], axis=1), form, preferred_element_type=F32
            )
            both = one + two
            total = both if total is None else total + both
        low = total[:64]
        high = total[64:]
        mine = jnp.where(upper, low, high)
        other = jnp.where(upper, high, low)
        for p in range(2):
            keep[p, k] = mine[:, 128 * p : 128 * p + 128]
            send[p, k] = other[:, 128 * p : 128 * p + 128]


def products(ids, panel, own, sib):
    half = jax.ShapeDtypeStruct((2, 8, 64, 128), F32)
    return pl.pallas_call(
        product_kernel,
        in_specs=[pl.BlockSpec(memory_space=pltpu.SMEM)] + whole(3),
        out_specs=whole(2),
        out_shape=[half, half],
        compiler_params=params(),
    )(ids, panel, own, sib)


def diag_kernel(keep, got, below, total, out):
    for k in range(8):
        sums = [keep[p, k] + got[p, k] for p in range(2)]
        for p in range(2):
            for z in range(4):
                total[z, p, k] = sums[p][16 * z : 16 * z + 16]
        left = []
        for value in sums:
            high = value.astype(BF)
            left.append(high)
            left.append((value - high.astype(F32)).astype(BF))
        left = jnp.concatenate(left, axis=1)
        panel = []
        for p in range(2):
            part = below[:, :, :, p, k].astype(F32)
            part = part.reshape(2, 2, 2, 2, 8, 256).transpose(3, 1, 2, 0, 4, 5)
            panel.append(part.reshape(128, 256).astype(BF))
        re, im = panel
        right_re = jnp.concatenate([re, re, -im, -im], axis=0)
        right_im = jnp.concatenate([im, im, re, re], axis=0)
        out[k] = jnp.dot(left, right_re, preferred_element_type=F32)
        out[8 + k] = jnp.dot(left, right_im, preferred_element_type=F32)


def diag_terms(keep, got, below):
    return pl.pallas_call(
        diag_kernel,
        in_specs=whole(3),
        out_specs=whole(2),
        out_shape=[
            jax.ShapeDtypeStruct((4, 2, 8, 16, 128), F32),
            jax.ShapeDtypeStruct((16, 64, 256), F32),
        ],
        compiler_params=params(),
    )(keep, got, below)


def spread(value, axes, size):
    copies = jnp.broadcast_to(value[None], (size,) + value.shape)
    return lax.all_to_all(copies, axes, 0, 0, tiled=True)


def shards(inverse_anc, lower_panel, diag_inverse, structure):
    my_row = lax.axis_index(ROW)
    my_col = lax.axis_index(COL)
    ids = jnp.stack([my_row, my_col, lax.axis_index("core"), lax.axis_index("zc")]).astype(jnp.int32)
    own = lower_panel.reshape(2, 8, 8, 256)

    lanes = split_lanes(own)
    lanes = lax.all_to_all(lanes.reshape(4, 2, 8, 8, 128), ("core", "zh"), 0, 0, tiled=True)
    lanes = lanes.reshape(2, 2, 2, 8, 8, 128)
    panel = spread(lanes, PLANE, 16)

    far = pick_far_half(inverse_anc, structure, ids)
    got = lax.ppermute(far, "h", [(0, 1), (1, 0)])
    mine = merge_halves(inverse_anc, got, structure, ids)
    sib = lax.ppermute(mine, "core", [(0, 1), (1, 0)])

    moves = []
    for q in range(16):
        for h in range(2):
            for m in range(16):
                moves.append((q * 32 + 16 * h + m, m * 32 + 2 * q + h))
    below = lax.ppermute(own, ROW + COL, moves)
    below = spread(below, "za", 2)
    below = spread(below, ("zb", "zc"), 4)
    below = spread(below.reshape(8, 2, 8, 8, 256), "core", 2)
    below = below.reshape(2, 4, 2, 2, 8, 8, 256)

    keep, send = products(ids, panel, mine, sib)
    summed = lax.ppermute(send, "zc", [(0, 1), (1, 0)])
    total, terms = diag_terms(keep, summed, below)

    terms = lax.all_to_all(terms, PLANE, 0, 0, tiled=True)
    part = jnp.sum(terms, axis=0).reshape(4, 1, 16, 256)
    part = jnp.broadcast_to(part, (4, 2, 16, 256)).reshape(8, 16, 256)
    part = lax.all_to_all(part, ("za", "zb", "zh"), 0, 0, tiled=True)
    place = lax.axis_index(PLANE)
    start = lax.dynamic_index_in_dim(diag_inverse.reshape(16, 16, 256), place, 0, keepdims=False)
    diag = spread(start + jnp.sum(part, axis=0), PLANE, 16)
    diag_block = diag.reshape(2, 8, 16, 256)

    rows = lax.all_to_all(total, ("za", "zb"), 0, 0, tiled=True)
    half = (-jnp.sum(rows, axis=0)).astype(BF)
    pair = spread(half, "h", 2)
    block = jnp.concatenate([pair[0], pair[1]], axis=-1)
    slots = lax.dynamic_index_in_dim(structure, my_col // 2, 1, keepdims=False)
    pieces = []
    for column in range(2):
        keep_it = (slots == 2 * my_col + column)[None, :, None, None]
        pieces.append(jnp.where(keep_it, block, jnp.zeros_like(block)))
    upper_inverse = jnp.concatenate(pieces, axis=3)
    return upper_inverse, diag_block


def solution(mesh):
    fine = Mesh(mesh.devices.reshape(2, 2, 2, 2, 2, 4, 2, 2), ROW + COL)
    placed = (
        P(None, ROW, COL),
        P(None, None, ROW, COL, None),
        P(None, None, ROW, None),
        P(),
    )
    return jax.shard_map(
        shards,
        mesh=fine,
        in_specs=placed,
        out_specs=(P(None, None, ROW, COL), P(None, None, ROW, None)),
        check_vma=False,
    )
```

time: 1060 us -> 241 us (0.23)
  waiting for transfers between devices: 998 us -> 106 us
  blocking collectives: 0 us -> 60 us
  starting transfers between devices: 0.16 us -> 54.4 us
  other arithmetic: 24.5 us -> 1.95 us
  between operations: 13.9 us -> 0.75 us
    psum x2 -> x0, waiting for transfers between devices: 746 us -> none  [the longest x1 567 us: shards(): total = lax.psum(jnp.stack([dreal, dimag]), 'col')]
    all_gather x1 -> x0, waiting for transfers between devices: 137 us -> none  [shards(): gathered = lax.all_gather(lower_panel, 'col', axis=3, tiled=True)]
    reduce_scatter x1 -> x0, waiting for transfers between devices: 114 us -> none  [row_sums(): return lax.psum_scatter(parts, 'row', scatter_dimension=2, tiled=True)]
    all_to_all x0 -> x6, waiting for transfers between devices: none -> 66.6 us  [the longest x5 41.3 us: spread(): return lax.all_to_all(copies, axes, 0, 0, tiled=True)]
    all_to_all x0 -> x4, blocking collectives: none -> 60 us  [the longest x1 23.5 us: shards(): terms = lax.all_to_all(terms, PLANE, 0, 0, tiled=True)]
    all_to_all x0 -> x6, starting transfers between devices: none -> 41.1 us  [the longest x5 36.6 us: spread(): return lax.all_to_all(copies, axes, 0, 0, tiled=True)]
    ppermute x0 -> x4, waiting for transfers between devices: none -> 39.4 us  [the longest x1 16.4 us: shards(): below = lax.ppermute(own, ROW + COL, moves)]
    ppermute x0 -> x4, starting transfers between devices: none -> 13.3 us  [the longest x1 7.37 us: shards(): summed = lax.ppermute(send, 'zc', [(0, 1), (1, 0)])]
  transfers between devices with their start and end apart: 4 -> 10, of which waited for: 4 -> 9; matrix products, arithmetic and copies ran while one was open for 3% -> 2% of each run, Pallas kernels for 0% -> 3%
where the time goes in v1:
time: 241 us; the launch traced here: 240 us
  waiting for transfers between devices  106 us (44%)
  blocking collectives  60 us (25%)
  starting transfers between devices  54.4 us (23%)
  Pallas kernels  9.4 us (4%)
  local copies, waits for them, and re-layouts  7.48 us (3%)
    all_to_all x5, waiting for transfers between devices, spread(): return lax.all_to_all(copies, axes, 0, 0, tiled=True)  41.3 us
    all_to_all x5, starting transfers between devices, spread(): return lax.all_to_all(copies, axes, 0, 0, tiled=True)  36.6 us
    all_to_all x1, waiting for transfers between devices, shards(): rows = lax.all_to_all(total, ('za', 'zb'), 0, 0, tiled=True)  25.2 us
    all_to_all x1, blocking collectives, shards(): terms = lax.all_to_all(terms, PLANE, 0, 0, tiled=True)  23.5 us
    all_to_all x1, blocking collectives, shards(): lax.all_to_all(lanes.reshape(4, 2, 8, 8, 128), ('core', 'zh'), 0, 0, tile...  16.5 us
    ppermute x1, waiting for transfers between devices, shards(): below = lax.ppermute(own, ROW + COL, moves)  16.4 us
    all_to_all x1, blocking collectives, shards(): part = lax.all_to_all(part, ('za', 'zb', 'zh'), 0, 0, tiled=True)  15.4 us
    ppermute x1, waiting for transfers between devices, shards(): got = lax.ppermute(far, 'h', [(0, 1), (1, 0)])  13.8 us
  transfers between devices with their start and end apart: 10, of which 9 were waited for; matrix products, arithmetic and copies ran while one was open for 2% of the time, Pallas kernels for 3%

profile of v1, /device:TPU:2, one launch (start us, length us, event | category | flops | bytes accessed | tf_op | source)
XLA Modules:
  0.0 239.9 jit_solution(16695237459421047916)
XLA Ops:
  0.6 1.9 collective-permute-start.3
  2.6 16.4 %collective-permute-done.3 = bf16[2,8,8,256]{3,2,1,0:T(8,128)(2,1)S(1)} collective-permute-done((bf16[2,8,8,256]{3,2,1,0:T(8,128)(2,1)}, bf16[2,8,8,256]{3,2,1,0:T(8,128)(2,1)S(1)}, u32[]{:S(2)}, u32[]{:S(2)}) %collective-permute-start.3) | collective-permute-done | bytes 65568 | tf_op jit(solution)/shard_map/ppermute | solution.py:223
  19.6 9.4 %all-to-all-start.2 = ((bf16[2,2,8,8,256]{4,3,2,1,0:T(8,128)(2,1)}), bf16[2,2,8,8,256]{4,3,2,1,0:T(8,128)(2,1)S(1)}, u32[]{:S(2)}, u32[]{:S(2)}) async-start(bf16[2,2,8,8,256]{4,3,2,1,0:T(8,128)(2,1)} %broadcast_in_dim.65), calls=%async_computation.2 | async-start | bytes 262144 | tf_op jit(solution)/shard_map/all_to_all | solution.py:199
  29.0 0.8 copy-done.1
  30.1 10.1 %all-to-all-done.2 = bf16[2,2,8,8,256]{4,3,2,1,0:T(8,128)(2,1)S(1)} async-done(((bf16[2,2,8,8,256]{4,3,2,1,0:T(8,128)(2,1)}), bf16[2,2,8,8,256]{4,3,2,1,0:T(8,128)(2,1)S(1)}, u32[]{:S(2)}, u32[]{:S(2)}) %all-to-all-start.2) | async-done | bytes 131104 | tf_op jit(solution)/shard_map/all_to_all | solution.py:199
  40.2 16.5 %all_to_all.50 = bf16[4,2,8,8,128]{4,3,2,1,0:T(8,128)(2,1)S(1)} all-to-all(bf16[4,2,8,8,128]{4,3,2,1,0:T(8,128)(2,1)S(1)} %bitcast.24), channel_id=1, replica_groups=mesh['za'=2,'zb'=2,'zc'=2,'core'=2,'zh'=2,'y'=4,'xa'=2,'h'=2] {'core','zh'}, dimensions={0} | all-to-all | bytes 262144 | tf_op jit(solution)/shard_map/all_to_all | solution.py:209
  56.7 1.8 broadcast_in_dim.64
  58.6 12.4 %all-to-all-start.1 = ((bf16[16,2,2,2,8,8,128]{6,5,4,3,2,1,0:T(8,128)(2,1)}), bf16[16,2,2,2,8,8,128]{6,5,4,3,2,1,0:T(8,128)(2,1)}, u32[]{:S(2)}, u32[]{:S(2)}) async-start(bf16[16,2,2,2,8,8,128]{6,5,4,3,2,1,0:T(8,128)(2,1)} %broadcast_in_dim.64), calls=%async_computation.1 | async-start | bytes 4194304 | tf_op jit(solution)/shard_map/all_to_all | solution.py:199
  71.0 3.5 %shard_map.60 = bf16[2,8,256,128]{3,2,1,0:T(8,128)(2,1)} custom-call(s32[8,16]{1,0:T(8,128)S(1)} %copy-done.2, s32[4]{0:T(128)S(1)} %pad_add_fusion.ids, bf16[2,1024,512]{2,1,0:T(8,128)(2,1)S(1)} %copy-done), custom_call_target="tpu_custom_call" | custom-call | tf_op jit(solution)/shard_map/pallas_call | solution.py:47
  74.6 2.1 collective-permute-start
  76.6 22.9 %all-to-all-done.1.panel = bf16[16,2,2,2,8,8,128]{6,5,4,3,2,1,0:T(8,128)(2,1)} async-done(((bf16[16,2,2,2,8,8,128]{6,5,4,3,2,1,0:T(8,128)(2,1)}), bf16[16,2,2,2,8,8,128]{6,5,4,3,2,1,0:T(8,128)(2,1)}, u32[]{:S(2)}, u32[]{:S(2)}) %all-to-all-start.1) | async-done | bytes 2097184 | tf_op jit(solution)/shard_map/all_to_all | solution.py:199
  99.5 0.9 broadcast_in_dim.66
  100.4 4.6 %all-to-all-start.3 = ((bf16[4,2,2,8,8,256]{5,4,3,2,1,0:T(8,128)(2,1)}), bf16[4,2,2,8,8,256]{5,4,3,2,1,0:T(8,128)(2,1)}, u32[]{:S(2)}, u32[]{:S(2)}) async-start(bf16[4,2,2,8,8,256]{5,4,3,2,1,0:T(8,128)(2,1)} %broadcast_in_dim.66), calls=%async_computation.3 | async-start | bytes 1048576 | tf_op jit(solution)/shard_map/all_to_all | solution.py:199
  104.9 13.8 %collective-permute-done.got = bf16[2,8,256,128]{3,2,1,0:T(8,128)(2,1)S(1)} collective-permute-done((bf16[2,8,256,128]{3,2,1,0:T(8,128)(2,1)}, bf16[2,8,256,128]{3,2,1,0:T(8,128)(2,1)S(1)}, u32[]{:S(2)}, u32[]{:S(2)}) %collective-permute-start) | collective-permute-done | bytes 1048608 | tf_op jit(solution)/shard_map/ppermute | solution.py:214
  118.8 1.7 shard_map.61.own
  120.5 1.9 collective-permute-start.1
  122.4 2.6 %collective-permute-done.1.sib = bf16[2,8,256,128]{3,2,1,0:T(8,128)(2,1)S(1)} collective-permute-done((bf16[2,8,256,128]{3,2,1,0:T(8,128)(2,1)S(1)}, bf16[2,8,256,128]{3,2,1,0:T(8,128)(2,1)S(1)}, u32[]{:S(2)}, u32[]{:S(2)}) %collective-permute-start.1) | collective-permute-done | bytes 1048608 | tf_op jit(solution)/shard_map/ppermute | solution.py:216
  125.1 2.5 %shard_map.62 = (f32[2,8,64,128]{3,2,1,0:T(8,128)S(1)}, f32[2,8,64,128]{3,2,1,0:T(8,128)S(1)}) custom-call(s32[4]{0:T(128)S(1)} %pad_add_fusion.ids, bf16[16,2,2,2,8,8,128]{6,5,4,3,2,1,0:T(8,128)(2,1)} %all-to-all-done.1.panel, bf16[2,8,256,128]{3,2,1,0:T(8,128)(2,1)S(1)} %shard_map.61.own, bf16[2,8,256,128]{3,2,1,0:T(8,128)(2,1)S(1)} %collective-permute-done.1.sib), custom_call_target="tpu_custom_call" | custom-call | tf_op jit(solution)/shard_map/pallas_call | solution.py:151
  127.6 7.4 %collective-permute-start.2 = (f32[2,8,64,128]{3,2,1,0:T(8,128)S(1)}, f32[2,8,64,128]{3,2,1,0:T(8,128)S(1)}, u32[]{:S(2)}, u32[]{:S(2)}) collective-permute-start(f32[2,8,64,128]{3,2,1,0:T(8,128)S(1)} %get-tuple-element.7), channel_id=1, source_target_pairs={{0,64},{64,0},{1,65},{65,1},{2,66},{66,2},{3,67},{67,3},{4,68},{68... | collective-permute-start | bytes 1572872 | tf_op jit(solution)/shard_map/ppermute | solution.py:230
  135.0 1.2 broadcast_in_dim.68
  136.1 4.6 %all_to_all.51 = bf16[2,8,2,8,8,256]{5,4,3,2,1,0:T(8,128)(2,1)S(1)} all-to-all(bf16[2,8,2,8,8,256]{5,4,3,2,1,0:T(8,128)(2,1)S(1)} %broadcast_in_dim.68), channel_id=1, replica_groups=mesh['za'=2,'zb'=2,'zc'=2,'core'=2,'zh'=2,'y'=4,'xa'=2,'h'=2] {'core'}, dimensions={0} | all-to-all | bytes 2097152 | tf_op jit(solution)/shard_map/all_to_all | solution.py:199
  140.7 6.5 %collective-permute-done.2.got = f32[2,8,64,128]{3,2,1,0:T(8,128)S(1)} collective-permute-done((f32[2,8,64,128]{3,2,1,0:T(8,128)S(1)}, f32[2,8,64,128]{3,2,1,0:T(8,128)S(1)}, u32[]{:S(2)}, u32[]{:S(2)}) %collective-permute-start.2) | collective-permute-done | bytes 524320 | tf_op jit(solution)/shard_map/ppermute | solution.py:230
  147.2 1.4 shard_map.63
  148.6 23.5 %all_to_all.52 = f32[16,64,256]{2,1,0:T(8,128)S(1)} all-to-all(f32[16,64,256]{2,1,0:T(8,128)S(1)} %get-tuple-element.9), channel_id=1, replica_groups=mesh['za'=2,'zb'=2,'zc'=2,'core'=2,'zh'=2,'y'=4,'xa'=2,'h'=2] {'y','xa',..., dimensions={0} | all-to-all | bytes 2097152 | tf_op jit(solution)/shard_map/all_to_all | solution.py:233
  172.2 15.4 %all_to_all.53 = f32[8,16,256]{2,1,0:T(8,128)S(1)} all-to-all(f32[8,16,256]{2,1,0:T(8,128)S(1)} %bitcast.29), channel_id=1, replica_groups=mesh['za'=2,'zb'=2,'zc'=2,'core'=2,'zh'=2,'y'=4,'xa'=2,'h'=2] {'za','zb'..., dimensions={0} | all-to-all | bytes 262144 | tf_op jit(solution)/shard_map/all_to_all | solution.py:236
  187.6 4.5 %all-to-all-start.5 = ((f32[4,2,8,16,128]{4,3,2,1,0:T(8,128)}), f32[4,2,8,16,128]{4,3,2,1,0:T(8,128)S(1)}, u32[]{:S(2)}, u32[]{:S(2)}) async-start(f32[4,2,8,16,128]{4,3,2,1,0:T(8,128)} %get-tuple-element.8), calls=%async_computation.5 | async-start | bytes 1048576 | tf_op jit(solution)/shard_map/all_to_all | solution.py:242
  192.3 25.2 %all-to-all-done.5 = f32[4,2,8,16,128]{4,3,2,1,0:T(8,128)S(1)} async-done(((f32[4,2,8,16,128]{4,3,2,1,0:T(8,128)}), f32[4,2,8,16,128]{4,3,2,1,0:T(8,128)S(1)}, u32[]{:S(2)}, u32[]{:S(2)}) %all-to-all-start.5) | async-done | bytes 524320 | tf_op jit(solution)/shard_map/all_to_all | solution.py:242
  218.3 4.9 %all-to-all-start.6 = ((bf16[2,2,8,16,128]{4,3,2,1,0:T(8,128)(2,1)}), bf16[2,2,8,16,128]{4,3,2,1,0:T(8,128)(2,1)S(1)}, u32[]{:S(2)}, u32[]{:S(2)}) async-start(bf16[2,2,8,16,128]{4,3,2,1,0:T(8,128)(2,1)} %broadcast_in_dim.69), calls=%async_computation.6 | async-start | bytes 262144 | tf_op jit(solution)/shard_map/all_to_all | solution.py:199
  223.9 1.7 all-to-all-done.6
  226.4 5.4 %all-to-all-start.9 = ((f32[16,16,256]{2,1,0:T(8,128)}), f32[16,16,256]{2,1,0:T(8,128)S(1)}, u32[]{:S(2)}, u32[]{:S(2)}) async-start(f32[16,16,256]{2,1,0:T(8,128)} %broadcast_in_dim.74), calls=%async_computation.9 | async-start | bytes 524288 | tf_op jit(solution)/shard_map/all_to_all | solution.py:199
  231.9 0.7 pad_maximum_fusion
  232.6 6.5 %all-to-all-done.9 = f32[16,16,256]{2,1,0:T(8,128)S(1)} async-done(((f32[16,16,256]{2,1,0:T(8,128)}), f32[16,16,256]{2,1,0:T(8,128)S(1)}, u32[]{:S(2)}, u32[]{:S(2)}) %all-to-all-start.9) | async-done | bytes 262176 | tf_op jit(solution)/shard_map/all_to_all | solution.py:199
  (21 shorter events, 4.2 us)
Async XLA Ops:
  0.6 18.3 %collective-permute-start.3 = (bf16[2,8,8,256]{3,2,1,0:T(8,128)(2,1)}, bf16[2,8,8,256]{3,2,1,0:T(8,128)(2,1)S(1)}, u32[]{:S(2)}, u32[]{:S(2)}) collective-permute-start(bf16[2,8,8,256]{3,2,1,0:T(8,128)(2,1)} %bitcast.25), channel_id=1, source_target_pairs={{0,0},{1,32},{2,64},{3,96},{4,128},{5,160},{6,192},{7,224},{8,256}... | collective-permute-start | bytes 196616 | tf_op jit(solution)/shard_map/ppermute | solution.py:223
  19.6 20.6 %all-to-all-start.2 = ((bf16[2,2,8,8,256]{4,3,2,1,0:T(8,128)(2,1)}), bf16[2,2,8,8,256]{4,3,2,1,0:T(8,128)(2,1)S(1)}, u32[]{:S(2)}, u32[]{:S(2)}) async-start(bf16[2,2,8,8,256]{4,3,2,1,0:T(8,128)(2,1)} %broadcast_in_dim.65), calls=%async_computation.2 | async-start | bytes 262144 | tf_op jit(solution)/shard_map/all_to_all | solution.py:199
  29.0 0.8 copy-start.1
  58.5 12.5 %copy-start = (bf16[2,1024,512]{2,1,0:T(8,128)(2,1)S(1)}, bf16[2,1024,512]{2,1,0:T(8,128)(2,1)}, u32[]{:S(2)}) copy-start(bf16[2,1024,512]{2,1,0:T(8,128)(2,1)} %block.3) | copy-start | bytes 6291460
  58.5 12.5 %copy-start.2 = (s32[8,16]{1,0:T(8,128)S(1)}, s32[8,16]{1,0:T(8,128)}, u32[]{:S(2)}) copy-start(s32[8,16]{1,0:T(8,128)} %st.3) | copy-start | bytes 1540
  58.6 41.0 %all-to-all-start.1 = ((bf16[16,2,2,2,8,8,128]{6,5,4,3,2,1,0:T(8,128)(2,1)}), bf16[16,2,2,2,8,8,128]{6,5,4,3,2,1,0:T(8,128)(2,1)}, u32[]{:S(2)}, u32[]{:S(2)}) async-start(bf16[16,2,2,2,8,8,128]{6,5,4,3,2,1,0:T(8,128)(2,1)} %broadcast_in_dim.64), calls=%async_computation.1 | async-start | bytes 4194304 | tf_op jit(solution)/shard_map/all_to_all | solution.py:199
  74.6 44.2 %collective-permute-start = (bf16[2,8,256,128]{3,2,1,0:T(8,128)(2,1)}, bf16[2,8,256,128]{3,2,1,0:T(8,128)(2,1)S(1)}, u32[]{:S(2)}, u32[]{:S(2)}) collective-permute-start(bf16[2,8,256,128]{3,2,1,0:T(8,128)(2,1)} %shard_map.60), channel_id=1, source_target_pairs={{0,1},{1,0},{2,3},{3,2},{4,5},{5,4},{6,7},{7,6},{8,9},{9,8},{10,11... | collective-permute-start | bytes 3145736 | tf_op jit(solution)/shard_map/ppermute | solution.py:214
  100.4 34.6 %all-to-all-start.3 = ((bf16[4,2,2,8,8,256]{5,4,3,2,1,0:T(8,128)(2,1)}), bf16[4,2,2,8,8,256]{5,4,3,2,1,0:T(8,128)(2,1)}, u32[]{:S(2)}, u32[]{:S(2)}) async-start(bf16[4,2,2,8,8,256]{5,4,3,2,1,0:T(8,128)(2,1)} %broadcast_in_dim.66), calls=%async_computation.3 | async-start | bytes 1048576 | tf_op jit(solution)/shard_map/all_to_all | solution.py:199
  120.5 4.6 %collective-permute-start.1 = (bf16[2,8,256,128]{3,2,1,0:T(8,128)(2,1)S(1)}, bf16[2,8,256,128]{3,2,1,0:T(8,128)(2,1)S(1)}, u32[]{:S(2)}, u32[]{:S(2)}) collective-permute-start(bf16[2,8,256,128]{3,2,1,0:T(8,128)(2,1)S(1)} %shard_map.61.own), channel_id=1, source_target_pairs={{0,32},{32,0},{1,33},{33,1},{2,34},{34,2},{3,35},{35,3},{4,36},{36... | collective-permute-start | bytes 3145736 | tf_op jit(solution)/shard_map/ppermute | solution.py:216
  127.6 19.6 %collective-permute-start.2 = (f32[2,8,64,128]{3,2,1,0:T(8,128)S(1)}, f32[2,8,64,128]{3,2,1,0:T(8,128)S(1)}, u32[]{:S(2)}, u32[]{:S(2)}) collective-permute-start(f32[2,8,64,128]{3,2,1,0:T(8,128)S(1)} %get-tuple-element.7), channel_id=1, source_target_pairs={{0,64},{64,0},{1,65},{65,1},{2,66},{66,2},{3,67},{67,3},{4,68},{68... | collective-permute-start | bytes 1572872 | tf_op jit(solution)/shard_map/ppermute | solution.py:230
  187.6 30.0 %all-to-all-start.5 = ((f32[4,2,8,16,128]{4,3,2,1,0:T(8,128)}), f32[4,2,8,16,128]{4,3,2,1,0:T(8,128)S(1)}, u32[]{:S(2)}, u32[]{:S(2)}) async-start(f32[4,2,8,16,128]{4,3,2,1,0:T(8,128)} %get-tuple-element.8), calls=%async_computation.5 | async-start | bytes 1048576 | tf_op jit(solution)/shard_map/all_to_all | solution.py:242
  218.3 7.3 %all-to-all-start.6 = ((bf16[2,2,8,16,128]{4,3,2,1,0:T(8,128)(2,1)}), bf16[2,2,8,16,128]{4,3,2,1,0:T(8,128)(2,1)S(1)}, u32[]{:S(2)}, u32[]{:S(2)}) async-start(bf16[2,2,8,16,128]{4,3,2,1,0:T(8,128)(2,1)} %broadcast_in_dim.69), calls=%async_computation.6 | async-start | bytes 262144 | tf_op jit(solution)/shard_map/all_to_all | solution.py:199
  226.4 12.8 %all-to-all-start.9 = ((f32[16,16,256]{2,1,0:T(8,128)}), f32[16,16,256]{2,1,0:T(8,128)S(1)}, u32[]{:S(2)}, u32[]{:S(2)}) async-start(f32[16,16,256]{2,1,0:T(8,128)} %broadcast_in_dim.74), calls=%async_computation.9 | async-start | bytes 524288 | tf_op jit(solution)/shard_map/all_to_all | solution.py:199

commit v2 on v1

v2 whole, which is shorter than its diff:
```python
import jax
import jax.numpy as jnp
from jax import lax
from jax.experimental import pallas as pl
from jax.experimental.pallas import tpu as pltpu
from jax.sharding import Mesh, PartitionSpec as P

BF = jnp.bfloat16
F32 = jnp.float32
ROW = ("za", "zb", "zc", "core")
COL = ("zh", "y", "xa", "h")
PLANE = ("y", "xa", "h")
VMEM_LIMIT = 48 * 1024 * 1024


def params():
    return pltpu.CompilerParams(vmem_limit_bytes=VMEM_LIMIT)


def whole(count):
    return [pl.BlockSpec(memory_space=pltpu.VMEM)] * count


def block_row(k, st, ids):
    return st[k, ids[0]] - 4 * ids[0]


def block_col(k, st, ids):
    return lax.rem(st[k, ids[1] // 2], 2)


def present(k, st, ids):
    return st[k, ids[1] // 2] // 2 == ids[1]


def pick_kernel(st, ids, block, out):
    out[:, 0] = jnp.where(present(pl.program_id(0), st, ids), block[...], 0)


def pick_blocks(inverse_anc, structure, ids):
    def at(k, st, ids):
        return (0, block_row(k, st, ids), block_col(k, st, ids))

    return pl.pallas_call(
        pick_kernel,
        grid_spec=pltpu.PrefetchScalarGridSpec(
            num_scalar_prefetch=2,
            grid=(8,),
            in_specs=[pl.BlockSpec((2, 256, 256), at)],
            out_specs=pl.BlockSpec((2, 1, 256, 256), lambda k, st, ids: (0, k, 0, 0)),
        ),
        out_shape=jax.ShapeDtypeStruct((2, 8, 256, 256), BF),
        compiler_params=params(),
    )(structure, ids, inverse_anc)


def lanes_kernel(panel, out):
    x = panel[...].astype(F32).reshape(128, 256).astype(BF)
    src = lax.broadcasted_iota(jnp.int32, (256, 256), 0)
    dst = lax.broadcasted_iota(jnp.int32, (256, 256), 1)
    t = src % 16
    core = (src // 16) % 2
    zc = (src // 32) % 2
    zb = (src // 64) % 2
    za = src // 128
    place = core * 128 + zc * 64 + za * 32 + zb * 16 + t
    perm = jnp.where(place == dst, 1.0, 0.0).astype(BF)
    y = jnp.dot(x, perm, preferred_element_type=F32)
    for c in range(2):
        half = y[:, 128 * c : 128 * c + 128].reshape(2, 8, 8, 128).astype(BF)
        for z in range(16):
            out[c, z] = half


def split_lanes(panel):
    return pl.pallas_call(
        lanes_kernel,
        in_specs=whole(1),
        out_specs=whole(1)[0],
        out_shape=jax.ShapeDtypeStruct((2, 16, 2, 8, 8, 128), BF),
        compiler_params=params(),
    )(panel)


def product_kernel(ids, near, far, own, sib, out):
    core = ids[2]
    zh = ids[4]
    form = (((0,), (0,)), ((), ()))
    for k in range(8):
        total = None
        for source, blocks in ((core, own), (1 - core, sib)):
            left = []
            for p in range(2):
                parts = []
                for panel in (near, far):
                    parts.append(panel[source, :, p, k].astype(F32).reshape(128, 128))
                lower = jnp.where(zh == 0, parts[0], parts[1])
                upper = jnp.where(zh == 0, parts[1], parts[0])
                left.append(jnp.concatenate([lower, upper], axis=0).astype(BF))
            re = blocks[0, k]
            im = blocks[1, k]
            one = lax.dot_general(
                left[0], jnp.concatenate([re, im], axis=1), form, preferred_element_type=F32
            )
            two = lax.dot_general(
                left[1], jnp.concatenate([-im, re], axis=1), form, preferred_element_type=F32
            )
            both = one + two
            total = both if total is None else total + both
        for z in range(2):
            for h in range(2):
                for p in range(2):
                    at = 256 * p + 128 * h
                    out[2 * z + h, p, k] = total[64 * z : 64 * z + 64, at : at + 128]


def products(ids, near, far, own, sib):
    return pl.pallas_call(
        product_kernel,
        in_specs=[pl.BlockSpec(memory_space=pltpu.SMEM)] + whole(4),
        out_specs=whole(1)[0],
        out_shape=jax.ShapeDtypeStruct((4, 2, 8, 64, 128), F32),
        compiler_params=params(),
    )(ids, near, far, own, sib)


def diag_kernel(ids, parts, below, *outs):
    row = ids[0]
    zab = 2 * ids[6] + ids[5]
    out = outs[4]
    for k in range(8):
        sums = []
        for p in range(2):
            value = (parts[0, p, k] + parts[1, p, k]) + (parts[2, p, k] + parts[3, p, k])
            sums.append(value)
            quarters = [value[16 * i : 16 * i + 16] for i in range(4)]
            for i in range(4):
                rows = quarters[i]
                for mine in range(1, 4):
                    rows = jnp.where(zab == mine, quarters[i ^ mine], rows)
                outs[i][p, k] = rows
        left = []
        for value in sums:
            high = value.astype(BF)
            left.append(high)
            left.append((value - high.astype(F32)).astype(BF))
        left = jnp.concatenate(left, axis=1)
        panel = []
        for p in range(2):
            part = []
            for m in range(16):
                far = jnp.bitwise_xor(row, m)
                at = (far % 2) * 8 + (far // 2 % 2) * 4 + (far // 4 % 2) * 2 + far // 8
                part.append(below[at, p, k].astype(F32))
            panel.append(jnp.concatenate(part, axis=0).astype(BF))
        re, im = panel
        right_re = jnp.concatenate([re, re, -im, -im], axis=0)
        right_im = jnp.concatenate([im, im, re, re], axis=0)
        out[k] = jnp.dot(left, right_re, preferred_element_type=F32)
        out[8 + k] = jnp.dot(left, right_im, preferred_element_type=F32)


def diag_terms(ids, parts, below):
    quarter = jax.ShapeDtypeStruct((2, 8, 16, 128), F32)
    return pl.pallas_call(
        diag_kernel,
        in_specs=[pl.BlockSpec(memory_space=pltpu.SMEM)] + whole(2),
        out_specs=whole(5),
        out_shape=[quarter] * 4 + [jax.ShapeDtypeStruct((16, 64, 256), F32)],
        compiler_params=params(),
    )(ids, parts, below)


def spread(value, axes, size):
    copies = jnp.broadcast_to(value[None], (size,) + value.shape)
    return lax.all_to_all(copies, axes, 0, 0, tiled=True)


PAIR = [(0, 1), (1, 0)]


def doubled(value, axis):
    return jnp.concatenate([value, lax.ppermute(value, axis, PAIR)], axis=0)


def shards(inverse_anc, lower_panel, diag_inverse, structure):
    my_row = lax.axis_index(ROW)
    my_col = lax.axis_index(COL)
    ids = [my_row, my_col] + [lax.axis_index(axis) for axis in ("core", "zc", "zh", "zb", "za")]
    ids = jnp.stack(ids).astype(jnp.int32)
    own = lower_panel.reshape(2, 8, 8, 256)
    tie = lax.optimization_barrier

    moves = []
    for q in range(16):
        for h in range(2):
            for m in range(16):
                moves.append((q * 32 + 16 * h + m, m * 32 + 2 * q + h))
    below = lax.ppermute(own, ROW + COL, moves).reshape(1, 2, 8, 8, 256)

    group = ("core",) + PLANE
    other = lax.ppermute(own, "zh", PAIR)
    lanes = split_lanes(own)
    near = lax.all_to_all(lanes.reshape(32, 2, 8, 8, 128), group, 0, 0, tiled=True)

    other, near, below = tie((other, near, below))
    lanes = split_lanes(other)
    far = lax.all_to_all(lanes.reshape(32, 2, 8, 8, 128), group, 0, 0, tiled=True)

    mine = pick_blocks(inverse_anc, structure, ids)
    sib = lax.ppermute(mine, "core", PAIR)
    below = doubled(below, "za")
    below = doubled(below, "zb")
    far, below = tie((far, below))
    near = near.reshape(2, 16, 2, 8, 8, 128)
    far = far.reshape(2, 16, 2, 8, 8, 128)
    parts = products(ids, near, far, mine, sib)
    parts = lax.all_to_all(parts, ("zc", "h"), 0, 0, tiled=True)
    below = doubled(below, "zc")
    below = doubled(below, "core")
    rows, by_zb, by_za, by_both, terms = diag_terms(ids, parts, below)

    terms = lax.all_to_all(terms, PLANE, 0, 0, tiled=True)
    by_za = lax.ppermute(by_za, "za", PAIR)
    by_zb = lax.ppermute(by_zb, "zb", PAIR)
    by_both = lax.ppermute(by_both, ("za", "zb"), [(0, 3), (1, 2), (2, 1), (3, 0)])
    terms, by_za, by_zb, by_both = tie((terms, by_za, by_zb, by_both))
    half = (-((rows + by_za) + (by_zb + by_both))).astype(BF)
    part = jnp.sum(terms, axis=0).reshape(4, 1, 16, 256)
    part = jnp.broadcast_to(part, (4, 2, 16, 256)).reshape(8, 16, 256)
    part = lax.all_to_all(part, ("za", "zb", "zh"), 0, 0, tiled=True)
    place = lax.axis_index(PLANE)
    start = lax.dynamic_index_in_dim(diag_inverse.reshape(16, 16, 256), place, 0, keepdims=False)
    diag = spread(start + jnp.sum(part, axis=0), PLANE, 16)
    diag_block = diag.reshape(2, 8, 16, 256)

    partner = lax.ppermute(half, "h", PAIR)
    first = my_col % 2 == 0
    left = jnp.where(first, half, partner)
    right = jnp.where(first, partner, half)
    block = jnp.concatenate([left, right], axis=-1)
    slots = lax.dynamic_index_in_dim(structure, my_col // 2, 1, keepdims=False)
    pieces = []
    for column in range(2):
        keep_it = (slots == 2 * my_col + column)[None, :, None, None]
        pieces.append(jnp.where(keep_it, block, jnp.zeros_like(block)))
    upper_inverse = jnp.concatenate(pieces, axis=3)
    return upper_inverse, diag_block


def solution(mesh):
    fine = Mesh(mesh.devices.reshape(2, 2, 2, 2, 2, 4, 2, 2), ROW + COL)
    placed = (
        P(None, ROW, COL),
        P(None, None, ROW, COL, None),
        P(None, None, ROW, None),
        P(),
    )
    return jax.shard_map(
        shards,
        mesh=fine,
        in_specs=placed,
        out_specs=(P(None, None, ROW, COL), P(None, None, ROW, None)),
        check_vma=False,
    )
```

time: 241 us -> 200 us (0.83)
  blocking collectives: 60 us -> 0 us
  starting transfers between devices: 54.4 us -> 90.7 us
  waiting for transfers between devices: 106 us -> 87.4 us
    all_to_all x4 -> x0, blocking collectives: 60 us -> none  [the longest x1 23.5 us: shards(): terms = lax.all_to_all(terms, PLANE, 0, 0, tiled=True)]
    all_to_all x1 -> x5, starting transfers between devices: 4.53 us -> 40.3 us  [the longest x2 21.5 us: shards(): lax.all_to_all(lanes.reshape(32, 2, 8, 8, 128), group, 0, 0, tiled=True)]
    all_to_all x5 -> x1, waiting for transfers between devices: 41.3 us -> 6.49 us  [spread(): return lax.all_to_all(copies, axes, 0, 0, tiled=True)]
    ppermute x4 -> x11, waiting for transfers between devices: 39.4 us -> 73.9 us  [the longest x4 46.2 us: doubled(): return jnp.concatenate([value, lax.ppermute(value, axis, PAIR)], axis=0)]
    ppermute x4 -> x11, starting transfers between devices: 13.3 us -> 43.2 us  [the longest x1 14 us: shards(): other = lax.ppermute(own, 'zh', PAIR)]
    all_to_all x5 -> x1, starting transfers between devices: 36.6 us -> 7.23 us  [spread(): return lax.all_to_all(copies, axes, 0, 0, tiled=True)]
    all_to_all x1 -> x5, waiting for transfers between devices: 25.2 us -> 6.95 us  [the longest x1 6.94 us: shards(): part = lax.all_to_all(part, ('za', 'zb', 'zh'), 0, 0, tiled=True)]
    unnamed x7 -> x25, local copies, waits for them, and re-layouts: 1.55 us -> 7.95 us
  transfers between devices with their start and end apart: 10 -> 17, of which waited for: 9 -> 11; matrix products, arithmetic and copies ran while one was open for 2% -> 1% of each run, Pallas kernels for 3% -> 0%
where the time goes in v2:
time: 200 us; the launch traced here: 199 us
  starting transfers between devices  90.7 us (45%)
  waiting for transfers between devices  87.4 us (44%)
  local copies, waits for them, and re-layouts  9.43 us (5%)
  Pallas kernels  7.87 us (4%)
  other arithmetic  2.92 us (1%)
    ppermute x4, waiting for transfers between devices, doubled(): return jnp.concatenate([value, lax.ppermute(value, axis, PAIR)], axis=0)  46.2 us
    all_to_all x2, starting transfers between devices, shards(): lax.all_to_all(lanes.reshape(32, 2, 8, 8, 128), group, 0, 0, tiled=True)  21.5 us
    ppermute x1, starting transfers between devices, shards(): other = lax.ppermute(own, 'zh', PAIR)  14 us
    ppermute x1, waiting for transfers between devices, shards(): below = lax.ppermute(own, ROW + COL, moves).reshape(1, 2, 8, 8, 256)  13.4 us
    ppermute x1, starting transfers between devices, shards(): lax.ppermute(by_both, ('za', 'zb'), [(0, 3), (1, 2), (2, 1), (3, 0)])  10.2 us
    ppermute x4, starting transfers between devices, doubled(): return jnp.concatenate([value, lax.ppermute(value, axis, PAIR)], axis=0)  9.13 us
    unnamed x25, local copies, waits for them, and re-layouts  7.95 us
    all_to_all x1, starting transfers between devices, shards(): terms = lax.all_to_all(terms, PLANE, 0, 0, tiled=True)  7.57 us
  transfers between devices with their start and end apart: 17, of which 11 were waited for; matrix products, arithmetic and copies ran while one was open for 1% of the time, Pallas kernels for 0%

profile of v2, /device:TPU:2, one launch (start us, length us, event | category | flops | bytes accessed | tf_op | source)
XLA Modules:
  0.0 199.3 jit_solution(4449784004859339400)
XLA Ops:
  0.7 1.6 copy-done.4
  3.0 1.7 shard_map.61.own
  4.7 1.9 collective-permute-start.4
  8.0 9.5 %all-to-all-start = ((bf16[32,2,8,8,128]{4,3,2,1,0:T(8,128)(2,1)}), bf16[32,2,8,8,128]{4,3,2,1,0:T(8,128)(2,1)S(1)}, u32[]{:S(2)}, u32[]{:S(2)}) async-start(bf16[32,2,8,8,128]{4,3,2,1,0:T(8,128)(2,1)} %bitcast.25), calls=%async_computation | async-start | bytes 2097152 | tf_op jit(solution)/shard_map/all_to_all | solution.py:204
  17.5 14.0 %collective-permute-start = (bf16[2,8,8,256]{3,2,1,0:T(8,128)(2,1)S(1)}, bf16[2,8,8,256]{3,2,1,0:T(8,128)(2,1)S(1)}, u32[]{:S(2)}, u32[]{:S(2)}) collective-permute-start(bf16[2,8,8,256]{3,2,1,0:T(8,128)(2,1)S(1)} %bitcast.27), channel_id=1, source_target_pairs={{0,16},{16,0},{1,17},{17,1},{2,18},{18,2},{3,19},{19,3},{4,20},{20... | collective-permute-start | bytes 196616 | tf_op jit(solution)/shard_map/ppermute | solution.py:202
  31.5 1.9 collective-permute-start.1
  34.2 13.4 %collective-permute-done.1 = bf16[2,8,8,256]{3,2,1,0:T(8,128)(2,1)S(1)} collective-permute-done((bf16[2,8,8,256]{3,2,1,0:T(8,128)(2,1)S(1)}, bf16[2,8,8,256]{3,2,1,0:T(8,128)(2,1)S(1)}, u32[]{:S(2)}, u32[]{:S(2)}) %collective-permute-start.1) | collective-permute-done | bytes 65568 | tf_op jit(solution)/shard_map/ppermute | solution.py:199
  48.9 12.0 %all-to-all-start.1 = ((bf16[32,2,8,8,128]{4,3,2,1,0:T(8,128)(2,1)}), bf16[32,2,8,8,128]{4,3,2,1,0:T(8,128)(2,1)}, u32[]{:S(2)}, u32[]{:S(2)}) async-start(bf16[32,2,8,8,128]{4,3,2,1,0:T(8,128)(2,1)} %bitcast.24), calls=%async_computation.1 | async-start | bytes 2097152 | tf_op jit(solution)/shard_map/all_to_all | solution.py:208
  60.9 1.9 collective-permute-start.2
  62.8 10.0 %collective-permute-done.2 = bf16[1,2,8,8,256]{4,3,2,1,0:T(8,128)(2,1)S(1)} collective-permute-done((bf16[1,2,8,8,256]{4,3,2,1,0:T(8,128)(2,1)S(1)}, bf16[1,2,8,8,256]{4,3,2,1,0:T(8,128)(2,1)S(1)}, u32[]{:S(2)}, u32[]{:S(2)}) %collective-permute-start.2) | collective-permute-done | bytes 65568 | tf_op jit(solution)/shard_map/ppermute | solution.py:183
  72.8 1.9 collective-permute-start.3
  74.8 7.3 %collective-permute-done.3 = bf16[2,2,8,8,256]{4,3,2,1,0:T(8,128)(2,1)S(1)} collective-permute-done((bf16[2,2,8,8,256]{4,3,2,1,0:T(8,128)(2,1)S(1)}, bf16[2,2,8,8,256]{4,3,2,1,0:T(8,128)(2,1)S(1)}, u32[]{:S(2)}, u32[]{:S(2)}) %collective-permute-start.3) | collective-permute-done | bytes 131104 | tf_op jit(solution)/shard_map/ppermute | solution.py:183
  83.0 3.9 %shard_map.62 = f32[4,2,8,64,128]{4,3,2,1,0:T(8,128)S(1)} custom-call(s32[7]{0:T(128)S(1)} %stack.31.ids, bf16[2,16,2,8,8,128]{5,4,3,2,1,0:T(8,128)(2,1)S(1)} %bitcast.23, bf16[2,16,2,8,8,128]{5,4,3,2,1,0:T(8,128)(2,1)} %bitcast.12.far, bf16[2,8,256,256]{3,2,1,0:T(8,128)(2,1)} %copy-done, bf16[2,8,256,256]{3,2,1,0:T(8,128)(2,1)} %collective-permute-done.4.sib), custom_call_target="tpu_custom_call" | custom-call | tf_op jit(solution)/shard_map/pallas_call | solution.py:118
  86.8 1.3 copy-done.1
  88.2 3.9 %all-to-all-start.2 = ((f32[4,2,8,64,128]{4,3,2,1,0:T(8,128)}), f32[4,2,8,64,128]{4,3,2,1,0:T(8,128)S(1)}, u32[]{:S(2)}, u32[]{:S(2)}) async-start(f32[4,2,8,64,128]{4,3,2,1,0:T(8,128)} %copy-done.1), calls=%async_computation.2 | async-start | bytes 4194304 | tf_op jit(solution)/shard_map/all_to_all | solution.py:218
  92.1 3.4 %collective-permute-start.5 = (bf16[4,2,8,8,256]{4,3,2,1,0:T(8,128)(2,1)S(1)}, bf16[4,2,8,8,256]{4,3,2,1,0:T(8,128)(2,1)S(1)}, u32[]{:S(2)}, u32[]{:S(2)}) collective-permute-start(bf16[4,2,8,8,256]{4,3,2,1,0:T(8,128)(2,1)S(1)} %pad_maximum_fusion.2), channel_id=1, source_target_pairs={{0,64},{64,0},{1,65},{65,1},{2,66},{66,2},{3,67},{67,3},{4,68},{68... | collective-permute-start | bytes 786440 | tf_op jit(solution)/shard_map/ppermute | solution.py:183
  95.5 27.0 %collective-permute-done.5 = bf16[4,2,8,8,256]{4,3,2,1,0:T(8,128)(2,1)S(1)} collective-permute-done((bf16[4,2,8,8,256]{4,3,2,1,0:T(8,128)(2,1)S(1)}, bf16[4,2,8,8,256]{4,3,2,1,0:T(8,128)(2,1)S(1)}, u32[]{:S(2)}, u32[]{:S(2)}) %collective-permute-start.5) | collective-permute-done | bytes 262176 | tf_op jit(solution)/shard_map/ppermute | solution.py:183
  122.6 1.9 collective-permute-start.6
  124.5 1.9 collective-permute-done.6
  126.5 1.7 shard_map.63
  129.8 7.6 %all-to-all-start.3 = ((f32[16,64,256]{2,1,0:T(8,128)}), f32[16,64,256]{2,1,0:T(8,128)S(1)}, u32[]{:S(2)}, u32[]{:S(2)}) async-start(f32[16,64,256]{2,1,0:T(8,128)} %copy-done.5), calls=%async_computation.3 | async-start | bytes 2097152 | tf_op jit(solution)/shard_map/all_to_all | solution.py:223
  137.4 1.9 collective-permute-start.7
  139.3 1.9 collective-permute-start.8
  141.2 10.2 %collective-permute-start.9 = (f32[2,8,16,128]{3,2,1,0:T(8,128)S(1)}, f32[2,8,16,128]{3,2,1,0:T(8,128)S(1)}, u32[]{:S(2)}, u32[]{:S(2)}) collective-permute-start(f32[2,8,16,128]{3,2,1,0:T(8,128)S(1)} %get-tuple-element.25), channel_id=1, source_target_pairs={{0,384},{128,256},{256,128},{384,0},{1,385},{129,257},{257,129},{3... | collective-permute-start | bytes 393224 | tf_op jit(solution)/shard_map/ppermute | solution.py:226
  151.4 7.2 %collective-permute-done.7 = f32[2,8,16,128]{3,2,1,0:T(8,128)S(1)} collective-permute-done((f32[2,8,16,128]{3,2,1,0:T(8,128)S(1)}, f32[2,8,16,128]{3,2,1,0:T(8,128)S(1)}, u32[]{:S(2)}, u32[]{:S(2)}) %collective-permute-start.7) | collective-permute-done | bytes 131104 | tf_op jit(solution)/shard_map/ppermute | solution.py:224
  158.6 2.8 %collective-permute-done.9 = f32[2,8,16,128]{3,2,1,0:T(8,128)S(1)} collective-permute-done((f32[2,8,16,128]{3,2,1,0:T(8,128)S(1)}, f32[2,8,16,128]{3,2,1,0:T(8,128)S(1)}, u32[]{:S(2)}, u32[]{:S(2)}) %collective-permute-start.9) | collective-permute-done | bytes 131104 | tf_op jit(solution)/shard_map/ppermute | solution.py:226
  162.1 7.3 %all-to-all-start.4 = ((f32[8,16,256]{2,1,0:T(8,128)}), f32[8,16,256]{2,1,0:T(8,128)S(1)}, u32[]{:S(2)}, u32[]{:S(2)}) async-start(f32[8,16,256]{2,1,0:T(8,128)} %bitcast.15), calls=%async_computation.4 | async-start | bytes 262144 | tf_op jit(solution)/shard_map/all_to_all | solution.py:231
  169.4 2.3 %collective-permute-start.10 = (bf16[2,8,16,128]{3,2,1,0:T(8,128)(2,1)S(1)}, bf16[2,8,16,128]{3,2,1,0:T(8,128)(2,1)S(1)}, u32[]{:S(2)}, u32[]{:S(2)}) collective-permute-start(bf16[2,8,16,128]{3,2,1,0:T(8,128)(2,1)S(1)} %negate_convert_fusion), channel_id=1, source_target_pairs={{0,1},{1,0},{2,3},{3,2},{4,5},{5,4},{6,7},{7,6},{8,9},{9,8},{10,11... | collective-permute-start | bytes 196616 | tf_op jit(solution)/shard_map/ppermute | solution.py:237
  171.9 3.6 %collective-permute-done.10 = bf16[2,8,16,128]{3,2,1,0:T(8,128)(2,1)S(1)} collective-permute-done((bf16[2,8,16,128]{3,2,1,0:T(8,128)(2,1)S(1)}, bf16[2,8,16,128]{3,2,1,0:T(8,128)(2,1)S(1)}, u32[]{:S(2)}, u32[]{:S(2)}) %collective-permute-start.10) | collective-permute-done | bytes 65568 | tf_op jit(solution)/shard_map/ppermute | solution.py:237
  175.6 6.9 %all-to-all-done.4 = f32[8,16,256]{2,1,0:T(8,128)S(1)} async-done(((f32[8,16,256]{2,1,0:T(8,128)}), f32[8,16,256]{2,1,0:T(8,128)S(1)}, u32[]{:S(2)}, u32[]{:S(2)}) %all-to-all-start.4) | async-done | bytes 131104 | tf_op jit(solution)/shard_map/all_to_all | solution.py:231
  184.0 7.2 %all-to-all-start.5 = ((f32[16,16,256]{2,1,0:T(8,128)}), f32[16,16,256]{2,1,0:T(8,128)S(1)}, u32[]{:S(2)}, u32[]{:S(2)}) async-start(f32[16,16,256]{2,1,0:T(8,128)} %broadcast_in_dim.35), calls=%async_computation.5 | async-start | bytes 524288 | tf_op jit(solution)/shard_map/all_to_all | solution.py:176
  192.1 6.5 %all-to-all-done.5 = f32[16,16,256]{2,1,0:T(8,128)S(1)} async-done(((f32[16,16,256]{2,1,0:T(8,128)}), f32[16,16,256]{2,1,0:T(8,128)S(1)}, u32[]{:S(2)}, u32[]{:S(2)}) %all-to-all-start.5) | async-done | bytes 262176 | tf_op jit(solution)/shard_map/all_to_all | solution.py:176
  (47 shorter events, 10.9 us)
Async XLA Ops:
  0.7 1.6 copy-start.4
  2.3 0.7 copy-start.7
  3.0 3.7 %copy-start.6 = (bf16[2,8,1,8,256]{4,3,2,1,0:T(8,128)(2,1)S(1)}, bf16[2,8,1,8,256]{4,3,2,1,0:T(8,128)(2,1)}, u32[]{:S(2)}) copy-start(bf16[2,8,1,8,256]{4,3,2,1,0:T(8,128)(2,1)} %param.5) | copy-start | bytes 196612
  4.7 43.2 %copy-start = (bf16[2,8,256,256]{3,2,1,0:T(8,128)(2,1)}, bf16[2,8,256,256]{3,2,1,0:T(8,128)(2,1)S(1)}, u32[]{:S(2)}) copy-start(bf16[2,8,256,256]{3,2,1,0:T(8,128)(2,1)S(1)} %shard_map.61.own) | copy-start | bytes 6291460
  4.7 78.2 %collective-permute-start.4 = (bf16[2,8,256,256]{3,2,1,0:T(8,128)(2,1)S(1)}, bf16[2,8,256,256]{3,2,1,0:T(8,128)(2,1)}, u32[]{:S(2)}, u32[]{:S(2)}) collective-permute-start(bf16[2,8,256,256]{3,2,1,0:T(8,128)(2,1)S(1)} %shard_map.61.own), channel_id=1, source_target_pairs={{0,32},{32,0},{1,33},{33,1},{2,34},{34,2},{3,35},{35,3},{4,36},{36... | collective-permute-start | bytes 6291464 | tf_op jit(solution)/shard_map/ppermute | solution.py:211
  7.0 1.0 copy-start.3
  8.0 39.6 %all-to-all-start = ((bf16[32,2,8,8,128]{4,3,2,1,0:T(8,128)(2,1)}), bf16[32,2,8,8,128]{4,3,2,1,0:T(8,128)(2,1)S(1)}, u32[]{:S(2)}, u32[]{:S(2)}) async-start(bf16[32,2,8,8,128]{4,3,2,1,0:T(8,128)(2,1)} %bitcast.25), calls=%async_computation | async-start | bytes 2097152 | tf_op jit(solution)/shard_map/all_to_all | solution.py:204
  17.5 16.7 %collective-permute-start = (bf16[2,8,8,256]{3,2,1,0:T(8,128)(2,1)S(1)}, bf16[2,8,8,256]{3,2,1,0:T(8,128)(2,1)S(1)}, u32[]{:S(2)}, u32[]{:S(2)}) collective-permute-start(bf16[2,8,8,256]{3,2,1,0:T(8,128)(2,1)S(1)} %bitcast.27), channel_id=1, source_target_pairs={{0,16},{16,0},{1,17},{17,1},{2,18},{18,2},{3,19},{19,3},{4,20},{20... | collective-permute-start | bytes 196616 | tf_op jit(solution)/shard_map/ppermute | solution.py:202
  31.5 16.1 %collective-permute-start.1 = (bf16[2,8,8,256]{3,2,1,0:T(8,128)(2,1)S(1)}, bf16[2,8,8,256]{3,2,1,0:T(8,128)(2,1)S(1)}, u32[]{:S(2)}, u32[]{:S(2)}) collective-permute-start(bf16[2,8,8,256]{3,2,1,0:T(8,128)(2,1)S(1)} %bitcast.28), channel_id=1, source_target_pairs={{0,0},{1,32},{2,64},{3,96},{4,128},{5,160},{6,192},{7,224},{8,256}... | collective-permute-start | bytes 196616 | tf_op jit(solution)/shard_map/ppermute | solution.py:199
  47.6 27.2 %copy-start.11 = (bf16[2,8,8,256]{3,2,1,0:T(8,128)(2,1)}, bf16[2,8,8,256]{3,2,1,0:T(8,128)(2,1)S(1)}, u32[]{:S(2)}) copy-start(bf16[2,8,8,256]{3,2,1,0:T(8,128)(2,1)S(1)} %collective-permute-done.1) | copy-start | bytes 196612
  47.9 1.0 copy-start.2
  48.9 34.0 %all-to-all-start.1 = ((bf16[32,2,8,8,128]{4,3,2,1,0:T(8,128)(2,1)}), bf16[32,2,8,8,128]{4,3,2,1,0:T(8,128)(2,1)}, u32[]{:S(2)}, u32[]{:S(2)}) async-start(bf16[32,2,8,8,128]{4,3,2,1,0:T(8,128)(2,1)} %bitcast.24), calls=%async_computation.1 | async-start | bytes 2097152 | tf_op jit(solution)/shard_map/all_to_all | solution.py:208
  60.9 11.9 %collective-permute-start.2 = (bf16[1,2,8,8,256]{4,3,2,1,0:T(8,128)(2,1)S(1)}, bf16[1,2,8,8,256]{4,3,2,1,0:T(8,128)(2,1)S(1)}, u32[]{:S(2)}, u32[]{:S(2)}) collective-permute-start(bf16[1,2,8,8,256]{4,3,2,1,0:T(8,128)(2,1)S(1)} %bitcast.31), channel_id=1, source_target_pairs={{0,256},{256,0},{1,257},{257,1},{2,258},{258,2},{3,259},{259,3},{4... | collective-permute-start | bytes 196616 | tf_op jit(solution)/shard_map/ppermute | solution.py:183
  72.8 9.3 %collective-permute-start.3 = (bf16[2,2,8,8,256]{4,3,2,1,0:T(8,128)(2,1)S(1)}, bf16[2,2,8,8,256]{4,3,2,1,0:T(8,128)(2,1)S(1)}, u32[]{:S(2)}, u32[]{:S(2)}) collective-permute-start(bf16[2,2,8,8,256]{4,3,2,1,0:T(8,128)(2,1)S(1)} %pad_maximum_fusion.4), channel_id=1, source_target_pairs={{0,128},{128,0},{1,129},{129,1},{2,130},{130,2},{3,131},{131,3},{4... | collective-permute-start | bytes 393224 | tf_op jit(solution)/shard_map/ppermute | solution.py:183
  86.8 1.3 copy-start.1
  88.2 38.3 %all-to-all-start.2 = ((f32[4,2,8,64,128]{4,3,2,1,0:T(8,128)}), f32[4,2,8,64,128]{4,3,2,1,0:T(8,128)S(1)}, u32[]{:S(2)}, u32[]{:S(2)}) async-start(f32[4,2,8,64,128]{4,3,2,1,0:T(8,128)} %copy-done.1), calls=%async_computation.2 | async-start | bytes 4194304 | tf_op jit(solution)/shard_map/all_to_all | solution.py:218
  92.1 30.4 %collective-permute-start.5 = (bf16[4,2,8,8,256]{4,3,2,1,0:T(8,128)(2,1)S(1)}, bf16[4,2,8,8,256]{4,3,2,1,0:T(8,128)(2,1)S(1)}, u32[]{:S(2)}, u32[]{:S(2)}) collective-permute-start(bf16[4,2,8,8,256]{4,3,2,1,0:T(8,128)(2,1)S(1)} %pad_maximum_fusion.2), channel_id=1, source_target_pairs={{0,64},{64,0},{1,65},{65,1},{2,66},{66,2},{3,67},{67,3},{4,68},{68... | collective-permute-start | bytes 786440 | tf_op jit(solution)/shard_map/ppermute | solution.py:183
  122.6 3.8 %collective-permute-start.6 = (bf16[8,2,8,8,256]{4,3,2,1,0:T(8,128)(2,1)S(1)}, bf16[8,2,8,8,256]{4,3,2,1,0:T(8,128)(2,1)S(1)}, u32[]{:S(2)}, u32[]{:S(2)}) collective-permute-start(bf16[8,2,8,8,256]{4,3,2,1,0:T(8,128)(2,1)S(1)} %pad_maximum_fusion.1), channel_id=1, source_target_pairs={{0,32},{32,0},{1,33},{33,1},{2,34},{34,2},{3,35},{35,3},{4,36},{36... | collective-permute-start | bytes 1572872 | tf_op jit(solution)/shard_map/ppermute | solution.py:183
  128.1 1.0 copy-start.5
  129.2 0.7 copy-start.9
  129.8 7.6 %copy-start.10 = (f32[2,8,16,128]{3,2,1,0:T(8,128)S(1)}, f32[2,8,16,128]{3,2,1,0:T(8,128)}, u32[]{:S(2)}) copy-start(f32[2,8,16,128]{3,2,1,0:T(8,128)} %copy-done.9) | copy-start | bytes 393220
  129.8 41.9 %copy-start.8 = (s32[8,16]{1,0:T(8,128)S(1)}, s32[8,16]{1,0:T(8,128)}, u32[]{:S(2)}) copy-start(s32[8,16]{1,0:T(8,128)} %st.1) | copy-start | bytes 1540
  129.8 31.6 %all-to-all-start.3 = ((f32[16,64,256]{2,1,0:T(8,128)}), f32[16,64,256]{2,1,0:T(8,128)S(1)}, u32[]{:S(2)}, u32[]{:S(2)}) async-start(f32[16,64,256]{2,1,0:T(8,128)} %copy-done.5), calls=%async_computation.3 | async-start | bytes 2097152 | tf_op jit(solution)/shard_map/all_to_all | solution.py:223
  137.4 21.2 %collective-permute-start.7 = (f32[2,8,16,128]{3,2,1,0:T(8,128)S(1)}, f32[2,8,16,128]{3,2,1,0:T(8,128)S(1)}, u32[]{:S(2)}, u32[]{:S(2)}) collective-permute-start(f32[2,8,16,128]{3,2,1,0:T(8,128)S(1)} %copy-done.10), channel_id=1, source_target_pairs={{0,256},{256,0},{1,257},{257,1},{2,258},{258,2},{3,259},{259,3},{4... | collective-permute-start | bytes 393224 | tf_op jit(solution)/shard_map/ppermute | solution.py:224
  139.3 19.3 %collective-permute-start.8 = (f32[2,8,16,128]{3,2,1,0:T(8,128)S(1)}, f32[2,8,16,128]{3,2,1,0:T(8,128)S(1)}, u32[]{:S(2)}, u32[]{:S(2)}) collective-permute-start(f32[2,8,16,128]{3,2,1,0:T(8,128)S(1)} %get-tuple-element.24), channel_id=1, source_target_pairs={{0,128},{128,0},{1,129},{129,1},{2,130},{130,2},{3,131},{131,3},{4... | collective-permute-start | bytes 393224 | tf_op jit(solution)/shard_map/ppermute | solution.py:225
  141.2 20.1 %collective-permute-start.9 = (f32[2,8,16,128]{3,2,1,0:T(8,128)S(1)}, f32[2,8,16,128]{3,2,1,0:T(8,128)S(1)}, u32[]{:S(2)}, u32[]{:S(2)}) collective-permute-start(f32[2,8,16,128]{3,2,1,0:T(8,128)S(1)} %get-tuple-element.25), channel_id=1, source_target_pairs={{0,384},{128,256},{256,128},{384,0},{1,385},{129,257},{257,129},{3... | collective-permute-start | bytes 393224 | tf_op jit(solution)/shard_map/ppermute | solution.py:226
  162.1 20.4 %all-to-all-start.4 = ((f32[8,16,256]{2,1,0:T(8,128)}), f32[8,16,256]{2,1,0:T(8,128)S(1)}, u32[]{:S(2)}, u32[]{:S(2)}) async-start(f32[8,16,256]{2,1,0:T(8,128)} %bitcast.15), calls=%async_computation.4 | async-start | bytes 262144 | tf_op jit(solution)/shard_map/all_to_all | solution.py:231
  169.4 6.2 %collective-permute-start.10 = (bf16[2,8,16,128]{3,2,1,0:T(8,128)(2,1)S(1)}, bf16[2,8,16,128]{3,2,1,0:T(8,128)(2,1)S(1)}, u32[]{:S(2)}, u32[]{:S(2)}) collective-permute-start(bf16[2,8,16,128]{3,2,1,0:T(8,128)(2,1)S(1)} %negate_convert_fusion), channel_id=1, source_target_pairs={{0,1},{1,0},{2,3},{3,2},{4,5},{5,4},{6,7},{7,6},{8,9},{9,8},{10,11... | collective-permute-start | bytes 196616 | tf_op jit(solution)/shard_map/ppermute | solution.py:237
  184.0 14.6 %all-to-all-start.5 = ((f32[16,16,256]{2,1,0:T(8,128)}), f32[16,16,256]{2,1,0:T(8,128)S(1)}, u32[]{:S(2)}, u32[]{:S(2)}) async-start(f32[16,16,256]{2,1,0:T(8,128)} %broadcast_in_dim.35), calls=%async_computation.5 | async-start | bytes 524288 | tf_op jit(solution)/shard_map/all_to_all | solution.py:176

commit v3 on v2

--- a/solution.py
+++ b/solution.py
@@ -7,6 +7,7 @@
 
 BF = jnp.bfloat16
 F32 = jnp.float32
+F16 = jnp.float16
 ROW = ("za", "zb", "zc", "core")
 COL = ("zh", "y", "xa", "h")
 PLANE = ("y", "xa", "h")
@@ -86,6 +87,7 @@
     core = ids[2]
     zh = ids[4]
     form = (((0,), (0,)), ((), ()))
+    largest = jnp.zeros((8, 128), F32)
     for k in range(8):
         total = None
         for source, blocks in ((core, own), (1 - core, sib)):
@@ -107,11 +109,23 @@
             )
             both = one + two
             total = both if total is None else total + both
-        for z in range(2):
+        size = jnp.max(jnp.abs(total).reshape(16, 8, 512), axis=0)
+        for lane in range(4):
+            largest = jnp.maximum(largest, size[:, 128 * lane : 128 * lane + 128])
+        for zc in range(2):
             for h in range(2):
-                for p in range(2):
-                    at = 256 * p + 128 * h
-                    out[2 * z + h, p, k] = total[64 * z : 64 * z + 64, at : at + 128]
+                for zab in range(4):
+                    for p in range(2):
+                        row = 64 * zc + 16 * zab
+                        lane = 256 * p + 128 * h
+                        to = ((2 * zab + p) * 8 + k) * 16
+                        out[2 * zc + h, to : to + 16] = total[row : row + 16, lane : lane + 128]
+    largest = jnp.max(jnp.max(largest, axis=0, keepdims=True), axis=1, keepdims=True)
+    power = jnp.clip(jnp.ceil(jnp.log2(largest)), -100.0, 100.0)
+    scale = jnp.exp2(14.0 - power)
+    for chunk in range(4):
+        out[chunk, :1024] = out[chunk, :1024] * scale
+        out[chunk, 1024:] = jnp.broadcast_to(power, (16, 128))
 
 
 def products(ids, near, far, own, sib):
@@ -119,31 +133,19 @@
         product_kernel,
         in_specs=[pl.BlockSpec(memory_space=pltpu.SMEM)] + whole(4),
         out_specs=whole(1)[0],
-        out_shape=jax.ShapeDtypeStruct((4, 2, 8, 64, 128), F32),
+        out_shape=jax.ShapeDtypeStruct((4, 1040, 128), F32),
         compiler_params=params(),
     )(ids, near, far, own, sib)
 
 
-def diag_kernel(ids, parts, below, *outs):
+def diag_kernel(ids, summed, below, half, out):
     row = ids[0]
-    zab = 2 * ids[6] + ids[5]
-    out = outs[4]
     for k in range(8):
-        sums = []
+        left = []
         for p in range(2):
-            value = (parts[0, p, k] + parts[1, p, k]) + (parts[2, p, k] + parts[3, p, k])
-            sums.append(value)
-            quarters = [value[16 * i : 16 * i + 16] for i in range(4)]
-            for i in range(4):
-                rows = quarters[i]
-                for mine in range(1, 4):
-                    rows = jnp.where(zab == mine, quarters[i ^ mine], rows)
-                outs[i][p, k] = rows
-        left = []
-        for value in sums:
-            high = value.astype(BF)
-            left.append(high)
-            left.append((value - high.astype(F32)).astype(BF))
+            upper = (-summed[p, k]).astype(BF)
+            half[p, k] = upper
+            left.append(upper)
         left = jnp.concatenate(left, axis=1)
         panel = []
         for p in range(2):
@@ -154,26 +156,23 @@
                 part.append(below[at, p, k].astype(F32))
             panel.append(jnp.concatenate(part, axis=0).astype(BF))
         re, im = panel
-        right_re = jnp.concatenate([re, re, -im, -im], axis=0)
-        right_im = jnp.concatenate([im, im, re, re], axis=0)
+        right_re = jnp.concatenate([re, -im], axis=0)
+        right_im = jnp.concatenate([im, re], axis=0)
         out[k] = jnp.dot(left, right_re, preferred_element_type=F32)
         out[8 + k] = jnp.dot(left, right_im, preferred_element_type=F32)
 
 
-def diag_terms(ids, parts, below):
-    quarter = jax.ShapeDtypeStruct((2, 8, 16, 128), F32)
+def diag_terms(ids, summed, below):
     return pl.pallas_call(
         diag_kernel,
         in_specs=[pl.BlockSpec(memory_space=pltpu.SMEM)] + whole(2),
-        out_specs=whole(5),
-        out_shape=[quarter] * 4 + [jax.ShapeDtypeStruct((16, 64, 256), F32)],
-        compiler_params=params(),
-    )(ids, parts, below)
-
-
-def spread(value, axes, size):
-    copies = jnp.broadcast_to(value[None], (size,) + value.shape)
-    return lax.all_to_all(copies, axes, 0, 0, tiled=True)
+        out_specs=whole(2),
+        out_shape=[
+            jax.ShapeDtypeStruct((2, 8, 16, 128), BF),
+            jax.ShapeDtypeStruct((16, 16, 256), F32),
+        ],
+        compiler_params=params(),
+    )(ids, summed, below)
 
 
 PAIR = [(0, 1), (1, 0)]
@@ -196,45 +195,51 @@
         for h in range(2):
             for m in range(16):
                 moves.append((q * 32 + 16 * h + m, m * 32 + 2 * q + h))
-    below = lax.ppermute(own, ROW + COL, moves).reshape(1, 2, 8, 8, 256)
 
     group = ("core",) + PLANE
     other = lax.ppermute(own, "zh", PAIR)
     lanes = split_lanes(own)
     near = lax.all_to_all(lanes.reshape(32, 2, 8, 8, 128), group, 0, 0, tiled=True)
 
-    other, near, below = tie((other, near, below))
+    mine = pick_blocks(inverse_anc, structure, ids)
+    sib = lax.ppermute(mine, "core", PAIR)
+    other, near, mine = tie((other, near, mine))
     lanes = split_lanes(other)
     far = lax.all_to_all(lanes.reshape(32, 2, 8, 8, 128), group, 0, 0, tiled=True)
-
-    mine = pick_blocks(inverse_anc, structure, ids)
-    sib = lax.ppermute(mine, "core", PAIR)
+    own = tie((own, lanes))[0]
+    below = lax.ppermute(own, ROW + COL, moves).reshape(1, 2, 8, 8, 256)
     below = doubled(below, "za")
-    below = doubled(below, "zb")
     far, below = tie((far, below))
+
     near = near.reshape(2, 16, 2, 8, 8, 128)
     far = far.reshape(2, 16, 2, 8, 8, 128)
     parts = products(ids, near, far, mine, sib)
-    parts = lax.all_to_all(parts, ("zc", "h"), 0, 0, tiled=True)
+    below, parts = tie((below, parts))
+    below = doubled(below, "zb")
+    got = lax.all_to_all(parts.astype(F16), ("zc", "h"), 0, 0, tiled=True).astype(F32)
+    power = got[:, 1024:1025]
+    most = jnp.max(power, axis=0, keepdims=True) + 2.0
+    parts = jnp.sum(got[:, :1024] * jnp.exp2(power - most), axis=0).reshape(4, 256, 128)
+    parts = jnp.concatenate([parts, jnp.broadcast_to(most, (4, 16, 128))], axis=1)
+
+    below, parts = tie((below, parts))
     below = doubled(below, "zc")
     below = doubled(below, "core")
-    rows, by_zb, by_za, by_both, terms = diag_terms(ids, parts, below)
+    got = lax.all_to_all(parts.astype(F16), ("za", "zb"), 0, 0, tiled=True).astype(F32)
+    summed = jnp.sum(got[:, :256] * jnp.exp2(got[:, 256:257] - 14.0), axis=0)
+    half, terms = diag_terms(ids, summed.reshape(2, 8, 16, 128), below)
 
     terms = lax.all_to_all(terms, PLANE, 0, 0, tiled=True)
-    by_za = lax.ppermute(by_za, "za", PAIR)
-    by_zb = lax.ppermute(by_zb, "zb", PAIR)
-    by_both = lax.ppermute(by_both, ("za", "zb"), [(0, 3), (1, 2), (2, 1), (3, 0)])
-    terms, by_za, by_zb, by_both = tie((terms, by_za, by_zb, by_both))
-    half = (-((rows + by_za) + (by_zb + by_both))).astype(BF)
-    part = jnp.sum(terms, axis=0).reshape(4, 1, 16, 256)
-    part = jnp.broadcast_to(part, (4, 2, 16, 256)).reshape(8, 16, 256)
-    part = lax.all_to_all(part, ("za", "zb", "zh"), 0, 0, tiled=True)
+    partner = lax.ppermute(half, "h", PAIR)
+    terms, partner = tie((terms, partner))
+    part = jnp.sum(terms, axis=0)
+    part = part + lax.ppermute(part, "zh", PAIR)
     place = lax.axis_index(PLANE)
     start = lax.dynamic_index_in_dim(diag_inverse.reshape(16, 16, 256), place, 0, keepdims=False)
-    diag = spread(start + jnp.sum(part, axis=0), PLANE, 16)
+    diag = jnp.broadcast_to((start - part)[None], (16, 16, 256))
+    diag = lax.all_to_all(diag, PLANE, 0, 0, tiled=True)
     diag_block = diag.reshape(2, 8, 16, 256)
 
-    partner = lax.ppermute(half, "h", PAIR)
     first = my_col % 2 == 0
     left = jnp.where(first, half, partner)
     right = jnp.where(first, partner, half)

time: 200 us -> 176 us (0.88)
  waiting for transfers between devices: 87.4 us -> 67.9 us
  starting transfers between devices: 90.7 us -> 85.3 us
  local copies, waits for them, and re-layouts: 9.43 us -> 5.75 us
  other arithmetic: 2.92 us -> 5.9 us
    ppermute x4, waiting for transfers between devices: 46.2 us -> 22.3 us  [doubled(): return jnp.concatenate([value, lax.ppermute(value, axis, PAIR)], axis=0)]
    ppermute x3 -> x1, waiting for transfers between devices: 9.94 us -> 1.68 us  [shards(): part = part + lax.ppermute(part, 'zh', PAIR)]
    all_to_all x3, waiting for transfers between devices: 13.4 us -> 20.8 us  [the longest x1 12.4 us: shards(): lax.all_to_all(parts.astype(F16), ('za', 'zb'), 0, 0, tiled=True)]
    all_to_all x2, starting transfers between devices: 21.5 us -> 16.9 us  [shards(): lax.all_to_all(lanes.reshape(32, 2, 8, 8, 128), group, 0, 0, tiled=True)]
    ppermute x4, starting transfers between devices: 9.13 us -> 12.9 us  [doubled(): return jnp.concatenate([value, lax.ppermute(value, axis, PAIR)], axis=0)]
    convert_element_type x1 -> x4, other arithmetic: 0.04 us -> 3.64 us  [the longest x2 3.46 us: shards(): parts.astype(F16)]
    unnamed x25 -> x13, local copies, waits for them, and re-layouts: 7.95 us -> 4.93 us
    all_to_all x3, starting transfers between devices: 18.4 us -> 15.5 us  [the longest x1 6.52 us: shards(): lax.all_to_all(parts.astype(F16), ('za', 'zb'), 0, 0, tiled=True)]
  transfers between devices with their start and end apart: 17 -> 15, of which waited for: 11 -> 12; matrix products, arithmetic and copies ran while one was open for 1% -> 1% of each run, Pallas kernels for 0% -> 0%
where the time goes in v3:
time: 176 us; the launch traced here: 175 us
  starting transfers between devices  85.3 us (48%)
  waiting for transfers between devices  67.9 us (39%)
  Pallas kernels  9.13 us (5%)
  other arithmetic  5.9 us (3%)
  local copies, waits for them, and re-layouts  5.75 us (3%)
    ppermute x4, waiting for transfers between devices, doubled(): return jnp.concatenate([value, lax.ppermute(value, axis, PAIR)], axis=0)  22.3 us
    all_to_all x2, starting transfers between devices, shards(): lax.all_to_all(lanes.reshape(32, 2, 8, 8, 128), group, 0, 0, tiled=True)  16.9 us
    ppermute x1, waiting for transfers between devices, shards(): below = lax.ppermute(own, ROW + COL, moves).reshape(1, 2, 8, 8, 256)  14.7 us
    ppermute x1, starting transfers between devices, shards(): other = lax.ppermute(own, 'zh', PAIR)  14 us
    ppermute x1, starting transfers between devices, shards(): part = part + lax.ppermute(part, 'zh', PAIR)  13.2 us
    ppermute x4, starting transfers between devices, doubled(): return jnp.concatenate([value, lax.ppermute(value, axis, PAIR)], axis=0)  12.9 us
    all_to_all x1, waiting for transfers between devices, shards(): lax.all_to_all(parts.astype(F16), ('za', 'zb'), 0, 0, tiled=True)  12.4 us
    all_to_all x1, starting transfers between devices, shards(): terms = lax.all_to_all(terms, PLANE, 0, 0, tiled=True)  6.94 us
  transfers between devices with their start and end apart: 15, of which 12 were waited for; matrix products, arithmetic and copies ran while one was open for 1% of the time, Pallas kernels for 0%

profile of v3, /device:TPU:2, one launch (start us, length us, event | category | flops | bytes accessed | tf_op | source)
XLA Modules:
  0.0 174.9 jit_solution(8080512320583391120)
XLA Ops:
  0.7 1.6 copy-done.2
  3.0 1.7 shard_map.60.own
  4.7 1.9 %collective-permute-start.3 = (bf16[2,8,256,256]{3,2,1,0:T(8,128)(2,1)S(1)}, bf16[2,8,256,256]{3,2,1,0:T(8,128)(2,1)}, u32[]{:S(2)}, u32[]{:S(2)}) collective-permute-start(bf16[2,8,256,256]{3,2,1,0:T(8,128)(2,1)S(1)} %shard_map.60.own), channel_id=1, source_target_pairs={{0,32},{32,0},{1,33},{33,1},{2,34},{34,2},{3,35},{35,3},{4,36},{36... | collective-permute-start | bytes 6291464 | tf_op jit(solution)/shard_map/ppermute | solution.py:205
  7.0 1.0 copy-done.1
  8.0 9.5 %all-to-all-start = ((bf16[32,2,8,8,128]{4,3,2,1,0:T(8,128)(2,1)}), bf16[32,2,8,8,128]{4,3,2,1,0:T(8,128)(2,1)S(1)}, u32[]{:S(2)}, u32[]{:S(2)}) async-start(bf16[32,2,8,8,128]{4,3,2,1,0:T(8,128)(2,1)} %bitcast.23), calls=%async_computation | async-start | bytes 2097152 | tf_op jit(solution)/shard_map/all_to_all | solution.py:202
  17.5 14.0 %collective-permute-start = (bf16[2,8,8,256]{3,2,1,0:T(8,128)(2,1)S(1)}, bf16[2,8,8,256]{3,2,1,0:T(8,128)(2,1)S(1)}, u32[]{:S(2)}, u32[]{:S(2)}) collective-permute-start(bf16[2,8,8,256]{3,2,1,0:T(8,128)(2,1)S(1)} %bitcast.26), channel_id=1, source_target_pairs={{0,16},{16,0},{1,17},{17,1},{2,18},{18,2},{3,19},{19,3},{4,20},{20... | collective-permute-start | bytes 196616 | tf_op jit(solution)/shard_map/ppermute | solution.py:200
  31.5 2.7 %collective-permute-done.panel = bf16[2,8,8,256]{3,2,1,0:T(8,128)(2,1)S(1)} collective-permute-done((bf16[2,8,8,256]{3,2,1,0:T(8,128)(2,1)S(1)}, bf16[2,8,8,256]{3,2,1,0:T(8,128)(2,1)S(1)}, u32[]{:S(2)}, u32[]{:S(2)}) %collective-permute-start) | collective-permute-done | bytes 65568 | tf_op jit(solution)/shard_map/ppermute | solution.py:200
  35.5 7.4 %all-to-all-start.1 = ((bf16[32,2,8,8,128]{4,3,2,1,0:T(8,128)(2,1)}), bf16[32,2,8,8,128]{4,3,2,1,0:T(8,128)(2,1)}, u32[]{:S(2)}, u32[]{:S(2)}) async-start(bf16[32,2,8,8,128]{4,3,2,1,0:T(8,128)(2,1)} %bitcast.22), calls=%async_computation.1 | async-start | bytes 2097152 | tf_op jit(solution)/shard_map/all_to_all | solution.py:208
  42.9 2.0 %collective-permute-start.1 = (bf16[2,8,8,256]{3,2,1,0:T(8,128)(2,1)S(1)}, bf16[2,8,8,256]{3,2,1,0:T(8,128)(2,1)S(1)}, u32[]{:S(2)}, u32[]{:S(2)}) collective-permute-start(bf16[2,8,8,256]{3,2,1,0:T(8,128)(2,1)S(1)} %bitcast.27), channel_id=1, source_target_pairs={{0,0},{1,32},{2,64},{3,96},{4,128},{5,160},{6,192},{7,224},{8,256}... | collective-permute-start | bytes 196616 | tf_op jit(solution)/shard_map/ppermute | solution.py:210
  44.9 14.7 %collective-permute-done.1 = bf16[2,8,8,256]{3,2,1,0:T(8,128)(2,1)S(1)} collective-permute-done((bf16[2,8,8,256]{3,2,1,0:T(8,128)(2,1)S(1)}, bf16[2,8,8,256]{3,2,1,0:T(8,128)(2,1)S(1)}, u32[]{:S(2)}, u32[]{:S(2)}) %collective-permute-start.1) | collective-permute-done | bytes 65568 | tf_op jit(solution)/shard_map/ppermute | solution.py:210
  59.6 6.7 %collective-permute-start.2 = (bf16[1,2,8,8,256]{4,3,2,1,0:T(8,128)(2,1)S(1)}, bf16[1,2,8,8,256]{4,3,2,1,0:T(8,128)(2,1)S(1)}, u32[]{:S(2)}, u32[]{:S(2)}) collective-permute-start(bf16[1,2,8,8,256]{4,3,2,1,0:T(8,128)(2,1)S(1)} %bitcast.30), channel_id=1, source_target_pairs={{0,256},{256,0},{1,257},{257,1},{2,258},{258,2},{3,259},{259,3},{4... | collective-permute-start | bytes 196616 | tf_op jit(solution)/shard_map/ppermute | solution.py:182
  66.3 6.9 %collective-permute-done.2 = bf16[1,2,8,8,256]{4,3,2,1,0:T(8,128)(2,1)S(1)} collective-permute-done((bf16[1,2,8,8,256]{4,3,2,1,0:T(8,128)(2,1)S(1)}, bf16[1,2,8,8,256]{4,3,2,1,0:T(8,128)(2,1)S(1)}, u32[]{:S(2)}, u32[]{:S(2)}) %collective-permute-start.2) | collective-permute-done | bytes 65568 | tf_op jit(solution)/shard_map/ppermute | solution.py:182
  73.3 4.9 %shard_map.62 = f32[4,1040,128]{2,1,0:T(8,128)} custom-call(s32[7]{0:T(128)S(1)} %stack.31.ids, bf16[2,16,2,8,8,128]{5,4,3,2,1,0:T(8,128)(2,1)S(1)} %bitcast.21, bf16[2,16,2,8,8,128]{5,4,3,2,1,0:T(8,128)(2,1)} %bitcast.12.far, bf16[2,8,256,256]{3,2,1,0:T(8,128)(2,1)S(1)} %shard_map.60.own, bf16[2,8,256,256]{3,2,1,0:T(8,128)(2,1)} %collective-permute-done.3.sib), custom_call_target="tpu_custom_call" | custom-call | tf_op jit(solution)/shard_map/pallas_call | solution.py:132
  78.2 2.7 %convert_element_type.12 = f16[4,1040,128]{2,1,0:T(8,128)(2,1)} convert(f32[4,1040,128]{2,1,0:T(8,128)} %shard_map.62) | non-fusion elementwise | flops 532480 | bytes 3194880 | tf_op jit(solution)/shard_map/convert_element_type | solution.py:219
  80.9 3.5 %all-to-all-start.2 = ((f16[4,1040,128]{2,1,0:T(8,128)(2,1)}), f16[4,1040,128]{2,1,0:T(8,128)(2,1)S(1)}, u32[]{:S(2)}, u32[]{:S(2)}) async-start(f16[4,1040,128]{2,1,0:T(8,128)(2,1)} %convert_element_type.12), calls=%async_computation.2 | async-start | bytes 2129920 | tf_op jit(solution)/shard_map/all_to_all | solution.py:219
  84.4 1.9 %collective-permute-start.4 = (bf16[2,2,8,8,256]{4,3,2,1,0:T(8,128)(2,1)S(1)}, bf16[2,2,8,8,256]{4,3,2,1,0:T(8,128)(2,1)S(1)}, u32[]{:S(2)}, u32[]{:S(2)}) collective-permute-start(bf16[2,2,8,8,256]{4,3,2,1,0:T(8,128)(2,1)S(1)} %pad_maximum_fusion.5), channel_id=1, source_target_pairs={{0,128},{128,0},{1,129},{129,1},{2,130},{130,2},{3,131},{131,3},{4... | collective-permute-start | bytes 393224 | tf_op jit(solution)/shard_map/ppermute | solution.py:182
  86.3 13.1 %collective-permute-done.4 = bf16[2,2,8,8,256]{4,3,2,1,0:T(8,128)(2,1)S(1)} collective-permute-done((bf16[2,2,8,8,256]{4,3,2,1,0:T(8,128)(2,1)S(1)}, bf16[2,2,8,8,256]{4,3,2,1,0:T(8,128)(2,1)S(1)}, u32[]{:S(2)}, u32[]{:S(2)}) %collective-permute-start.4) | collective-permute-done | bytes 131104 | tf_op jit(solution)/shard_map/ppermute | solution.py:182
  99.5 1.9 %all-to-all-done.2 = f16[4,1040,128]{2,1,0:T(8,128)(2,1)S(1)} async-done(((f16[4,1040,128]{2,1,0:T(8,128)(2,1)}), f16[4,1040,128]{2,1,0:T(8,128)(2,1)S(1)}, u32[]{:S(2)}, u32[]{:S(2)}) %all-to-all-start.2) | async-done | bytes 1064992 | tf_op jit(solution)/shard_map/all_to_all | solution.py:219
  101.8 2.3 %collective-permute-start.5 = (bf16[4,2,8,8,256]{4,3,2,1,0:T(8,128)(2,1)S(1)}, bf16[4,2,8,8,256]{4,3,2,1,0:T(8,128)(2,1)S(1)}, u32[]{:S(2)}, u32[]{:S(2)}) collective-permute-start(bf16[4,2,8,8,256]{4,3,2,1,0:T(8,128)(2,1)S(1)} %pad_maximum_fusion.3), channel_id=1, source_target_pairs={{0,64},{64,0},{1,65},{65,1},{2,66},{66,2},{3,67},{67,3},{4,68},{68... | collective-permute-start | bytes 786440 | tf_op jit(solution)/shard_map/ppermute | solution.py:182
  104.9 6.5 %all-to-all-start.3 = ((f16[4,272,128]{2,1,0:T(8,128)(2,1)}), f16[4,272,128]{2,1,0:T(8,128)(2,1)S(1)}, u32[]{:S(2)}, u32[]{:S(2)}) async-start(f16[4,272,128]{2,1,0:T(8,128)(2,1)} %convert_element_type.14), calls=%async_computation.3 | async-start | bytes 557056 | tf_op jit(solution)/shard_map/all_to_all | solution.py:228
  111.9 1.9 %collective-permute-start.6 = (bf16[8,2,8,8,256]{4,3,2,1,0:T(8,128)(2,1)S(1)}, bf16[8,2,8,8,256]{4,3,2,1,0:T(8,128)(2,1)S(1)}, u32[]{:S(2)}, u32[]{:S(2)}) collective-permute-start(bf16[8,2,8,8,256]{4,3,2,1,0:T(8,128)(2,1)S(1)} %pad_maximum_fusion.2), channel_id=1, source_target_pairs={{0,32},{32,0},{1,33},{33,1},{2,34},{34,2},{3,35},{35,3},{4,36},{36... | collective-permute-start | bytes 1572872 | tf_op jit(solution)/shard_map/ppermute | solution.py:182
  113.8 1.9 %collective-permute-done.6 = bf16[8,2,8,8,256]{4,3,2,1,0:T(8,128)(2,1)S(1)} collective-permute-done((bf16[8,2,8,8,256]{4,3,2,1,0:T(8,128)(2,1)S(1)}, bf16[8,2,8,8,256]{4,3,2,1,0:T(8,128)(2,1)S(1)}, u32[]{:S(2)}, u32[]{:S(2)}) %collective-permute-start.6) | collective-permute-done | bytes 524320 | tf_op jit(solution)/shard_map/ppermute | solution.py:182
  115.8 12.4 %all-to-all-done.3 = f16[4,272,128]{2,1,0:T(8,128)(2,1)S(1)} async-done(((f16[4,272,128]{2,1,0:T(8,128)(2,1)}), f16[4,272,128]{2,1,0:T(8,128)(2,1)S(1)}, u32[]{:S(2)}, u32[]{:S(2)}) %all-to-all-start.3) | async-done | bytes 278560 | tf_op jit(solution)/shard_map/all_to_all | solution.py:228
  128.3 1.9 %shard_map.63 = (bf16[2,8,16,128]{3,2,1,0:T(8,128)(2,1)S(1)}, f32[16,16,256]{2,1,0:T(8,128)}) custom-call(s32[7]{0:T(128)S(1)} %stack.31.ids, f32[2,8,16,128]{3,2,1,0:T(8,128)S(1)} %bitcast.24, bf16[16,2,8,8,256]{4,3,2,1,0:T(8,128)(2,1)S(1)} %pad_maximum_fusion.below), custom_call_target="tpu_custom_call" | custom-call | tf_op jit(solution)/shard_map/pallas_call | solution.py:166
  130.2 6.9 %all-to-all-start.4 = ((f32[16,16,256]{2,1,0:T(8,128)}), f32[16,16,256]{2,1,0:T(8,128)S(1)}, u32[]{:S(2)}, u32[]{:S(2)}) async-start(f32[16,16,256]{2,1,0:T(8,128)} %get-tuple-element.27), calls=%async_computation.4 | async-start | bytes 524288 | tf_op jit(solution)/shard_map/all_to_all | solution.py:232
  137.1 2.0 %collective-permute-start.7 = (bf16[2,8,16,128]{3,2,1,0:T(8,128)(2,1)S(1)}, bf16[2,8,16,128]{3,2,1,0:T(8,128)(2,1)S(1)}, u32[]{:S(2)}, u32[]{:S(2)}) collective-permute-start(bf16[2,8,16,128]{3,2,1,0:T(8,128)(2,1)S(1)} %get-tuple-element.26), channel_id=1, source_target_pairs={{0,1},{1,0},{2,3},{3,2},{4,5},{5,4},{6,7},{7,6},{8,9},{9,8},{10,11... | collective-permute-start | bytes 196616 | tf_op jit(solution)/shard_map/ppermute | solution.py:233
  139.3 3.9 %collective-permute-done.7 = bf16[2,8,16,128]{3,2,1,0:T(8,128)(2,1)S(1)} collective-permute-done((bf16[2,8,16,128]{3,2,1,0:T(8,128)(2,1)S(1)}, bf16[2,8,16,128]{3,2,1,0:T(8,128)(2,1)S(1)}, u32[]{:S(2)}, u32[]{:S(2)}) %collective-permute-start.7) | collective-permute-done | bytes 65568 | tf_op jit(solution)/shard_map/ppermute | solution.py:233
  143.3 1.8 %all-to-all-done.4 = f32[16,16,256]{2,1,0:T(8,128)S(1)} async-done(((f32[16,16,256]{2,1,0:T(8,128)}), f32[16,16,256]{2,1,0:T(8,128)S(1)}, u32[]{:S(2)}, u32[]{:S(2)}) %all-to-all-start.4) | async-done | bytes 262176 | tf_op jit(solution)/shard_map/all_to_all | solution.py:232
  145.1 13.2 %collective-permute-start.8 = (f32[16,256]{1,0:T(8,128)S(1)}, f32[16,256]{1,0:T(8,128)S(1)}, u32[]{:S(2)}, u32[]{:S(2)}) collective-permute-start(f32[16,256]{1,0:T(8,128)S(1)} %reduce_sum.29), channel_id=1, source_target_pairs={{0,16},{16,0},{1,17},{17,1},{2,18},{18,2},{3,19},{19,3},{4,20},{20... | collective-permute-start | bytes 49160 | tf_op jit(solution)/shard_map/ppermute | solution.py:236
  158.3 1.7 collective-permute-done.8
  161.4 5.5 %all-to-all-start.5 = ((f32[16,16,256]{2,1,0:T(8,128)}), f32[16,16,256]{2,1,0:T(8,128)S(1)}, u32[]{:S(2)}, u32[]{:S(2)}) async-start(f32[16,16,256]{2,1,0:T(8,128)} %broadcast_in_dim.30), calls=%async_computation.5 | async-start | bytes 524288 | tf_op jit(solution)/shard_map/all_to_all | solution.py:240
  167.7 6.5 %all-to-all-done.5 = f32[16,16,256]{2,1,0:T(8,128)S(1)} async-done(((f32[16,16,256]{2,1,0:T(8,128)}), f32[16,16,256]{2,1,0:T(8,128)S(1)}, u32[]{:S(2)}, u32[]{:S(2)}) %all-to-all-start.5) | async-done | bytes 262176 | tf_op jit(solution)/shard_map/all_to_all | solution.py:240
  (40 shorter events, 7.4 us)
Async XLA Ops:
  0.7 1.6 copy-start.2
  2.3 0.7 copy-start.4
  3.0 3.7 %copy-start.3 = (bf16[2,8,1,8,256]{4,3,2,1,0:T(8,128)(2,1)S(1)}, bf16[2,8,1,8,256]{4,3,2,1,0:T(8,128)(2,1)}, u32[]{:S(2)}) copy-start(bf16[2,8,1,8,256]{4,3,2,1,0:T(8,128)(2,1)} %param.5) | copy-start | bytes 196612
  4.7 68.5 %collective-permute-start.3 = (bf16[2,8,256,256]{3,2,1,0:T(8,128)(2,1)S(1)}, bf16[2,8,256,256]{3,2,1,0:T(8,128)(2,1)}, u32[]{:S(2)}, u32[]{:S(2)}) collective-permute-start(bf16[2,8,256,256]{3,2,1,0:T(8,128)(2,1)S(1)} %shard_map.60.own), channel_id=1, source_target_pairs={{0,32},{32,0},{1,33},{33,1},{2,34},{34,2},{3,35},{35,3},{4,36},{36... | collective-permute-start | bytes 6291464 | tf_op jit(solution)/shard_map/ppermute | solution.py:205
  7.0 1.0 copy-start.1
  8.0 26.2 %all-to-all-start = ((bf16[32,2,8,8,128]{4,3,2,1,0:T(8,128)(2,1)}), bf16[32,2,8,8,128]{4,3,2,1,0:T(8,128)(2,1)S(1)}, u32[]{:S(2)}, u32[]{:S(2)}) async-start(bf16[32,2,8,8,128]{4,3,2,1,0:T(8,128)(2,1)} %bitcast.23), calls=%async_computation | async-start | bytes 2097152 | tf_op jit(solution)/shard_map/all_to_all | solution.py:202
  17.5 16.7 %collective-permute-start = (bf16[2,8,8,256]{3,2,1,0:T(8,128)(2,1)S(1)}, bf16[2,8,8,256]{3,2,1,0:T(8,128)(2,1)S(1)}, u32[]{:S(2)}, u32[]{:S(2)}) collective-permute-start(bf16[2,8,8,256]{3,2,1,0:T(8,128)(2,1)S(1)} %bitcast.26), channel_id=1, source_target_pairs={{0,16},{16,0},{1,17},{17,1},{2,18},{18,2},{3,19},{19,3},{4,20},{20... | collective-permute-start | bytes 196616 | tf_op jit(solution)/shard_map/ppermute | solution.py:200
  34.5 1.0 copy-start
  35.5 37.8 %all-to-all-start.1 = ((bf16[32,2,8,8,128]{4,3,2,1,0:T(8,128)(2,1)}), bf16[32,2,8,8,128]{4,3,2,1,0:T(8,128)(2,1)}, u32[]{:S(2)}, u32[]{:S(2)}) async-start(bf16[32,2,8,8,128]{4,3,2,1,0:T(8,128)(2,1)} %bitcast.22), calls=%async_computation.1 | async-start | bytes 2097152 | tf_op jit(solution)/shard_map/all_to_all | solution.py:208
  42.9 16.7 %collective-permute-start.1 = (bf16[2,8,8,256]{3,2,1,0:T(8,128)(2,1)S(1)}, bf16[2,8,8,256]{3,2,1,0:T(8,128)(2,1)S(1)}, u32[]{:S(2)}, u32[]{:S(2)}) collective-permute-start(bf16[2,8,8,256]{3,2,1,0:T(8,128)(2,1)S(1)} %bitcast.27), channel_id=1, source_target_pairs={{0,0},{1,32},{2,64},{3,96},{4,128},{5,160},{6,192},{7,224},{8,256}... | collective-permute-start | bytes 196616 | tf_op jit(solution)/shard_map/ppermute | solution.py:210
  59.6 13.6 %collective-permute-start.2 = (bf16[1,2,8,8,256]{4,3,2,1,0:T(8,128)(2,1)S(1)}, bf16[1,2,8,8,256]{4,3,2,1,0:T(8,128)(2,1)S(1)}, u32[]{:S(2)}, u32[]{:S(2)}) collective-permute-start(bf16[1,2,8,8,256]{4,3,2,1,0:T(8,128)(2,1)S(1)} %bitcast.30), channel_id=1, source_target_pairs={{0,256},{256,0},{1,257},{257,1},{2,258},{258,2},{3,259},{259,3},{4... | collective-permute-start | bytes 196616 | tf_op jit(solution)/shard_map/ppermute | solution.py:182
  80.9 20.6 %all-to-all-start.2 = ((f16[4,1040,128]{2,1,0:T(8,128)(2,1)}), f16[4,1040,128]{2,1,0:T(8,128)(2,1)S(1)}, u32[]{:S(2)}, u32[]{:S(2)}) async-start(f16[4,1040,128]{2,1,0:T(8,128)(2,1)} %convert_element_type.12), calls=%async_computation.2 | async-start | bytes 2129920 | tf_op jit(solution)/shard_map/all_to_all | solution.py:219
  84.4 15.1 %collective-permute-start.4 = (bf16[2,2,8,8,256]{4,3,2,1,0:T(8,128)(2,1)S(1)}, bf16[2,2,8,8,256]{4,3,2,1,0:T(8,128)(2,1)S(1)}, u32[]{:S(2)}, u32[]{:S(2)}) collective-permute-start(bf16[2,2,8,8,256]{4,3,2,1,0:T(8,128)(2,1)S(1)} %pad_maximum_fusion.5), channel_id=1, source_target_pairs={{0,128},{128,0},{1,129},{129,1},{2,130},{130,2},{3,131},{131,3},{4... | collective-permute-start | bytes 393224 | tf_op jit(solution)/shard_map/ppermute | solution.py:182
  101.8 10.0 %collective-permute-start.5 = (bf16[4,2,8,8,256]{4,3,2,1,0:T(8,128)(2,1)S(1)}, bf16[4,2,8,8,256]{4,3,2,1,0:T(8,128)(2,1)S(1)}, u32[]{:S(2)}, u32[]{:S(2)}) collective-permute-start(bf16[4,2,8,8,256]{4,3,2,1,0:T(8,128)(2,1)S(1)} %pad_maximum_fusion.3), channel_id=1, source_target_pairs={{0,64},{64,0},{1,65},{65,1},{2,66},{66,2},{3,67},{67,3},{4,68},{68... | collective-permute-start | bytes 786440 | tf_op jit(solution)/shard_map/ppermute | solution.py:182
  104.9 23.2 %all-to-all-start.3 = ((f16[4,272,128]{2,1,0:T(8,128)(2,1)}), f16[4,272,128]{2,1,0:T(8,128)(2,1)S(1)}, u32[]{:S(2)}, u32[]{:S(2)}) async-start(f16[4,272,128]{2,1,0:T(8,128)(2,1)} %convert_element_type.14), calls=%async_computation.3 | async-start | bytes 557056 | tf_op jit(solution)/shard_map/all_to_all | solution.py:228
  111.9 3.8 %collective-permute-start.6 = (bf16[8,2,8,8,256]{4,3,2,1,0:T(8,128)(2,1)S(1)}, bf16[8,2,8,8,256]{4,3,2,1,0:T(8,128)(2,1)S(1)}, u32[]{:S(2)}, u32[]{:S(2)}) collective-permute-start(bf16[8,2,8,8,256]{4,3,2,1,0:T(8,128)(2,1)S(1)} %pad_maximum_fusion.2), channel_id=1, source_target_pairs={{0,32},{32,0},{1,33},{33,1},{2,34},{34,2},{3,35},{35,3},{4,36},{36... | collective-permute-start | bytes 1572872 | tf_op jit(solution)/shard_map/ppermute | solution.py:182
  115.8 23.4 %copy-start.5 = (s32[8,16]{1,0:T(8,128)S(1)}, s32[8,16]{1,0:T(8,128)}, u32[]{:S(2)}) copy-start(s32[8,16]{1,0:T(8,128)} %st.1) | copy-start | bytes 1540
  130.2 14.9 %all-to-all-start.4 = ((f32[16,16,256]{2,1,0:T(8,128)}), f32[16,16,256]{2,1,0:T(8,128)S(1)}, u32[]{:S(2)}, u32[]{:S(2)}) async-start(f32[16,16,256]{2,1,0:T(8,128)} %get-tuple-element.27), calls=%async_computation.4 | async-start | bytes 524288 | tf_op jit(solution)/shard_map/all_to_all | solution.py:232
  137.1 6.1 %collective-permute-start.7 = (bf16[2,8,16,128]{3,2,1,0:T(8,128)(2,1)S(1)}, bf16[2,8,16,128]{3,2,1,0:T(8,128)(2,1)S(1)}, u32[]{:S(2)}, u32[]{:S(2)}) collective-permute-start(bf16[2,8,16,128]{3,2,1,0:T(8,128)(2,1)S(1)} %get-tuple-element.26), channel_id=1, source_target_pairs={{0,1},{1,0},{2,3},{3,2},{4,5},{5,4},{6,7},{7,6},{8,9},{9,8},{10,11... | collective-permute-start | bytes 196616 | tf_op jit(solution)/shard_map/ppermute | solution.py:233
  145.1 14.9 %collective-permute-start.8 = (f32[16,256]{1,0:T(8,128)S(1)}, f32[16,256]{1,0:T(8,128)S(1)}, u32[]{:S(2)}, u32[]{:S(2)}) collective-permute-start(f32[16,256]{1,0:T(8,128)S(1)} %reduce_sum.29), channel_id=1, source_target_pairs={{0,16},{16,0},{1,17},{17,1},{2,18},{18,2},{3,19},{19,3},{4,20},{20... | collective-permute-start | bytes 49160 | tf_op jit(solution)/shard_map/ppermute | solution.py:236
  161.4 12.8 %all-to-all-start.5 = ((f32[16,16,256]{2,1,0:T(8,128)}), f32[16,16,256]{2,1,0:T(8,128)S(1)}, u32[]{:S(2)}, u32[]{:S(2)}) async-start(f32[16,16,256]{2,1,0:T(8,128)} %broadcast_in_dim.30), calls=%async_computation.5 | async-start | bytes 524288 | tf_op jit(solution)/shard_map/all_to_all | solution.py:240

commit v4 on v3

--- a/solution.py
+++ b/solution.py
@@ -34,23 +34,24 @@
     return st[k, ids[1] // 2] // 2 == ids[1]
 
 
-def pick_kernel(st, ids, block, out):
-    out[:, 0] = jnp.where(present(pl.program_id(0), st, ids), block[...], 0)
+def pick_kernel(st, ids, blocks, out, sem):
+    copies = []
+    for k in range(8):
+        rows = pl.ds(pl.multiple_of(256 * block_row(k, st, ids), 256), 256)
+        lanes = pl.ds(pl.multiple_of(256 * block_col(k, st, ids), 256), 256)
+        copies.append(pltpu.make_async_copy(blocks.at[:, rows, lanes], out.at[:, k], sem.at[k]))
+        copies[-1].start()
+    for copy in copies:
+        copy.wait()
 
 
 def pick_blocks(inverse_anc, structure, ids):
-    def at(k, st, ids):
-        return (0, block_row(k, st, ids), block_col(k, st, ids))
-
     return pl.pallas_call(
         pick_kernel,
-        grid_spec=pltpu.PrefetchScalarGridSpec(
-            num_scalar_prefetch=2,
-            grid=(8,),
-            in_specs=[pl.BlockSpec((2, 256, 256), at)],
-            out_specs=pl.BlockSpec((2, 1, 256, 256), lambda k, st, ids: (0, k, 0, 0)),
-        ),
+        in_specs=[pl.BlockSpec(memory_space=pltpu.SMEM)] * 2 + [pl.BlockSpec(memory_space=pl.ANY)],
+        out_specs=pl.BlockSpec(memory_space=pl.ANY),
         out_shape=jax.ShapeDtypeStruct((2, 8, 256, 256), BF),
+        scratch_shapes=[pltpu.SemaphoreType.DMA((8,))],
         compiler_params=params(),
     )(structure, ids, inverse_anc)
 
@@ -83,7 +84,7 @@
     )(panel)
 
 
-def product_kernel(ids, near, far, own, sib, out):
+def product_kernel(st, ids, near, far, own, sib, out):
     core = ids[2]
     zh = ids[4]
     form = (((0,), (0,)), ((), ()))
@@ -109,6 +110,7 @@
             )
             both = one + two
             total = both if total is None else total + both
+        total = jnp.where(present(k, st, ids), total, 0.0)
         size = jnp.max(jnp.abs(total).reshape(16, 8, 512), axis=0)
         for lane in range(4):
             largest = jnp.maximum(largest, size[:, 128 * lane : 128 * lane + 128])
@@ -128,14 +130,14 @@
         out[chunk, 1024:] = jnp.broadcast_to(power, (16, 128))
 
 
-def products(ids, near, far, own, sib):
+def products(structure, ids, near, far, own, sib):
     return pl.pallas_call(
         product_kernel,
-        in_specs=[pl.BlockSpec(memory_space=pltpu.SMEM)] + whole(4),
+        in_specs=[pl.BlockSpec(memory_space=pltpu.SMEM)] * 2 + whole(4),
         out_specs=whole(1)[0],
         out_shape=jax.ShapeDtypeStruct((4, 1040, 128), F32),
         compiler_params=params(),
-    )(ids, near, far, own, sib)
+    )(structure, ids, near, far, own, sib)
 
 
 def diag_kernel(ids, summed, below, half, out):
@@ -190,12 +192,6 @@
     own = lower_panel.reshape(2, 8, 8, 256)
     tie = lax.optimization_barrier
 
-    moves = []
-    for q in range(16):
-        for h in range(2):
-            for m in range(16):
-                moves.append((q * 32 + 16 * h + m, m * 32 + 2 * q + h))
-
     group = ("core",) + PLANE
     other = lax.ppermute(own, "zh", PAIR)
     lanes = split_lanes(own)
@@ -206,34 +202,42 @@
     other, near, mine = tie((other, near, mine))
     lanes = split_lanes(other)
     far = lax.all_to_all(lanes.reshape(32, 2, 8, 8, 128), group, 0, 0, tiled=True)
+
     own = tie((own, lanes))[0]
-    below = lax.ppermute(own, ROW + COL, moves).reshape(1, 2, 8, 8, 256)
-    below = doubled(below, "za")
+    below = []
+    for flip in (0, 8):
+        moves = []
+        for q in range(16):
+            for h in range(2):
+                for m in range(16):
+                    moves.append((q * 32 + 16 * h + m, (m ^ flip) * 32 + 2 * q + h))
+        below.append(lax.ppermute(own, ROW + COL, moves))
+    below = jnp.stack(below)
     far, below = tie((far, below))
 
     near = near.reshape(2, 16, 2, 8, 8, 128)
     far = far.reshape(2, 16, 2, 8, 8, 128)
-    parts = products(ids, near, far, mine, sib)
+    parts = products(structure, ids, near, far, mine, sib)
     below, parts = tie((below, parts))
     below = doubled(below, "zb")
     got = lax.all_to_all(parts.astype(F16), ("zc", "h"), 0, 0, tiled=True).astype(F32)
     power = got[:, 1024:1025]
     most = jnp.max(power, axis=0, keepdims=True) + 2.0
     parts = jnp.sum(got[:, :1024] * jnp.exp2(power - most), axis=0).reshape(4, 256, 128)
-    parts = jnp.concatenate([parts, jnp.broadcast_to(most, (4, 16, 128))], axis=1)
+    parts = jnp.concatenate([parts, jnp.broadcast_to(most, (4, 16, 128))], axis=1).astype(F16)
 
     below, parts = tie((below, parts))
     below = doubled(below, "zc")
     below = doubled(below, "core")
-    got = lax.all_to_all(parts.astype(F16), ("za", "zb"), 0, 0, tiled=True).astype(F32)
+    got = lax.all_to_all(parts, ("za", "zb"), 0, 0, tiled=True).astype(F32)
     summed = jnp.sum(got[:, :256] * jnp.exp2(got[:, 256:257] - 14.0), axis=0)
     half, terms = diag_terms(ids, summed.reshape(2, 8, 16, 128), below)
 
     terms = lax.all_to_all(terms, PLANE, 0, 0, tiled=True)
     partner = lax.ppermute(half, "h", PAIR)
-    terms, partner = tie((terms, partner))
     part = jnp.sum(terms, axis=0)
     part = part + lax.ppermute(part, "zh", PAIR)
+    part, partner = tie((part, partner))
     place = lax.axis_index(PLANE)
     start = lax.dynamic_index_in_dim(diag_inverse.reshape(16, 16, 256), place, 0, keepdims=False)
     diag = jnp.broadcast_to((start - part)[None], (16, 16, 256))

time: 176 us -> 174 us (0.989)
  waiting for transfers between devices: 67.9 us -> 54.2 us
  starting transfers between devices: 85.3 us -> 97.4 us
  local copies, waits for them, and re-layouts: 5.75 us -> 3.82 us
    ppermute x1 -> x2, starting transfers between devices: 2.03 us -> 16.8 us  [shards(): below.append(lax.ppermute(own, ROW + COL, moves))]
    ppermute x1 -> x2, waiting for transfers between devices: 14.7 us -> 4.46 us  [shards(): below.append(lax.ppermute(own, ROW + COL, moves))]
    ppermute x4 -> x3, waiting for transfers between devices: 22.3 us -> 13.3 us  [doubled(): return jnp.concatenate([value, lax.ppermute(value, axis, PAIR)], axis=0)]
    ppermute x1, starting transfers between devices: 13.2 us -> 6.32 us  [shards(): part = part + lax.ppermute(part, 'zh', PAIR)]
    ppermute x1, waiting for transfers between devices: 1.68 us -> 7.81 us  [shards(): part = part + lax.ppermute(part, 'zh', PAIR)]
    all_to_all x1, starting transfers between devices: 3.51 us -> 9.52 us  [shards(): lax.all_to_all(parts.astype(F16), ('zc', 'h'), 0, 0, tiled=True).astype(F32)]
    all_to_all x1, waiting for transfers between devices: 1.8 us -> 6.02 us  [shards(): terms = lax.all_to_all(terms, PLANE, 0, 0, tiled=True)]
    ppermute x1, waiting for transfers between devices: 3.91 us -> 0.01 us  [shards(): partner = lax.ppermute(half, 'h', PAIR)]
  transfers between devices with their start and end apart: 15 -> 15, of which waited for: 12 -> 10; matrix products, arithmetic and copies ran while one was open for 1% -> 1% of each run, Pallas kernels for 0% -> 2%
where the time goes in v4:
time: 174 us; the launch traced here: 173 us
  starting transfers between devices  97.4 us (56%)
  waiting for transfers between devices  54.2 us (31%)
  Pallas kernels  10.4 us (6%)
  other arithmetic  5.92 us (3%)
  local copies, waits for them, and re-layouts  3.82 us (2%)
    all_to_all x2, starting transfers between devices, shards(): lax.all_to_all(lanes.reshape(32, 2, 8, 8, 128), group, 0, 0, tiled=True)  16.9 us
    ppermute x2, starting transfers between devices, shards(): below.append(lax.ppermute(own, ROW + COL, moves))  16.8 us
    ppermute x1, starting transfers between devices, shards(): other = lax.ppermute(own, 'zh', PAIR)  14 us
    ppermute x3, waiting for transfers between devices, doubled(): return jnp.concatenate([value, lax.ppermute(value, axis, PAIR)], axis=0)  13.3 us
    ppermute x3, starting transfers between devices, doubled(): return jnp.concatenate([value, lax.ppermute(value, axis, PAIR)], axis=0)  12.7 us
    all_to_all x1, waiting for transfers between devices, shards(): got = lax.all_to_all(parts, ('za', 'zb'), 0, 0, tiled=True).astype(F32)  11.5 us
    all_to_all x1, starting transfers between devices, shards(): lax.all_to_all(parts.astype(F16), ('zc', 'h'), 0, 0, tiled=True).astype(F32)  9.52 us
    all_to_all x1, starting transfers between devices, shards(): terms = lax.all_to_all(terms, PLANE, 0, 0, tiled=True)  9 us
  transfers between devices with their start and end apart: 15, of which 10 were waited for; matrix products, arithmetic and copies ran while one was open for 1% of the time, Pallas kernels for 2%

profile of v4, /device:TPU:2, one launch (start us, length us, event | category | flops | bytes accessed | tf_op | source)
XLA Modules:
  0.0 172.7 jit_solution(1369870253205704625)
XLA Ops:
  0.7 1.6 copy-done
  3.0 1.0 shard_map.60.own
  4.0 1.9 %collective-permute-start.3 = (bf16[2,8,256,256]{3,2,1,0:T(8,128)(2,1)S(1)}, bf16[2,8,256,256]{3,2,1,0:T(8,128)(2,1)}, u32[]{:S(2)}, u32[]{:S(2)}) collective-permute-start(bf16[2,8,256,256]{3,2,1,0:T(8,128)(2,1)S(1)} %shard_map.60.own), channel_id=1, source_target_pairs={{0,32},{32,0},{1,33},{33,1},{2,34},{34,2},{3,35},{35,3},{4,36},{36... | collective-permute-start | bytes 6291464 | tf_op jit(solution)/shard_map/ppermute | solution.py:201
  6.0 1.3 shard_map.59
  7.3 9.5 %all-to-all-start = ((bf16[32,2,8,8,128]{4,3,2,1,0:T(8,128)(2,1)}), bf16[32,2,8,8,128]{4,3,2,1,0:T(8,128)(2,1)S(1)}, u32[]{:S(2)}, u32[]{:S(2)}) async-start(bf16[32,2,8,8,128]{4,3,2,1,0:T(8,128)(2,1)} %bitcast.8), calls=%async_computation | async-start | bytes 2097152 | tf_op jit(solution)/shard_map/all_to_all | solution.py:198
  16.8 14.0 %collective-permute-start = (bf16[2,8,8,256]{3,2,1,0:T(8,128)(2,1)S(1)}, bf16[2,8,8,256]{3,2,1,0:T(8,128)(2,1)S(1)}, u32[]{:S(2)}, u32[]{:S(2)}) collective-permute-start(bf16[2,8,8,256]{3,2,1,0:T(8,128)(2,1)S(1)} %bitcast.25), channel_id=1, source_target_pairs={{0,16},{16,0},{1,17},{17,1},{2,18},{18,2},{3,19},{19,3},{4,20},{20... | collective-permute-start | bytes 196616 | tf_op jit(solution)/shard_map/ppermute | solution.py:196
  30.7 2.7 %collective-permute-done.panel = bf16[2,8,8,256]{3,2,1,0:T(8,128)(2,1)S(1)} collective-permute-done((bf16[2,8,8,256]{3,2,1,0:T(8,128)(2,1)S(1)}, bf16[2,8,8,256]{3,2,1,0:T(8,128)(2,1)S(1)}, u32[]{:S(2)}, u32[]{:S(2)}) %collective-permute-start) | collective-permute-done | bytes 65568 | tf_op jit(solution)/shard_map/ppermute | solution.py:196
  33.4 1.3 shard_map.61
  34.7 7.4 %all-to-all-start.1 = ((bf16[32,2,8,8,128]{4,3,2,1,0:T(8,128)(2,1)}), bf16[32,2,8,8,128]{4,3,2,1,0:T(8,128)(2,1)}, u32[]{:S(2)}, u32[]{:S(2)}) async-start(bf16[32,2,8,8,128]{4,3,2,1,0:T(8,128)(2,1)} %bitcast.9), calls=%async_computation.1 | async-start | bytes 2097152 | tf_op jit(solution)/shard_map/all_to_all | solution.py:204
  42.2 2.0 %collective-permute-start.1 = (bf16[2,8,8,256]{3,2,1,0:T(8,128)(2,1)S(1)}, bf16[2,8,8,256]{3,2,1,0:T(8,128)(2,1)S(1)}, u32[]{:S(2)}, u32[]{:S(2)}) collective-permute-start(bf16[2,8,8,256]{3,2,1,0:T(8,128)(2,1)S(1)} %bitcast.26), channel_id=1, source_target_pairs={{0,0},{1,32},{2,64},{3,96},{4,128},{5,160},{6,192},{7,224},{8,256}... | collective-permute-start | bytes 196616 | tf_op jit(solution)/shard_map/ppermute | solution.py:214
  44.2 14.7 %collective-permute-start.2 = (bf16[2,8,8,256]{3,2,1,0:T(8,128)(2,1)S(1)}, bf16[2,8,8,256]{3,2,1,0:T(8,128)(2,1)S(1)}, u32[]{:S(2)}, u32[]{:S(2)}) collective-permute-start(bf16[2,8,8,256]{3,2,1,0:T(8,128)(2,1)S(1)} %bitcast.27), channel_id=1, source_target_pairs={{0,256},{1,288},{2,320},{3,352},{4,384},{5,416},{6,448},{7,480},{8... | collective-permute-start | bytes 196616 | tf_op jit(solution)/shard_map/ppermute | solution.py:214
  59.0 4.5 %collective-permute-done.2 = bf16[2,8,8,256]{3,2,1,0:T(8,128)(2,1)S(1)} collective-permute-done((bf16[2,8,8,256]{3,2,1,0:T(8,128)(2,1)S(1)}, bf16[2,8,8,256]{3,2,1,0:T(8,128)(2,1)S(1)}, u32[]{:S(2)}, u32[]{:S(2)}) %collective-permute-start.2) | collective-permute-done | bytes 65568 | tf_op jit(solution)/shard_map/ppermute | solution.py:214
  63.5 4.9 %shard_map.62 = f32[4,1040,128]{2,1,0:T(8,128)} custom-call(s32[8,16]{1,0:T(8,128)S(1)} %copy-done.3, s32[7]{0:T(128)S(1)} %stack.40.ids, bf16[2,16,2,8,8,128]{5,4,3,2,1,0:T(8,128)(2,1)S(1)} %bitcast.22, bf16[2,16,2,8,8,128]{5,4,3,2,1,0:T(8,128)(2,1)} %bitcast.13.far, bf16[2,8,256,256]{3,2,1,0:T(8,128)(2,1)S(1)} %shard_map.60.own, ...), custom_call_target="tpu_custom_call" | custom-call | tf_op jit(solution)/shard_map/pallas_call | solution.py:134
  68.4 2.7 %convert_element_type.10 = f16[4,1040,128]{2,1,0:T(8,128)(2,1)} convert(f32[4,1040,128]{2,1,0:T(8,128)} %shard_map.62) | non-fusion elementwise | flops 532480 | bytes 3194880 | tf_op jit(solution)/shard_map/convert_element_type | solution.py:223
  71.1 9.5 %all-to-all-start.2 = ((f16[4,1040,128]{2,1,0:T(8,128)(2,1)}), f16[4,1040,128]{2,1,0:T(8,128)(2,1)S(1)}, u32[]{:S(2)}, u32[]{:S(2)}) async-start(f16[4,1040,128]{2,1,0:T(8,128)(2,1)} %convert_element_type.10), calls=%async_computation.2 | async-start | bytes 2129920 | tf_op jit(solution)/shard_map/all_to_all | solution.py:223
  80.6 6.1 %collective-permute-start.4 = (bf16[2,2,8,8,256]{4,3,2,1,0:T(8,128)(2,1)S(1)}, bf16[2,2,8,8,256]{4,3,2,1,0:T(8,128)(2,1)S(1)}, u32[]{:S(2)}, u32[]{:S(2)}) collective-permute-start(bf16[2,2,8,8,256]{4,3,2,1,0:T(8,128)(2,1)S(1)} %pad_maximum_fusion.5), channel_id=1, source_target_pairs={{0,128},{128,0},{1,129},{129,1},{2,130},{130,2},{3,131},{131,3},{4... | collective-permute-start | bytes 393224 | tf_op jit(solution)/shard_map/ppermute | solution.py:184
  86.7 9.4 %collective-permute-done.4 = bf16[2,2,8,8,256]{4,3,2,1,0:T(8,128)(2,1)S(1)} collective-permute-done((bf16[2,2,8,8,256]{4,3,2,1,0:T(8,128)(2,1)S(1)}, bf16[2,2,8,8,256]{4,3,2,1,0:T(8,128)(2,1)S(1)}, u32[]{:S(2)}, u32[]{:S(2)}) %collective-permute-start.4) | collective-permute-done | bytes 131104 | tf_op jit(solution)/shard_map/ppermute | solution.py:184
  96.1 1.9 %all-to-all-done.2 = f16[4,1040,128]{2,1,0:T(8,128)(2,1)S(1)} async-done(((f16[4,1040,128]{2,1,0:T(8,128)(2,1)}), f16[4,1040,128]{2,1,0:T(8,128)(2,1)S(1)}, u32[]{:S(2)}, u32[]{:S(2)}) %all-to-all-start.2) | async-done | bytes 1064992 | tf_op jit(solution)/shard_map/all_to_all | solution.py:223
  99.2 4.7 %collective-permute-start.5 = (bf16[4,2,8,8,256]{4,3,2,1,0:T(8,128)(2,1)S(1)}, bf16[4,2,8,8,256]{4,3,2,1,0:T(8,128)(2,1)S(1)}, u32[]{:S(2)}, u32[]{:S(2)}) collective-permute-start(bf16[4,2,8,8,256]{4,3,2,1,0:T(8,128)(2,1)S(1)} %pad_maximum_fusion.3), channel_id=1, source_target_pairs={{0,64},{64,0},{1,65},{65,1},{2,66},{66,2},{3,67},{67,3},{4,68},{68... | collective-permute-start | bytes 786440 | tf_op jit(solution)/shard_map/ppermute | solution.py:184
  103.9 3.5 %all-to-all-start.3 = ((f16[4,272,128]{2,1,0:T(8,128)(2,1)}), f16[4,272,128]{2,1,0:T(8,128)(2,1)S(1)}, u32[]{:S(2)}, u32[]{:S(2)}) async-start(f16[4,272,128]{2,1,0:T(8,128)(2,1)} %pad_maximum_fusion.2), calls=%async_computation.3 | async-start | bytes 557056 | tf_op jit(solution)/shard_map/all_to_all | solution.py:232
  107.4 2.0 %collective-permute-done.5 = bf16[4,2,8,8,256]{4,3,2,1,0:T(8,128)(2,1)S(1)} collective-permute-done((bf16[4,2,8,8,256]{4,3,2,1,0:T(8,128)(2,1)S(1)}, bf16[4,2,8,8,256]{4,3,2,1,0:T(8,128)(2,1)S(1)}, u32[]{:S(2)}, u32[]{:S(2)}) %collective-permute-start.5) | collective-permute-done | bytes 262176 | tf_op jit(solution)/shard_map/ppermute | solution.py:184
  109.5 1.9 %collective-permute-start.6 = (bf16[8,2,8,8,256]{4,3,2,1,0:T(8,128)(2,1)S(1)}, bf16[8,2,8,8,256]{4,3,2,1,0:T(8,128)(2,1)S(1)}, u32[]{:S(2)}, u32[]{:S(2)}) collective-permute-start(bf16[8,2,8,8,256]{4,3,2,1,0:T(8,128)(2,1)S(1)} %pad_maximum_fusion.1), channel_id=1, source_target_pairs={{0,32},{32,0},{1,33},{33,1},{2,34},{34,2},{3,35},{35,3},{4,36},{36... | collective-permute-start | bytes 1572872 | tf_op jit(solution)/shard_map/ppermute | solution.py:184
  111.4 1.9 %collective-permute-done.6 = bf16[8,2,8,8,256]{4,3,2,1,0:T(8,128)(2,1)S(1)} collective-permute-done((bf16[8,2,8,8,256]{4,3,2,1,0:T(8,128)(2,1)S(1)}, bf16[8,2,8,8,256]{4,3,2,1,0:T(8,128)(2,1)S(1)}, u32[]{:S(2)}, u32[]{:S(2)}) %collective-permute-start.6) | collective-permute-done | bytes 524320 | tf_op jit(solution)/shard_map/ppermute | solution.py:184
  113.4 11.5 %all-to-all-done.3 = f16[4,272,128]{2,1,0:T(8,128)(2,1)S(1)} async-done(((f16[4,272,128]{2,1,0:T(8,128)(2,1)}), f16[4,272,128]{2,1,0:T(8,128)(2,1)S(1)}, u32[]{:S(2)}, u32[]{:S(2)}) %all-to-all-start.3) | async-done | bytes 278560 | tf_op jit(solution)/shard_map/all_to_all | solution.py:232
  125.0 1.9 %shard_map.63 = (bf16[2,8,16,128]{3,2,1,0:T(8,128)(2,1)S(1)}, f32[16,16,256]{2,1,0:T(8,128)}) custom-call(s32[7]{0:T(128)S(1)} %stack.40.ids, f32[2,8,16,128]{3,2,1,0:T(8,128)S(1)} %bitcast.23, bf16[16,2,8,8,256]{4,3,2,1,0:T(8,128)(2,1)S(1)} %pad_maximum_fusion.below), custom_call_target="tpu_custom_call" | custom-call | tf_op jit(solution)/shard_map/pallas_call | solution.py:168
  126.9 9.0 %all-to-all-start.4 = ((f32[16,16,256]{2,1,0:T(8,128)}), f32[16,16,256]{2,1,0:T(8,128)S(1)}, u32[]{:S(2)}, u32[]{:S(2)}) async-start(f32[16,16,256]{2,1,0:T(8,128)} %get-tuple-element.27), calls=%async_computation.4 | async-start | bytes 524288 | tf_op jit(solution)/shard_map/all_to_all | solution.py:236
  135.9 2.0 %collective-permute-start.8 = (bf16[2,8,16,128]{3,2,1,0:T(8,128)(2,1)S(1)}, bf16[2,8,16,128]{3,2,1,0:T(8,128)(2,1)S(1)}, u32[]{:S(2)}, u32[]{:S(2)}) collective-permute-start(bf16[2,8,16,128]{3,2,1,0:T(8,128)(2,1)S(1)} %get-tuple-element.26), channel_id=1, source_target_pairs={{0,1},{1,0},{2,3},{3,2},{4,5},{5,4},{6,7},{7,6},{8,9},{9,8},{10,11... | collective-permute-start | bytes 196616 | tf_op jit(solution)/shard_map/ppermute | solution.py:237
  137.9 6.0 %all-to-all-done.4 = f32[16,16,256]{2,1,0:T(8,128)S(1)} async-done(((f32[16,16,256]{2,1,0:T(8,128)}), f32[16,16,256]{2,1,0:T(8,128)S(1)}, u32[]{:S(2)}, u32[]{:S(2)}) %all-to-all-start.4) | async-done | bytes 262176 | tf_op jit(solution)/shard_map/all_to_all | solution.py:236
  143.9 6.3 %collective-permute-start.7 = (f32[16,256]{1,0:T(8,128)S(1)}, f32[16,256]{1,0:T(8,128)S(1)}, u32[]{:S(2)}, u32[]{:S(2)}) collective-permute-start(f32[16,256]{1,0:T(8,128)S(1)} %reduce_sum.29), channel_id=1, source_target_pairs={{0,16},{16,0},{1,17},{17,1},{2,18},{18,2},{3,19},{19,3},{4,20},{20... | collective-permute-start | bytes 49160 | tf_op jit(solution)/shard_map/ppermute | solution.py:239
  150.5 7.8 %collective-permute-done.7 = f32[16,256]{1,0:T(8,128)S(1)} collective-permute-done((f32[16,256]{1,0:T(8,128)S(1)}, f32[16,256]{1,0:T(8,128)S(1)}, u32[]{:S(2)}, u32[]{:S(2)}) %collective-permute-start.7) | collective-permute-done | bytes 16416 | tf_op jit(solution)/shard_map/ppermute | solution.py:239
  159.7 4.8 %all-to-all-start.5 = ((f32[16,16,256]{2,1,0:T(8,128)}), f32[16,16,256]{2,1,0:T(8,128)S(1)}, u32[]{:S(2)}, u32[]{:S(2)}) async-start(f32[16,16,256]{2,1,0:T(8,128)} %broadcast_in_dim.30), calls=%async_computation.5 | async-start | bytes 524288 | tf_op jit(solution)/shard_map/all_to_all | solution.py:244
  165.4 6.6 %all-to-all-done.5 = f32[16,16,256]{2,1,0:T(8,128)S(1)} async-done(((f32[16,16,256]{2,1,0:T(8,128)}), f32[16,16,256]{2,1,0:T(8,128)S(1)}, u32[]{:S(2)}, u32[]{:S(2)}) %all-to-all-start.5) | async-done | bytes 262176 | tf_op jit(solution)/shard_map/all_to_all | solution.py:244
  (37 shorter events, 5.4 us)
Async XLA Ops:
  0.7 1.6 copy-start
  2.3 0.7 copy-start.2
  3.0 2.9 %copy-start.1 = (bf16[2,8,1,8,256]{4,3,2,1,0:T(8,128)(2,1)S(1)}, bf16[2,8,1,8,256]{4,3,2,1,0:T(8,128)(2,1)}, u32[]{:S(2)}) copy-start(bf16[2,8,1,8,256]{4,3,2,1,0:T(8,128)(2,1)} %param.5) | copy-start | bytes 196612
  4.0 59.5 %collective-permute-start.3 = (bf16[2,8,256,256]{3,2,1,0:T(8,128)(2,1)S(1)}, bf16[2,8,256,256]{3,2,1,0:T(8,128)(2,1)}, u32[]{:S(2)}, u32[]{:S(2)}) collective-permute-start(bf16[2,8,256,256]{3,2,1,0:T(8,128)(2,1)S(1)} %shard_map.60.own), channel_id=1, source_target_pairs={{0,32},{32,0},{1,33},{33,1},{2,34},{34,2},{3,35},{35,3},{4,36},{36... | collective-permute-start | bytes 6291464 | tf_op jit(solution)/shard_map/ppermute | solution.py:201
  7.3 26.2 %all-to-all-start = ((bf16[32,2,8,8,128]{4,3,2,1,0:T(8,128)(2,1)}), bf16[32,2,8,8,128]{4,3,2,1,0:T(8,128)(2,1)S(1)}, u32[]{:S(2)}, u32[]{:S(2)}) async-start(bf16[32,2,8,8,128]{4,3,2,1,0:T(8,128)(2,1)} %bitcast.8), calls=%async_computation | async-start | bytes 2097152 | tf_op jit(solution)/shard_map/all_to_all | solution.py:198
  16.8 46.7 %copy-start.3 = (s32[8,16]{1,0:T(8,128)S(1)}, s32[8,16]{1,0:T(8,128)}, u32[]{:S(2)}) copy-start(s32[8,16]{1,0:T(8,128)} %st.3) | copy-start | bytes 1540
  16.8 16.7 %collective-permute-start = (bf16[2,8,8,256]{3,2,1,0:T(8,128)(2,1)S(1)}, bf16[2,8,8,256]{3,2,1,0:T(8,128)(2,1)S(1)}, u32[]{:S(2)}, u32[]{:S(2)}) collective-permute-start(bf16[2,8,8,256]{3,2,1,0:T(8,128)(2,1)S(1)} %bitcast.25), channel_id=1, source_target_pairs={{0,16},{16,0},{1,17},{17,1},{2,18},{18,2},{3,19},{19,3},{4,20},{20... | collective-permute-start | bytes 196616 | tf_op jit(solution)/shard_map/ppermute | solution.py:196
  34.7 28.7 %all-to-all-start.1 = ((bf16[32,2,8,8,128]{4,3,2,1,0:T(8,128)(2,1)}), bf16[32,2,8,8,128]{4,3,2,1,0:T(8,128)(2,1)}, u32[]{:S(2)}, u32[]{:S(2)}) async-start(bf16[32,2,8,8,128]{4,3,2,1,0:T(8,128)(2,1)} %bitcast.9), calls=%async_computation.1 | async-start | bytes 2097152 | tf_op jit(solution)/shard_map/all_to_all | solution.py:204
  42.2 16.8 %collective-permute-start.1 = (bf16[2,8,8,256]{3,2,1,0:T(8,128)(2,1)S(1)}, bf16[2,8,8,256]{3,2,1,0:T(8,128)(2,1)S(1)}, u32[]{:S(2)}, u32[]{:S(2)}) collective-permute-start(bf16[2,8,8,256]{3,2,1,0:T(8,128)(2,1)S(1)} %bitcast.26), channel_id=1, source_target_pairs={{0,0},{1,32},{2,64},{3,96},{4,128},{5,160},{6,192},{7,224},{8,256}... | collective-permute-start | bytes 196616 | tf_op jit(solution)/shard_map/ppermute | solution.py:214
  44.2 19.2 %collective-permute-start.2 = (bf16[2,8,8,256]{3,2,1,0:T(8,128)(2,1)S(1)}, bf16[2,8,8,256]{3,2,1,0:T(8,128)(2,1)S(1)}, u32[]{:S(2)}, u32[]{:S(2)}) collective-permute-start(bf16[2,8,8,256]{3,2,1,0:T(8,128)(2,1)S(1)} %bitcast.27), channel_id=1, source_target_pairs={{0,256},{1,288},{2,320},{3,352},{4,384},{5,416},{6,448},{7,480},{8... | collective-permute-start | bytes 196616 | tf_op jit(solution)/shard_map/ppermute | solution.py:214
  71.1 26.9 %all-to-all-start.2 = ((f16[4,1040,128]{2,1,0:T(8,128)(2,1)}), f16[4,1040,128]{2,1,0:T(8,128)(2,1)S(1)}, u32[]{:S(2)}, u32[]{:S(2)}) async-start(f16[4,1040,128]{2,1,0:T(8,128)(2,1)} %convert_element_type.10), calls=%async_computation.2 | async-start | bytes 2129920 | tf_op jit(solution)/shard_map/all_to_all | solution.py:223
  80.6 15.4 %collective-permute-start.4 = (bf16[2,2,8,8,256]{4,3,2,1,0:T(8,128)(2,1)S(1)}, bf16[2,2,8,8,256]{4,3,2,1,0:T(8,128)(2,1)S(1)}, u32[]{:S(2)}, u32[]{:S(2)}) collective-permute-start(bf16[2,2,8,8,256]{4,3,2,1,0:T(8,128)(2,1)S(1)} %pad_maximum_fusion.5), channel_id=1, source_target_pairs={{0,128},{128,0},{1,129},{129,1},{2,130},{130,2},{3,131},{131,3},{4... | collective-permute-start | bytes 393224 | tf_op jit(solution)/shard_map/ppermute | solution.py:184
  99.2 10.2 %collective-permute-start.5 = (bf16[4,2,8,8,256]{4,3,2,1,0:T(8,128)(2,1)S(1)}, bf16[4,2,8,8,256]{4,3,2,1,0:T(8,128)(2,1)S(1)}, u32[]{:S(2)}, u32[]{:S(2)}) collective-permute-start(bf16[4,2,8,8,256]{4,3,2,1,0:T(8,128)(2,1)S(1)} %pad_maximum_fusion.3), channel_id=1, source_target_pairs={{0,64},{64,0},{1,65},{65,1},{2,66},{66,2},{3,67},{67,3},{4,68},{68... | collective-permute-start | bytes 786440 | tf_op jit(solution)/shard_map/ppermute | solution.py:184
  103.9 20.9 %all-to-all-start.3 = ((f16[4,272,128]{2,1,0:T(8,128)(2,1)}), f16[4,272,128]{2,1,0:T(8,128)(2,1)S(1)}, u32[]{:S(2)}, u32[]{:S(2)}) async-start(f16[4,272,128]{2,1,0:T(8,128)(2,1)} %pad_maximum_fusion.2), calls=%async_computation.3 | async-start | bytes 557056 | tf_op jit(solution)/shard_map/all_to_all | solution.py:232
  109.5 3.8 %collective-permute-start.6 = (bf16[8,2,8,8,256]{4,3,2,1,0:T(8,128)(2,1)S(1)}, bf16[8,2,8,8,256]{4,3,2,1,0:T(8,128)(2,1)S(1)}, u32[]{:S(2)}, u32[]{:S(2)}) collective-permute-start(bf16[8,2,8,8,256]{4,3,2,1,0:T(8,128)(2,1)S(1)} %pad_maximum_fusion.1), channel_id=1, source_target_pairs={{0,32},{32,0},{1,33},{33,1},{2,34},{34,2},{3,35},{35,3},{4,36},{36... | collective-permute-start | bytes 1572872 | tf_op jit(solution)/shard_map/ppermute | solution.py:184
  126.9 17.0 %all-to-all-start.4 = ((f32[16,16,256]{2,1,0:T(8,128)}), f32[16,16,256]{2,1,0:T(8,128)S(1)}, u32[]{:S(2)}, u32[]{:S(2)}) async-start(f32[16,16,256]{2,1,0:T(8,128)} %get-tuple-element.27), calls=%async_computation.4 | async-start | bytes 524288 | tf_op jit(solution)/shard_map/all_to_all | solution.py:236
  135.9 22.4 %collective-permute-start.8 = (bf16[2,8,16,128]{3,2,1,0:T(8,128)(2,1)S(1)}, bf16[2,8,16,128]{3,2,1,0:T(8,128)(2,1)S(1)}, u32[]{:S(2)}, u32[]{:S(2)}) collective-permute-start(bf16[2,8,16,128]{3,2,1,0:T(8,128)(2,1)S(1)} %get-tuple-element.26), channel_id=1, source_target_pairs={{0,1},{1,0},{2,3},{3,2},{4,5},{5,4},{6,7},{7,6},{8,9},{9,8},{10,11... | collective-permute-start | bytes 196616 | tf_op jit(solution)/shard_map/ppermute | solution.py:237
  143.9 14.3 %collective-permute-start.7 = (f32[16,256]{1,0:T(8,128)S(1)}, f32[16,256]{1,0:T(8,128)S(1)}, u32[]{:S(2)}, u32[]{:S(2)}) collective-permute-start(f32[16,256]{1,0:T(8,128)S(1)} %reduce_sum.29), channel_id=1, source_target_pairs={{0,16},{16,0},{1,17},{17,1},{2,18},{18,2},{3,19},{19,3},{4,20},{20... | collective-permute-start | bytes 49160 | tf_op jit(solution)/shard_map/ppermute | solution.py:239
  159.7 12.2 %all-to-all-start.5 = ((f32[16,16,256]{2,1,0:T(8,128)}), f32[16,16,256]{2,1,0:T(8,128)S(1)}, u32[]{:S(2)}, u32[]{:S(2)}) async-start(f32[16,16,256]{2,1,0:T(8,128)} %broadcast_in_dim.30), calls=%async_computation.5 | async-start | bytes 524288 | tf_op jit(solution)/shard_map/all_to_all | solution.py:244

commit v5 on v4

--- a/solution.py
+++ b/solution.py
@@ -22,38 +22,14 @@
     return [pl.BlockSpec(memory_space=pltpu.VMEM)] * count
 
 
-def block_row(k, st, ids):
-    return st[k, ids[0]] - 4 * ids[0]
-
-
-def block_col(k, st, ids):
-    return lax.rem(st[k, ids[1] // 2], 2)
-
-
 def present(k, st, ids):
     return st[k, ids[1] // 2] // 2 == ids[1]
 
 
-def pick_kernel(st, ids, blocks, out, sem):
-    copies = []
-    for k in range(8):
-        rows = pl.ds(pl.multiple_of(256 * block_row(k, st, ids), 256), 256)
-        lanes = pl.ds(pl.multiple_of(256 * block_col(k, st, ids), 256), 256)
-        copies.append(pltpu.make_async_copy(blocks.at[:, rows, lanes], out.at[:, k], sem.at[k]))
-        copies[-1].start()
-    for copy in copies:
-        copy.wait()
-
-
-def pick_blocks(inverse_anc, structure, ids):
-    return pl.pallas_call(
-        pick_kernel,
-        in_specs=[pl.BlockSpec(memory_space=pltpu.SMEM)] * 2 + [pl.BlockSpec(memory_space=pl.ANY)],
-        out_specs=pl.BlockSpec(memory_space=pl.ANY),
-        out_shape=jax.ShapeDtypeStruct((2, 8, 256, 256), BF),
-        scratch_shapes=[pltpu.SemaphoreType.DMA((8,))],
-        compiler_params=params(),
-    )(structure, ids, inverse_anc)
+def block_at(k, row, st, ids):
+    down = 256 * (st[k, row] - 4 * row)
+    right = 256 * lax.rem(st[k, ids[1] // 2], 2)
+    return down, right
 
 
 def lanes_kernel(panel, out):
@@ -92,16 +68,19 @@
     for k in range(8):
         total = None
         for source, blocks in ((core, own), (1 - core, sib)):
+            down, right = block_at(k, ids[0] - core + source, st, ids)
             left = []
+            right_re, right_im = [], []
+            for panel, half in ((near, zh), (far, 1 - zh)):
+                rows = pl.ds(pl.multiple_of(down + 128 * half, 128), 128)
+                lanes = pl.ds(pl.multiple_of(right, 256), 256)
+                right_re.append(blocks[0, rows, lanes])
+                right_im.append(blocks[1, rows, lanes])
             for p in range(2):
-                parts = []
-                for panel in (near, far):
-                    parts.append(panel[source, :, p, k].astype(F32).reshape(128, 128))
-                lower = jnp.where(zh == 0, parts[0], parts[1])
-                upper = jnp.where(zh == 0, parts[1], parts[0])
-                left.append(jnp.concatenate([lower, upper], axis=0).astype(BF))
-            re = blocks[0, k]
-            im = blocks[1, k]
+                parts = [panel[source, :, p, k].reshape(128, 128) for panel in (near, far)]
+                left.append(jnp.concatenate(parts, axis=0))
+            re = jnp.concatenate(right_re, axis=0)
+            im = jnp.concatenate(right_im, axis=0)
             one = lax.dot_general(
                 left[0], jnp.concatenate([re, im], axis=1), form, preferred_element_type=F32
             )
@@ -177,6 +156,22 @@
     )(ids, summed, below)
 
 
+def copies_kernel(start, part, other, out):
+    value = start[...] - (part[...] + other[...])
+    for chip in range(16):
+        out[chip] = value
+
+
+def diag_copies(start, part, other):
+    return pl.pallas_call(
+        copies_kernel,
+        in_specs=whole(3),
+        out_specs=whole(1)[0],
+        out_shape=jax.ShapeDtypeStruct((16, 16, 256), F32),
+        compiler_params=params(),
+    )(start, part, other)
+
+
 PAIR = [(0, 1), (1, 0)]
 
 
@@ -190,6 +185,7 @@
     ids = [my_row, my_col] + [lax.axis_index(axis) for axis in ("core", "zc", "zh", "zb", "za")]
     ids = jnp.stack(ids).astype(jnp.int32)
     own = lower_panel.reshape(2, 8, 8, 256)
+    sib = lax.ppermute(inverse_anc, "core", PAIR)
     tie = lax.optimization_barrier
 
     group = ("core",) + PLANE
@@ -197,9 +193,7 @@
     lanes = split_lanes(own)
     near = lax.all_to_all(lanes.reshape(32, 2, 8, 8, 128), group, 0, 0, tiled=True)
 
-    mine = pick_blocks(inverse_anc, structure, ids)
-    sib = lax.ppermute(mine, "core", PAIR)
-    other, near, mine = tie((other, near, mine))
+    other, near = tie((other, near))
     lanes = split_lanes(other)
     far = lax.all_to_all(lanes.reshape(32, 2, 8, 8, 128), group, 0, 0, tiled=True)
 
@@ -217,7 +211,7 @@
 
     near = near.reshape(2, 16, 2, 8, 8, 128)
     far = far.reshape(2, 16, 2, 8, 8, 128)
-    parts = products(structure, ids, near, far, mine, sib)
+    parts = products(structure, ids, near, far, inverse_anc, sib)
     below, parts = tie((below, parts))
     below = doubled(below, "zb")
     got = lax.all_to_all(parts.astype(F16), ("zc", "h"), 0, 0, tiled=True).astype(F32)
@@ -236,11 +230,10 @@
     terms = lax.all_to_all(terms, PLANE, 0, 0, tiled=True)
     partner = lax.ppermute(half, "h", PAIR)
     part = jnp.sum(terms, axis=0)
-    part = part + lax.ppermute(part, "zh", PAIR)
-    part, partner = tie((part, partner))
+    other, partner = tie((lax.ppermute(part, "zh", PAIR), partner))
     place = lax.axis_index(PLANE)
     start = lax.dynamic_index_in_dim(diag_inverse.reshape(16, 16, 256), place, 0, keepdims=False)
-    diag = jnp.broadcast_to((start - part)[None], (16, 16, 256))
+    diag = diag_copies(start, part, other)
     diag = lax.all_to_all(diag, PLANE, 0, 0, tiled=True)
     diag_block = diag.reshape(2, 8, 16, 256)
 

time: 174 us -> 172 us (0.989)
  no operation moved by 1% of the time
where the time goes in v5:
time: 172 us; the launch traced here: 171 us
  starting transfers between devices  97.4 us (57%)
  waiting for transfers between devices  54.1 us (31%)
  Pallas kernels  9.77 us (6%)
  other arithmetic  5.2 us (3%)
  local copies, waits for them, and re-layouts  3.25 us (2%)
    all_to_all x2, starting transfers between devices, shards(): lax.all_to_all(lanes.reshape(32, 2, 8, 8, 128), group, 0, 0, tiled=True)  16.9 us
    ppermute x2, starting transfers between devices, shards(): below.append(lax.ppermute(own, ROW + COL, moves))  16.8 us
    ppermute x1, starting transfers between devices, shards(): other = lax.ppermute(own, 'zh', PAIR)  14 us
    ppermute x3, waiting for transfers between devices, doubled(): return jnp.concatenate([value, lax.ppermute(value, axis, PAIR)], axis=0)  13.3 us
    ppermute x3, starting transfers between devices, doubled(): return jnp.concatenate([value, lax.ppermute(value, axis, PAIR)], axis=0)  12.7 us
    all_to_all x1, waiting for transfers between devices, shards(): got = lax.all_to_all(parts, ('za', 'zb'), 0, 0, tiled=True).astype(F32)  11.5 us
    all_to_all x1, starting transfers between devices, shards(): lax.all_to_all(parts.astype(F16), ('zc', 'h'), 0, 0, tiled=True).astype(F32)  9.51 us
    all_to_all x1, starting transfers between devices, shards(): terms = lax.all_to_all(terms, PLANE, 0, 0, tiled=True)  8.99 us
  transfers between devices with their start and end apart: 15, of which 10 were waited for; matrix products, arithmetic and copies ran while one was open for 1% of the time, Pallas kernels for 2%

profile of v5, /device:TPU:2, one launch (start us, length us, event | category | flops | bytes accessed | tf_op | source)
XLA Modules:
  0.0 170.7 jit_solution(6268499748712905288)
XLA Ops:
  0.6 2.1 %collective-permute-start.3 = (bf16[2,1024,512]{2,1,0:T(8,128)(2,1)}, bf16[2,1024,512]{2,1,0:T(8,128)(2,1)}, u32[]{:S(2)}, u32[]{:S(2)}) collective-permute-start(bf16[2,1024,512]{2,1,0:T(8,128)(2,1)} %own.1), channel_id=1, source_target_pairs={{0,32},{32,0},{1,33},{33,1},{2,34},{34,2},{3,35},{35,3},{4,36},{36... | collective-permute-start | bytes 6291464 | tf_op jit(solution)/shard_map/ppermute | solution.py:188
  2.7 0.8 copy-done.2
  3.6 1.3 shard_map.59
  4.9 9.5 %all-to-all-start = ((bf16[32,2,8,8,128]{4,3,2,1,0:T(8,128)(2,1)}), bf16[32,2,8,8,128]{4,3,2,1,0:T(8,128)(2,1)S(1)}, u32[]{:S(2)}, u32[]{:S(2)}) async-start(bf16[32,2,8,8,128]{4,3,2,1,0:T(8,128)(2,1)} %bitcast.8), calls=%async_computation | async-start | bytes 2097152 | tf_op jit(solution)/shard_map/all_to_all | solution.py:194
  14.4 14.0 %collective-permute-start = (bf16[2,8,8,256]{3,2,1,0:T(8,128)(2,1)S(1)}, bf16[2,8,8,256]{3,2,1,0:T(8,128)(2,1)S(1)}, u32[]{:S(2)}, u32[]{:S(2)}) collective-permute-start(bf16[2,8,8,256]{3,2,1,0:T(8,128)(2,1)S(1)} %bitcast.27), channel_id=1, source_target_pairs={{0,16},{16,0},{1,17},{17,1},{2,18},{18,2},{3,19},{19,3},{4,20},{20... | collective-permute-start | bytes 196616 | tf_op jit(solution)/shard_map/ppermute | solution.py:192
  28.3 2.7 %collective-permute-done.panel = bf16[2,8,8,256]{3,2,1,0:T(8,128)(2,1)S(1)} collective-permute-done((bf16[2,8,8,256]{3,2,1,0:T(8,128)(2,1)S(1)}, bf16[2,8,8,256]{3,2,1,0:T(8,128)(2,1)S(1)}, u32[]{:S(2)}, u32[]{:S(2)}) %collective-permute-start) | collective-permute-done | bytes 65568 | tf_op jit(solution)/shard_map/ppermute | solution.py:192
  31.0 1.3 shard_map.60
  32.3 7.4 %all-to-all-start.1 = ((bf16[32,2,8,8,128]{4,3,2,1,0:T(8,128)(2,1)}), bf16[32,2,8,8,128]{4,3,2,1,0:T(8,128)(2,1)S(1)}, u32[]{:S(2)}, u32[]{:S(2)}) async-start(bf16[32,2,8,8,128]{4,3,2,1,0:T(8,128)(2,1)} %bitcast.9), calls=%async_computation.1 | async-start | bytes 2097152 | tf_op jit(solution)/shard_map/all_to_all | solution.py:198
  39.7 2.0 %collective-permute-start.1 = (bf16[2,8,8,256]{3,2,1,0:T(8,128)(2,1)S(1)}, bf16[2,8,8,256]{3,2,1,0:T(8,128)(2,1)S(1)}, u32[]{:S(2)}, u32[]{:S(2)}) collective-permute-start(bf16[2,8,8,256]{3,2,1,0:T(8,128)(2,1)S(1)} %bitcast.28), channel_id=1, source_target_pairs={{0,0},{1,32},{2,64},{3,96},{4,128},{5,160},{6,192},{7,224},{8,256}... | collective-permute-start | bytes 196616 | tf_op jit(solution)/shard_map/ppermute | solution.py:208
  41.8 14.7 %collective-permute-start.2 = (bf16[2,8,8,256]{3,2,1,0:T(8,128)(2,1)S(1)}, bf16[2,8,8,256]{3,2,1,0:T(8,128)(2,1)S(1)}, u32[]{:S(2)}, u32[]{:S(2)}) collective-permute-start(bf16[2,8,8,256]{3,2,1,0:T(8,128)(2,1)S(1)} %bitcast.29), channel_id=1, source_target_pairs={{0,256},{1,288},{2,320},{3,352},{4,384},{5,416},{6,448},{7,480},{8... | collective-permute-start | bytes 196616 | tf_op jit(solution)/shard_map/ppermute | solution.py:208
  56.6 4.4 %collective-permute-done.2 = bf16[2,8,8,256]{3,2,1,0:T(8,128)(2,1)S(1)} collective-permute-done((bf16[2,8,8,256]{3,2,1,0:T(8,128)(2,1)S(1)}, bf16[2,8,8,256]{3,2,1,0:T(8,128)(2,1)S(1)}, u32[]{:S(2)}, u32[]{:S(2)}) %collective-permute-start.2) | collective-permute-done | bytes 65568 | tf_op jit(solution)/shard_map/ppermute | solution.py:208
  61.0 1.6 copy-done.1
  62.6 4.5 %shard_map.61 = f32[4,1040,128]{2,1,0:T(8,128)} custom-call(s32[8,16]{1,0:T(8,128)S(1)} %copy-done.4, s32[7]{0:T(128)S(1)} %stack.40.ids, bf16[2,16,2,8,8,128]{5,4,3,2,1,0:T(8,128)(2,1)S(1)} %bitcast.23, bf16[2,16,2,8,8,128]{5,4,3,2,1,0:T(8,128)(2,1)S(1)} %bitcast.24, bf16[2,1024,512]{2,1,0:T(8,128)(2,1)S(1)} %copy-done.1, ...), custom_call_target="tpu_custom_call" | custom-call | tf_op jit(solution)/shard_map/pallas_call | solution.py:113
  67.1 2.7 %convert_element_type.10 = f16[4,1040,128]{2,1,0:T(8,128)(2,1)} convert(f32[4,1040,128]{2,1,0:T(8,128)} %shard_map.61) | non-fusion elementwise | flops 532480 | bytes 3194880 | tf_op jit(solution)/shard_map/convert_element_type | solution.py:217
  69.8 9.5 %all-to-all-start.2 = ((f16[4,1040,128]{2,1,0:T(8,128)(2,1)}), f16[4,1040,128]{2,1,0:T(8,128)(2,1)S(1)}, u32[]{:S(2)}, u32[]{:S(2)}) async-start(f16[4,1040,128]{2,1,0:T(8,128)(2,1)} %convert_element_type.10), calls=%async_computation.2 | async-start | bytes 2129920 | tf_op jit(solution)/shard_map/all_to_all | solution.py:217
  79.4 6.1 %collective-permute-start.4 = (bf16[2,2,8,8,256]{4,3,2,1,0:T(8,128)(2,1)S(1)}, bf16[2,2,8,8,256]{4,3,2,1,0:T(8,128)(2,1)S(1)}, u32[]{:S(2)}, u32[]{:S(2)}) collective-permute-start(bf16[2,2,8,8,256]{4,3,2,1,0:T(8,128)(2,1)S(1)} %pad_maximum_fusion.5), channel_id=1, source_target_pairs={{0,128},{128,0},{1,129},{129,1},{2,130},{130,2},{3,131},{131,3},{4... | collective-permute-start | bytes 393224 | tf_op jit(solution)/shard_map/ppermute | solution.py:179
  85.4 9.4 %collective-permute-done.4 = bf16[2,2,8,8,256]{4,3,2,1,0:T(8,128)(2,1)S(1)} collective-permute-done((bf16[2,2,8,8,256]{4,3,2,1,0:T(8,128)(2,1)S(1)}, bf16[2,2,8,8,256]{4,3,2,1,0:T(8,128)(2,1)S(1)}, u32[]{:S(2)}, u32[]{:S(2)}) %collective-permute-start.4) | collective-permute-done | bytes 131104 | tf_op jit(solution)/shard_map/ppermute | solution.py:179
  94.8 1.9 %all-to-all-done.2 = f16[4,1040,128]{2,1,0:T(8,128)(2,1)S(1)} async-done(((f16[4,1040,128]{2,1,0:T(8,128)(2,1)}), f16[4,1040,128]{2,1,0:T(8,128)(2,1)S(1)}, u32[]{:S(2)}, u32[]{:S(2)}) %all-to-all-start.2) | async-done | bytes 1064992 | tf_op jit(solution)/shard_map/all_to_all | solution.py:217
  98.0 4.7 %collective-permute-start.5 = (bf16[4,2,8,8,256]{4,3,2,1,0:T(8,128)(2,1)S(1)}, bf16[4,2,8,8,256]{4,3,2,1,0:T(8,128)(2,1)S(1)}, u32[]{:S(2)}, u32[]{:S(2)}) collective-permute-start(bf16[4,2,8,8,256]{4,3,2,1,0:T(8,128)(2,1)S(1)} %pad_maximum_fusion.3), channel_id=1, source_target_pairs={{0,64},{64,0},{1,65},{65,1},{2,66},{66,2},{3,67},{67,3},{4,68},{68... | collective-permute-start | bytes 786440 | tf_op jit(solution)/shard_map/ppermute | solution.py:179
  102.7 3.5 %all-to-all-start.3 = ((f16[4,272,128]{2,1,0:T(8,128)(2,1)}), f16[4,272,128]{2,1,0:T(8,128)(2,1)S(1)}, u32[]{:S(2)}, u32[]{:S(2)}) async-start(f16[4,272,128]{2,1,0:T(8,128)(2,1)} %pad_maximum_fusion.2), calls=%async_computation.3 | async-start | bytes 557056 | tf_op jit(solution)/shard_map/all_to_all | solution.py:226
  106.2 2.0 %collective-permute-done.5 = bf16[4,2,8,8,256]{4,3,2,1,0:T(8,128)(2,1)S(1)} collective-permute-done((bf16[4,2,8,8,256]{4,3,2,1,0:T(8,128)(2,1)S(1)}, bf16[4,2,8,8,256]{4,3,2,1,0:T(8,128)(2,1)S(1)}, u32[]{:S(2)}, u32[]{:S(2)}) %collective-permute-start.5) | collective-permute-done | bytes 262176 | tf_op jit(solution)/shard_map/ppermute | solution.py:179
  108.2 1.9 %collective-permute-start.6 = (bf16[8,2,8,8,256]{4,3,2,1,0:T(8,128)(2,1)S(1)}, bf16[8,2,8,8,256]{4,3,2,1,0:T(8,128)(2,1)S(1)}, u32[]{:S(2)}, u32[]{:S(2)}) collective-permute-start(bf16[8,2,8,8,256]{4,3,2,1,0:T(8,128)(2,1)S(1)} %pad_maximum_fusion.1), channel_id=1, source_target_pairs={{0,32},{32,0},{1,33},{33,1},{2,34},{34,2},{3,35},{35,3},{4,36},{36... | collective-permute-start | bytes 1572872 | tf_op jit(solution)/shard_map/ppermute | solution.py:179
  110.2 1.9 %collective-permute-done.6 = bf16[8,2,8,8,256]{4,3,2,1,0:T(8,128)(2,1)S(1)} collective-permute-done((bf16[8,2,8,8,256]{4,3,2,1,0:T(8,128)(2,1)S(1)}, bf16[8,2,8,8,256]{4,3,2,1,0:T(8,128)(2,1)S(1)}, u32[]{:S(2)}, u32[]{:S(2)}) %collective-permute-start.6) | collective-permute-done | bytes 524320 | tf_op jit(solution)/shard_map/ppermute | solution.py:179
  112.1 11.5 %all-to-all-done.3 = f16[4,272,128]{2,1,0:T(8,128)(2,1)S(1)} async-done(((f16[4,272,128]{2,1,0:T(8,128)(2,1)}), f16[4,272,128]{2,1,0:T(8,128)(2,1)S(1)}, u32[]{:S(2)}, u32[]{:S(2)}) %all-to-all-start.3) | async-done | bytes 278560 | tf_op jit(solution)/shard_map/all_to_all | solution.py:226
  123.8 1.9 %shard_map.62 = (bf16[2,8,16,128]{3,2,1,0:T(8,128)(2,1)S(1)}, f32[16,16,256]{2,1,0:T(8,128)}) custom-call(s32[7]{0:T(128)S(1)} %stack.40.ids, f32[2,8,16,128]{3,2,1,0:T(8,128)S(1)} %bitcast.25, bf16[16,2,8,8,256]{4,3,2,1,0:T(8,128)(2,1)S(1)} %pad_maximum_fusion.below), custom_call_target="tpu_custom_call" | custom-call | tf_op jit(solution)/shard_map/pallas_call | solution.py:147
  125.7 9.0 %all-to-all-start.4 = ((f32[16,16,256]{2,1,0:T(8,128)}), f32[16,16,256]{2,1,0:T(8,128)S(1)}, u32[]{:S(2)}, u32[]{:S(2)}) async-start(f32[16,16,256]{2,1,0:T(8,128)} %get-tuple-element.25), calls=%async_computation.4 | async-start | bytes 524288 | tf_op jit(solution)/shard_map/all_to_all | solution.py:230
  134.7 2.0 %collective-permute-start.8 = (bf16[2,8,16,128]{3,2,1,0:T(8,128)(2,1)S(1)}, bf16[2,8,16,128]{3,2,1,0:T(8,128)(2,1)S(1)}, u32[]{:S(2)}, u32[]{:S(2)}) collective-permute-start(bf16[2,8,16,128]{3,2,1,0:T(8,128)(2,1)S(1)} %get-tuple-element.24), channel_id=1, source_target_pairs={{0,1},{1,0},{2,3},{3,2},{4,5},{5,4},{6,7},{7,6},{8,9},{9,8},{10,11... | collective-permute-start | bytes 196616 | tf_op jit(solution)/shard_map/ppermute | solution.py:231
  136.7 6.0 %all-to-all-done.4 = f32[16,16,256]{2,1,0:T(8,128)S(1)} async-done(((f32[16,16,256]{2,1,0:T(8,128)}), f32[16,16,256]{2,1,0:T(8,128)S(1)}, u32[]{:S(2)}, u32[]{:S(2)}) %all-to-all-start.4) | async-done | bytes 262176 | tf_op jit(solution)/shard_map/all_to_all | solution.py:230
  142.7 6.3 %collective-permute-start.7 = (f32[16,256]{1,0:T(8,128)S(1)}, f32[16,256]{1,0:T(8,128)S(1)}, u32[]{:S(2)}, u32[]{:S(2)}) collective-permute-start(f32[16,256]{1,0:T(8,128)S(1)} %reduce_sum.29.part), channel_id=1, source_target_pairs={{0,16},{16,0},{1,17},{17,1},{2,18},{18,2},{3,19},{19,3},{4,20},{20... | collective-permute-start | bytes 49160 | tf_op jit(solution)/shard_map/ppermute | solution.py:233
  149.3 7.8 %collective-permute-done.7.other = f32[16,256]{1,0:T(8,128)S(1)} collective-permute-done((f32[16,256]{1,0:T(8,128)S(1)}, f32[16,256]{1,0:T(8,128)S(1)}, u32[]{:S(2)}, u32[]{:S(2)}) %collective-permute-start.7) | collective-permute-done | bytes 16416 | tf_op jit(solution)/shard_map/ppermute | solution.py:233
  157.8 4.8 %all-to-all-start.5 = ((f32[16,16,256]{2,1,0:T(8,128)}), f32[16,16,256]{2,1,0:T(8,128)S(1)}, u32[]{:S(2)}, u32[]{:S(2)}) async-start(f32[16,16,256]{2,1,0:T(8,128)} %shard_map.63), calls=%async_computation.5 | async-start | bytes 524288 | tf_op jit(solution)/shard_map/all_to_all | solution.py:237
  163.4 6.6 %all-to-all-done.5 = f32[16,16,256]{2,1,0:T(8,128)S(1)} async-done(((f32[16,16,256]{2,1,0:T(8,128)}), f32[16,16,256]{2,1,0:T(8,128)S(1)}, u32[]{:S(2)}, u32[]{:S(2)}) %all-to-all-start.5) | async-done | bytes 262176 | tf_op jit(solution)/shard_map/all_to_all | solution.py:237
  (37 shorter events, 4.1 us)
Async XLA Ops:
  0.6 148.4 %copy-start = (f32[2,8,16,256]{3,2,1,0:T(8,128)S(1)}, f32[2,8,16,256]{3,2,1,0:T(8,128)}, u32[]{:S(2)}) copy-start(f32[2,8,16,256]{3,2,1,0:T(8,128)} %param.6) | copy-start | bytes 786436
  0.6 60.4 %collective-permute-start.3 = (bf16[2,1024,512]{2,1,0:T(8,128)(2,1)}, bf16[2,1024,512]{2,1,0:T(8,128)(2,1)}, u32[]{:S(2)}, u32[]{:S(2)}) collective-permute-start(bf16[2,1024,512]{2,1,0:T(8,128)(2,1)} %own.1), channel_id=1, source_target_pairs={{0,32},{32,0},{1,33},{33,1},{2,34},{34,2},{3,35},{35,3},{4,36},{36... | collective-permute-start | bytes 6291464 | tf_op jit(solution)/shard_map/ppermute | solution.py:188
  2.7 0.8 copy-start.2
  3.5 10.8 %copy-start.3 = (bf16[2,8,1,8,256]{4,3,2,1,0:T(8,128)(2,1)S(1)}, bf16[2,8,1,8,256]{4,3,2,1,0:T(8,128)(2,1)}, u32[]{:S(2)}) copy-start(bf16[2,8,1,8,256]{4,3,2,1,0:T(8,128)(2,1)} %param.5) | copy-start | bytes 196612
  4.9 26.2 %all-to-all-start = ((bf16[32,2,8,8,128]{4,3,2,1,0:T(8,128)(2,1)}), bf16[32,2,8,8,128]{4,3,2,1,0:T(8,128)(2,1)S(1)}, u32[]{:S(2)}, u32[]{:S(2)}) async-start(bf16[32,2,8,8,128]{4,3,2,1,0:T(8,128)(2,1)} %bitcast.8), calls=%async_computation | async-start | bytes 2097152 | tf_op jit(solution)/shard_map/all_to_all | solution.py:194
  14.4 46.7 %copy-start.4 = (s32[8,16]{1,0:T(8,128)S(1)}, s32[8,16]{1,0:T(8,128)}, u32[]{:S(2)}) copy-start(s32[8,16]{1,0:T(8,128)} %st.1) | copy-start | bytes 1540
  14.4 16.7 %collective-permute-start = (bf16[2,8,8,256]{3,2,1,0:T(8,128)(2,1)S(1)}, bf16[2,8,8,256]{3,2,1,0:T(8,128)(2,1)S(1)}, u32[]{:S(2)}, u32[]{:S(2)}) collective-permute-start(bf16[2,8,8,256]{3,2,1,0:T(8,128)(2,1)S(1)} %bitcast.27), channel_id=1, source_target_pairs={{0,16},{16,0},{1,17},{17,1},{2,18},{18,2},{3,19},{19,3},{4,20},{20... | collective-permute-start | bytes 196616 | tf_op jit(solution)/shard_map/ppermute | solution.py:192
  32.3 28.7 %all-to-all-start.1 = ((bf16[32,2,8,8,128]{4,3,2,1,0:T(8,128)(2,1)}), bf16[32,2,8,8,128]{4,3,2,1,0:T(8,128)(2,1)S(1)}, u32[]{:S(2)}, u32[]{:S(2)}) async-start(bf16[32,2,8,8,128]{4,3,2,1,0:T(8,128)(2,1)} %bitcast.9), calls=%async_computation.1 | async-start | bytes 2097152 | tf_op jit(solution)/shard_map/all_to_all | solution.py:198
  39.7 16.9 %collective-permute-start.1 = (bf16[2,8,8,256]{3,2,1,0:T(8,128)(2,1)S(1)}, bf16[2,8,8,256]{3,2,1,0:T(8,128)(2,1)S(1)}, u32[]{:S(2)}, u32[]{:S(2)}) collective-permute-start(bf16[2,8,8,256]{3,2,1,0:T(8,128)(2,1)S(1)} %bitcast.28), channel_id=1, source_target_pairs={{0,0},{1,32},{2,64},{3,96},{4,128},{5,160},{6,192},{7,224},{8,256}... | collective-permute-start | bytes 196616 | tf_op jit(solution)/shard_map/ppermute | solution.py:208
  41.8 19.2 %collective-permute-start.2 = (bf16[2,8,8,256]{3,2,1,0:T(8,128)(2,1)S(1)}, bf16[2,8,8,256]{3,2,1,0:T(8,128)(2,1)S(1)}, u32[]{:S(2)}, u32[]{:S(2)}) collective-permute-start(bf16[2,8,8,256]{3,2,1,0:T(8,128)(2,1)S(1)} %bitcast.29), channel_id=1, source_target_pairs={{0,256},{1,288},{2,320},{3,352},{4,384},{5,416},{6,448},{7,480},{8... | collective-permute-start | bytes 196616 | tf_op jit(solution)/shard_map/ppermute | solution.py:208
  61.0 1.6 copy-start.1
  69.8 26.9 %all-to-all-start.2 = ((f16[4,1040,128]{2,1,0:T(8,128)(2,1)}), f16[4,1040,128]{2,1,0:T(8,128)(2,1)S(1)}, u32[]{:S(2)}, u32[]{:S(2)}) async-start(f16[4,1040,128]{2,1,0:T(8,128)(2,1)} %convert_element_type.10), calls=%async_computation.2 | async-start | bytes 2129920 | tf_op jit(solution)/shard_map/all_to_all | solution.py:217
  79.4 15.4 %collective-permute-start.4 = (bf16[2,2,8,8,256]{4,3,2,1,0:T(8,128)(2,1)S(1)}, bf16[2,2,8,8,256]{4,3,2,1,0:T(8,128)(2,1)S(1)}, u32[]{:S(2)}, u32[]{:S(2)}) collective-permute-start(bf16[2,2,8,8,256]{4,3,2,1,0:T(8,128)(2,1)S(1)} %pad_maximum_fusion.5), channel_id=1, source_target_pairs={{0,128},{128,0},{1,129},{129,1},{2,130},{130,2},{3,131},{131,3},{4... | collective-permute-start | bytes 393224 | tf_op jit(solution)/shard_map/ppermute | solution.py:179
  98.0 10.2 %collective-permute-start.5 = (bf16[4,2,8,8,256]{4,3,2,1,0:T(8,128)(2,1)S(1)}, bf16[4,2,8,8,256]{4,3,2,1,0:T(8,128)(2,1)S(1)}, u32[]{:S(2)}, u32[]{:S(2)}) collective-permute-start(bf16[4,2,8,8,256]{4,3,2,1,0:T(8,128)(2,1)S(1)} %pad_maximum_fusion.3), channel_id=1, source_target_pairs={{0,64},{64,0},{1,65},{65,1},{2,66},{66,2},{3,67},{67,3},{4,68},{68... | collective-permute-start | bytes 786440 | tf_op jit(solution)/shard_map/ppermute | solution.py:179
  102.7 21.0 %all-to-all-start.3 = ((f16[4,272,128]{2,1,0:T(8,128)(2,1)}), f16[4,272,128]{2,1,0:T(8,128)(2,1)S(1)}, u32[]{:S(2)}, u32[]{:S(2)}) async-start(f16[4,272,128]{2,1,0:T(8,128)(2,1)} %pad_maximum_fusion.2), calls=%async_computation.3 | async-start | bytes 557056 | tf_op jit(solution)/shard_map/all_to_all | solution.py:226
  108.2 3.8 %collective-permute-start.6 = (bf16[8,2,8,8,256]{4,3,2,1,0:T(8,128)(2,1)S(1)}, bf16[8,2,8,8,256]{4,3,2,1,0:T(8,128)(2,1)S(1)}, u32[]{:S(2)}, u32[]{:S(2)}) collective-permute-start(bf16[8,2,8,8,256]{4,3,2,1,0:T(8,128)(2,1)S(1)} %pad_maximum_fusion.1), channel_id=1, source_target_pairs={{0,32},{32,0},{1,33},{33,1},{2,34},{34,2},{3,35},{35,3},{4,36},{36... | collective-permute-start | bytes 1572872 | tf_op jit(solution)/shard_map/ppermute | solution.py:179
  125.7 17.0 %all-to-all-start.4 = ((f32[16,16,256]{2,1,0:T(8,128)}), f32[16,16,256]{2,1,0:T(8,128)S(1)}, u32[]{:S(2)}, u32[]{:S(2)}) async-start(f32[16,16,256]{2,1,0:T(8,128)} %get-tuple-element.25), calls=%async_computation.4 | async-start | bytes 524288 | tf_op jit(solution)/shard_map/all_to_all | solution.py:230
  134.7 14.6 %collective-permute-start.8 = (bf16[2,8,16,128]{3,2,1,0:T(8,128)(2,1)S(1)}, bf16[2,8,16,128]{3,2,1,0:T(8,128)(2,1)S(1)}, u32[]{:S(2)}, u32[]{:S(2)}) collective-permute-start(bf16[2,8,16,128]{3,2,1,0:T(8,128)(2,1)S(1)} %get-tuple-element.24), channel_id=1, source_target_pairs={{0,1},{1,0},{2,3},{3,2},{4,5},{5,4},{6,7},{7,6},{8,9},{9,8},{10,11... | collective-permute-start | bytes 196616 | tf_op jit(solution)/shard_map/ppermute | solution.py:231
  142.7 14.3 %collective-permute-start.7 = (f32[16,256]{1,0:T(8,128)S(1)}, f32[16,256]{1,0:T(8,128)S(1)}, u32[]{:S(2)}, u32[]{:S(2)}) collective-permute-start(f32[16,256]{1,0:T(8,128)S(1)} %reduce_sum.29.part), channel_id=1, source_target_pairs={{0,16},{16,0},{1,17},{17,1},{2,18},{18,2},{3,19},{19,3},{4,20},{20... | collective-permute-start | bytes 49160 | tf_op jit(solution)/shard_map/ppermute | solution.py:233
  157.8 12.2 %all-to-all-start.5 = ((f32[16,16,256]{2,1,0:T(8,128)}), f32[16,16,256]{2,1,0:T(8,128)S(1)}, u32[]{:S(2)}, u32[]{:S(2)}) async-start(f32[16,16,256]{2,1,0:T(8,128)} %shard_map.63), calls=%async_computation.5 | async-start | bytes 524288 | tf_op jit(solution)/shard_map/all_to_all | solution.py:237

commit v6 on v5

--- a/solution.py
+++ b/solution.py
@@ -185,7 +185,6 @@
     ids = [my_row, my_col] + [lax.axis_index(axis) for axis in ("core", "zc", "zh", "zb", "za")]
     ids = jnp.stack(ids).astype(jnp.int32)
     own = lower_panel.reshape(2, 8, 8, 256)
-    sib = lax.ppermute(inverse_anc, "core", PAIR)
     tie = lax.optimization_barrier
 
     group = ("core",) + PLANE
@@ -193,7 +192,8 @@
     lanes = split_lanes(own)
     near = lax.all_to_all(lanes.reshape(32, 2, 8, 8, 128), group, 0, 0, tiled=True)
 
-    other, near = tie((other, near))
+    other, near, shard = tie((other, near, inverse_anc))
+    sib = lax.ppermute(shard, "core", PAIR)
     lanes = split_lanes(other)
     far = lax.all_to_all(lanes.reshape(32, 2, 8, 8, 128), group, 0, 0, tiled=True)
 

time: 172 us -> 171 us (level)
  transfers between devices with their start and end apart: 15 -> 15, of which waited for: 10 -> 10; matrix products, arithmetic and copies ran while one was open for 1% -> 1% of each run, Pallas kernels for 2% -> 1%
where the time goes in v6:
time: 171 us; the launch traced here: 170 us
  starting transfers between devices  97.3 us (57%)
  waiting for transfers between devices  54.1 us (32%)
  Pallas kernels  10.4 us (6%)
  other arithmetic  5.19 us (3%)
    all_to_all x2, starting transfers between devices, shards(): lax.all_to_all(lanes.reshape(32, 2, 8, 8, 128), group, 0, 0, tiled=True)  17 us
    ppermute x2, starting transfers between devices, shards(): below.append(lax.ppermute(own, ROW + COL, moves))  16.8 us
    ppermute x1, starting transfers between devices, shards(): other = lax.ppermute(own, 'zh', PAIR)  13.9 us
    ppermute x3, waiting for transfers between devices, doubled(): return jnp.concatenate([value, lax.ppermute(value, axis, PAIR)], axis=0)  13.3 us
    ppermute x3, starting transfers between devices, doubled(): return jnp.concatenate([value, lax.ppermute(value, axis, PAIR)], axis=0)  12.7 us
    all_to_all x1, waiting for transfers between devices, shards(): got = lax.all_to_all(parts, ('za', 'zb'), 0, 0, tiled=True).astype(F32)  11.5 us
    all_to_all x1, starting transfers between devices, shards(): lax.all_to_all(parts.astype(F16), ('zc', 'h'), 0, 0, tiled=True).astype(F32)  9.51 us
    all_to_all x1, starting transfers between devices, shards(): terms = lax.all_to_all(terms, PLANE, 0, 0, tiled=True)  9.01 us
  transfers between devices with their start and end apart: 15, of which 10 were waited for; matrix products, arithmetic and copies ran while one was open for 1% of the time, Pallas kernels for 1%

profile of v6, /device:TPU:2, one launch (start us, length us, event | category | flops | bytes accessed | tf_op | source)
XLA Modules:
  0.0 169.7 jit_solution(16916088501256741033)
XLA Ops:
  0.7 0.9 copy-done.1
  1.5 1.3 shard_map.59
  2.8 9.5 %all-to-all-start = ((bf16[32,2,8,8,128]{4,3,2,1,0:T(8,128)(2,1)}), bf16[32,2,8,8,128]{4,3,2,1,0:T(8,128)(2,1)S(1)}, u32[]{:S(2)}, u32[]{:S(2)}) async-start(bf16[32,2,8,8,128]{4,3,2,1,0:T(8,128)(2,1)} %bitcast.8), calls=%async_computation | async-start | bytes 2097152 | tf_op jit(solution)/shard_map/all_to_all | solution.py:193
  12.4 13.9 %collective-permute-start = (bf16[2,8,8,256]{3,2,1,0:T(8,128)(2,1)S(1)}, bf16[2,8,8,256]{3,2,1,0:T(8,128)(2,1)S(1)}, u32[]{:S(2)}, u32[]{:S(2)}) collective-permute-start(bf16[2,8,8,256]{3,2,1,0:T(8,128)(2,1)S(1)} %bitcast.27), channel_id=1, source_target_pairs={{0,16},{16,0},{1,17},{17,1},{2,18},{18,2},{3,19},{19,3},{4,20},{20... | collective-permute-start | bytes 196616 | tf_op jit(solution)/shard_map/ppermute | solution.py:191
  26.2 2.7 %collective-permute-done.panel = bf16[2,8,8,256]{3,2,1,0:T(8,128)(2,1)S(1)} collective-permute-done((bf16[2,8,8,256]{3,2,1,0:T(8,128)(2,1)S(1)}, bf16[2,8,8,256]{3,2,1,0:T(8,128)(2,1)S(1)}, u32[]{:S(2)}, u32[]{:S(2)}) %collective-permute-start) | collective-permute-done | bytes 65568 | tf_op jit(solution)/shard_map/ppermute | solution.py:191
  28.9 1.9 %collective-permute-start.3 = (bf16[2,1024,512]{2,1,0:T(8,128)(2,1)}, bf16[2,1024,512]{2,1,0:T(8,128)(2,1)}, u32[]{:S(2)}, u32[]{:S(2)}) collective-permute-start(bf16[2,1024,512]{2,1,0:T(8,128)(2,1)} %own.1), channel_id=1, source_target_pairs={{0,32},{32,0},{1,33},{33,1},{2,34},{34,2},{3,35},{35,3},{4,36},{36... | collective-permute-start | bytes 6291464 | tf_op jit(solution)/shard_map/ppermute | solution.py:196
  30.8 1.3 shard_map.60
  32.1 7.5 %all-to-all-start.1 = ((bf16[32,2,8,8,128]{4,3,2,1,0:T(8,128)(2,1)}), bf16[32,2,8,8,128]{4,3,2,1,0:T(8,128)(2,1)S(1)}, u32[]{:S(2)}, u32[]{:S(2)}) async-start(bf16[32,2,8,8,128]{4,3,2,1,0:T(8,128)(2,1)} %bitcast.9), calls=%async_computation.1 | async-start | bytes 2097152 | tf_op jit(solution)/shard_map/all_to_all | solution.py:198
  39.6 2.0 %collective-permute-start.1 = (bf16[2,8,8,256]{3,2,1,0:T(8,128)(2,1)S(1)}, bf16[2,8,8,256]{3,2,1,0:T(8,128)(2,1)S(1)}, u32[]{:S(2)}, u32[]{:S(2)}) collective-permute-start(bf16[2,8,8,256]{3,2,1,0:T(8,128)(2,1)S(1)} %bitcast.28), channel_id=1, source_target_pairs={{0,0},{1,32},{2,64},{3,96},{4,128},{5,160},{6,192},{7,224},{8,256}... | collective-permute-start | bytes 196616 | tf_op jit(solution)/shard_map/ppermute | solution.py:208
  41.7 14.7 %collective-permute-start.2 = (bf16[2,8,8,256]{3,2,1,0:T(8,128)(2,1)S(1)}, bf16[2,8,8,256]{3,2,1,0:T(8,128)(2,1)S(1)}, u32[]{:S(2)}, u32[]{:S(2)}) collective-permute-start(bf16[2,8,8,256]{3,2,1,0:T(8,128)(2,1)S(1)} %bitcast.29), channel_id=1, source_target_pairs={{0,256},{1,288},{2,320},{3,352},{4,384},{5,416},{6,448},{7,480},{8... | collective-permute-start | bytes 196616 | tf_op jit(solution)/shard_map/ppermute | solution.py:208
  56.5 4.4 %collective-permute-done.2 = bf16[2,8,8,256]{3,2,1,0:T(8,128)(2,1)S(1)} collective-permute-done((bf16[2,8,8,256]{3,2,1,0:T(8,128)(2,1)S(1)}, bf16[2,8,8,256]{3,2,1,0:T(8,128)(2,1)S(1)}, u32[]{:S(2)}, u32[]{:S(2)}) %collective-permute-start.2) | collective-permute-done | bytes 65568 | tf_op jit(solution)/shard_map/ppermute | solution.py:208
  60.9 5.1 %shard_map.61 = f32[4,1040,128]{2,1,0:T(8,128)} custom-call(s32[8,16]{1,0:T(8,128)S(1)} %copy-done.3, s32[7]{0:T(128)S(1)} %stack.40.ids, bf16[2,16,2,8,8,128]{5,4,3,2,1,0:T(8,128)(2,1)S(1)} %bitcast.23, bf16[2,16,2,8,8,128]{5,4,3,2,1,0:T(8,128)(2,1)S(1)} %bitcast.24, bf16[2,1024,512]{2,1,0:T(8,128)(2,1)} %own.1, ...), custom_call_target="tpu_custom_call" | custom-call | tf_op jit(solution)/shard_map/pallas_call | solution.py:113
  66.1 2.7 %convert_element_type.10 = f16[4,1040,128]{2,1,0:T(8,128)(2,1)} convert(f32[4,1040,128]{2,1,0:T(8,128)} %shard_map.61) | non-fusion elementwise | flops 532480 | bytes 3194880 | tf_op jit(solution)/shard_map/convert_element_type | solution.py:217
  68.8 9.5 %all-to-all-start.2 = ((f16[4,1040,128]{2,1,0:T(8,128)(2,1)}), f16[4,1040,128]{2,1,0:T(8,128)(2,1)S(1)}, u32[]{:S(2)}, u32[]{:S(2)}) async-start(f16[4,1040,128]{2,1,0:T(8,128)(2,1)} %convert_element_type.10), calls=%async_computation.2 | async-start | bytes 2129920 | tf_op jit(solution)/shard_map/all_to_all | solution.py:217
  78.3 6.1 %collective-permute-start.4 = (bf16[2,2,8,8,256]{4,3,2,1,0:T(8,128)(2,1)S(1)}, bf16[2,2,8,8,256]{4,3,2,1,0:T(8,128)(2,1)S(1)}, u32[]{:S(2)}, u32[]{:S(2)}) collective-permute-start(bf16[2,2,8,8,256]{4,3,2,1,0:T(8,128)(2,1)S(1)} %pad_maximum_fusion.5), channel_id=1, source_target_pairs={{0,128},{128,0},{1,129},{129,1},{2,130},{130,2},{3,131},{131,3},{4... | collective-permute-start | bytes 393224 | tf_op jit(solution)/shard_map/ppermute | solution.py:179
  84.4 9.4 %collective-permute-done.4 = bf16[2,2,8,8,256]{4,3,2,1,0:T(8,128)(2,1)S(1)} collective-permute-done((bf16[2,2,8,8,256]{4,3,2,1,0:T(8,128)(2,1)S(1)}, bf16[2,2,8,8,256]{4,3,2,1,0:T(8,128)(2,1)S(1)}, u32[]{:S(2)}, u32[]{:S(2)}) %collective-permute-start.4) | collective-permute-done | bytes 131104 | tf_op jit(solution)/shard_map/ppermute | solution.py:179
  93.8 1.9 %all-to-all-done.2 = f16[4,1040,128]{2,1,0:T(8,128)(2,1)S(1)} async-done(((f16[4,1040,128]{2,1,0:T(8,128)(2,1)}), f16[4,1040,128]{2,1,0:T(8,128)(2,1)S(1)}, u32[]{:S(2)}, u32[]{:S(2)}) %all-to-all-start.2) | async-done | bytes 1064992 | tf_op jit(solution)/shard_map/all_to_all | solution.py:217
  96.1 0.8 pad_maximum_fusion.2
  96.9 4.7 %collective-permute-start.5 = (bf16[4,2,8,8,256]{4,3,2,1,0:T(8,128)(2,1)S(1)}, bf16[4,2,8,8,256]{4,3,2,1,0:T(8,128)(2,1)S(1)}, u32[]{:S(2)}, u32[]{:S(2)}) collective-permute-start(bf16[4,2,8,8,256]{4,3,2,1,0:T(8,128)(2,1)S(1)} %pad_maximum_fusion.3), channel_id=1, source_target_pairs={{0,64},{64,0},{1,65},{65,1},{2,66},{66,2},{3,67},{67,3},{4,68},{68... | collective-permute-start | bytes 786440 | tf_op jit(solution)/shard_map/ppermute | solution.py:179
  101.7 3.5 %all-to-all-start.3 = ((f16[4,272,128]{2,1,0:T(8,128)(2,1)}), f16[4,272,128]{2,1,0:T(8,128)(2,1)S(1)}, u32[]{:S(2)}, u32[]{:S(2)}) async-start(f16[4,272,128]{2,1,0:T(8,128)(2,1)} %pad_maximum_fusion.2), calls=%async_computation.3 | async-start | bytes 557056 | tf_op jit(solution)/shard_map/all_to_all | solution.py:226
  105.1 2.0 %collective-permute-done.5 = bf16[4,2,8,8,256]{4,3,2,1,0:T(8,128)(2,1)S(1)} collective-permute-done((bf16[4,2,8,8,256]{4,3,2,1,0:T(8,128)(2,1)S(1)}, bf16[4,2,8,8,256]{4,3,2,1,0:T(8,128)(2,1)S(1)}, u32[]{:S(2)}, u32[]{:S(2)}) %collective-permute-start.5) | collective-permute-done | bytes 262176 | tf_op jit(solution)/shard_map/ppermute | solution.py:179
  107.2 1.9 %collective-permute-start.6 = (bf16[8,2,8,8,256]{4,3,2,1,0:T(8,128)(2,1)S(1)}, bf16[8,2,8,8,256]{4,3,2,1,0:T(8,128)(2,1)S(1)}, u32[]{:S(2)}, u32[]{:S(2)}) collective-permute-start(bf16[8,2,8,8,256]{4,3,2,1,0:T(8,128)(2,1)S(1)} %pad_maximum_fusion.1), channel_id=1, source_target_pairs={{0,32},{32,0},{1,33},{33,1},{2,34},{34,2},{3,35},{35,3},{4,36},{36... | collective-permute-start | bytes 1572872 | tf_op jit(solution)/shard_map/ppermute | solution.py:179
  109.1 1.9 %collective-permute-done.6 = bf16[8,2,8,8,256]{4,3,2,1,0:T(8,128)(2,1)S(1)} collective-permute-done((bf16[8,2,8,8,256]{4,3,2,1,0:T(8,128)(2,1)S(1)}, bf16[8,2,8,8,256]{4,3,2,1,0:T(8,128)(2,1)S(1)}, u32[]{:S(2)}, u32[]{:S(2)}) %collective-permute-start.6) | collective-permute-done | bytes 524320 | tf_op jit(solution)/shard_map/ppermute | solution.py:179
  111.1 11.5 %all-to-all-done.3 = f16[4,272,128]{2,1,0:T(8,128)(2,1)S(1)} async-done(((f16[4,272,128]{2,1,0:T(8,128)(2,1)}), f16[4,272,128]{2,1,0:T(8,128)(2,1)S(1)}, u32[]{:S(2)}, u32[]{:S(2)}) %all-to-all-start.3) | async-done | bytes 278560 | tf_op jit(solution)/shard_map/all_to_all | solution.py:226
  122.7 1.9 %shard_map.62 = (bf16[2,8,16,128]{3,2,1,0:T(8,128)(2,1)S(1)}, f32[16,16,256]{2,1,0:T(8,128)}) custom-call(s32[7]{0:T(128)S(1)} %stack.40.ids, f32[2,8,16,128]{3,2,1,0:T(8,128)S(1)} %bitcast.25, bf16[16,2,8,8,256]{4,3,2,1,0:T(8,128)(2,1)S(1)} %pad_maximum_fusion.below), custom_call_target="tpu_custom_call" | custom-call | tf_op jit(solution)/shard_map/pallas_call | solution.py:147
  124.6 9.0 %all-to-all-start.4 = ((f32[16,16,256]{2,1,0:T(8,128)}), f32[16,16,256]{2,1,0:T(8,128)S(1)}, u32[]{:S(2)}, u32[]{:S(2)}) async-start(f32[16,16,256]{2,1,0:T(8,128)} %get-tuple-element.27), calls=%async_computation.4 | async-start | bytes 524288 | tf_op jit(solution)/shard_map/all_to_all | solution.py:230
  133.6 2.0 %collective-permute-start.8 = (bf16[2,8,16,128]{3,2,1,0:T(8,128)(2,1)S(1)}, bf16[2,8,16,128]{3,2,1,0:T(8,128)(2,1)S(1)}, u32[]{:S(2)}, u32[]{:S(2)}) collective-permute-start(bf16[2,8,16,128]{3,2,1,0:T(8,128)(2,1)S(1)} %get-tuple-element.26), channel_id=1, source_target_pairs={{0,1},{1,0},{2,3},{3,2},{4,5},{5,4},{6,7},{7,6},{8,9},{9,8},{10,11... | collective-permute-start | bytes 196616 | tf_op jit(solution)/shard_map/ppermute | solution.py:231
  135.6 6.0 %all-to-all-done.4 = f32[16,16,256]{2,1,0:T(8,128)S(1)} async-done(((f32[16,16,256]{2,1,0:T(8,128)}), f32[16,16,256]{2,1,0:T(8,128)S(1)}, u32[]{:S(2)}, u32[]{:S(2)}) %all-to-all-start.4) | async-done | bytes 262176 | tf_op jit(solution)/shard_map/all_to_all | solution.py:230
  141.7 6.3 %collective-permute-start.7 = (f32[16,256]{1,0:T(8,128)S(1)}, f32[16,256]{1,0:T(8,128)S(1)}, u32[]{:S(2)}, u32[]{:S(2)}) collective-permute-start(f32[16,256]{1,0:T(8,128)S(1)} %reduce_sum.29.part), channel_id=1, source_target_pairs={{0,16},{16,0},{1,17},{17,1},{2,18},{18,2},{3,19},{19,3},{4,20},{20... | collective-permute-start | bytes 49160 | tf_op jit(solution)/shard_map/ppermute | solution.py:233
  148.2 7.8 %collective-permute-done.7.other = f32[16,256]{1,0:T(8,128)S(1)} collective-permute-done((f32[16,256]{1,0:T(8,128)S(1)}, f32[16,256]{1,0:T(8,128)S(1)}, u32[]{:S(2)}, u32[]{:S(2)}) %collective-permute-start.7) | collective-permute-done | bytes 16416 | tf_op jit(solution)/shard_map/ppermute | solution.py:233
  156.7 4.8 %all-to-all-start.5 = ((f32[16,16,256]{2,1,0:T(8,128)}), f32[16,16,256]{2,1,0:T(8,128)S(1)}, u32[]{:S(2)}, u32[]{:S(2)}) async-start(f32[16,16,256]{2,1,0:T(8,128)} %shard_map.63), calls=%async_computation.5 | async-start | bytes 524288 | tf_op jit(solution)/shard_map/all_to_all | solution.py:237
  162.4 6.6 %all-to-all-done.5 = f32[16,16,256]{2,1,0:T(8,128)S(1)} async-done(((f32[16,16,256]{2,1,0:T(8,128)}), f32[16,16,256]{2,1,0:T(8,128)S(1)}, u32[]{:S(2)}, u32[]{:S(2)}) %all-to-all-start.5) | async-done | bytes 262176 | tf_op jit(solution)/shard_map/all_to_all | solution.py:237
  (35 shorter events, 3.3 us)
Async XLA Ops:
  0.6 147.4 %copy-start = (f32[2,8,16,256]{3,2,1,0:T(8,128)S(1)}, f32[2,8,16,256]{3,2,1,0:T(8,128)}, u32[]{:S(2)}) copy-start(f32[2,8,16,256]{3,2,1,0:T(8,128)} %param.6) | copy-start | bytes 786436
  0.6 0.9 copy-start.1
  1.5 10.8 %copy-start.2 = (bf16[2,8,1,8,256]{4,3,2,1,0:T(8,128)(2,1)S(1)}, bf16[2,8,1,8,256]{4,3,2,1,0:T(8,128)(2,1)}, u32[]{:S(2)}) copy-start(bf16[2,8,1,8,256]{4,3,2,1,0:T(8,128)(2,1)} %param.5) | copy-start | bytes 196612
  2.8 26.1 %all-to-all-start = ((bf16[32,2,8,8,128]{4,3,2,1,0:T(8,128)(2,1)}), bf16[32,2,8,8,128]{4,3,2,1,0:T(8,128)(2,1)S(1)}, u32[]{:S(2)}, u32[]{:S(2)}) async-start(bf16[32,2,8,8,128]{4,3,2,1,0:T(8,128)(2,1)} %bitcast.8), calls=%async_computation | async-start | bytes 2097152 | tf_op jit(solution)/shard_map/all_to_all | solution.py:193
  12.3 48.6 %copy-start.3 = (s32[8,16]{1,0:T(8,128)S(1)}, s32[8,16]{1,0:T(8,128)}, u32[]{:S(2)}) copy-start(s32[8,16]{1,0:T(8,128)} %st.1) | copy-start | bytes 1540
  12.4 16.6 %collective-permute-start = (bf16[2,8,8,256]{3,2,1,0:T(8,128)(2,1)S(1)}, bf16[2,8,8,256]{3,2,1,0:T(8,128)(2,1)S(1)}, u32[]{:S(2)}, u32[]{:S(2)}) collective-permute-start(bf16[2,8,8,256]{3,2,1,0:T(8,128)(2,1)S(1)} %bitcast.27), channel_id=1, source_target_pairs={{0,16},{16,0},{1,17},{17,1},{2,18},{18,2},{3,19},{19,3},{4,20},{20... | collective-permute-start | bytes 196616 | tf_op jit(solution)/shard_map/ppermute | solution.py:191
  28.9 32.0 %collective-permute-start.3 = (bf16[2,1024,512]{2,1,0:T(8,128)(2,1)}, bf16[2,1024,512]{2,1,0:T(8,128)(2,1)}, u32[]{:S(2)}, u32[]{:S(2)}) collective-permute-start(bf16[2,1024,512]{2,1,0:T(8,128)(2,1)} %own.1), channel_id=1, source_target_pairs={{0,32},{32,0},{1,33},{33,1},{2,34},{34,2},{3,35},{35,3},{4,36},{36... | collective-permute-start | bytes 6291464 | tf_op jit(solution)/shard_map/ppermute | solution.py:196
  32.1 28.8 %all-to-all-start.1 = ((bf16[32,2,8,8,128]{4,3,2,1,0:T(8,128)(2,1)}), bf16[32,2,8,8,128]{4,3,2,1,0:T(8,128)(2,1)S(1)}, u32[]{:S(2)}, u32[]{:S(2)}) async-start(bf16[32,2,8,8,128]{4,3,2,1,0:T(8,128)(2,1)} %bitcast.9), calls=%async_computation.1 | async-start | bytes 2097152 | tf_op jit(solution)/shard_map/all_to_all | solution.py:198
  39.6 16.9 %collective-permute-start.1 = (bf16[2,8,8,256]{3,2,1,0:T(8,128)(2,1)S(1)}, bf16[2,8,8,256]{3,2,1,0:T(8,128)(2,1)S(1)}, u32[]{:S(2)}, u32[]{:S(2)}) collective-permute-start(bf16[2,8,8,256]{3,2,1,0:T(8,128)(2,1)S(1)} %bitcast.28), channel_id=1, source_target_pairs={{0,0},{1,32},{2,64},{3,96},{4,128},{5,160},{6,192},{7,224},{8,256}... | collective-permute-start | bytes 196616 | tf_op jit(solution)/shard_map/ppermute | solution.py:208
  41.7 19.2 %collective-permute-start.2 = (bf16[2,8,8,256]{3,2,1,0:T(8,128)(2,1)S(1)}, bf16[2,8,8,256]{3,2,1,0:T(8,128)(2,1)S(1)}, u32[]{:S(2)}, u32[]{:S(2)}) collective-permute-start(bf16[2,8,8,256]{3,2,1,0:T(8,128)(2,1)S(1)} %bitcast.29), channel_id=1, source_target_pairs={{0,256},{1,288},{2,320},{3,352},{4,384},{5,416},{6,448},{7,480},{8... | collective-permute-start | bytes 196616 | tf_op jit(solution)/shard_map/ppermute | solution.py:208
  68.8 26.9 %all-to-all-start.2 = ((f16[4,1040,128]{2,1,0:T(8,128)(2,1)}), f16[4,1040,128]{2,1,0:T(8,128)(2,1)S(1)}, u32[]{:S(2)}, u32[]{:S(2)}) async-start(f16[4,1040,128]{2,1,0:T(8,128)(2,1)} %convert_element_type.10), calls=%async_computation.2 | async-start | bytes 2129920 | tf_op jit(solution)/shard_map/all_to_all | solution.py:217
  78.3 15.4 %collective-permute-start.4 = (bf16[2,2,8,8,256]{4,3,2,1,0:T(8,128)(2,1)S(1)}, bf16[2,2,8,8,256]{4,3,2,1,0:T(8,128)(2,1)S(1)}, u32[]{:S(2)}, u32[]{:S(2)}) collective-permute-start(bf16[2,2,8,8,256]{4,3,2,1,0:T(8,128)(2,1)S(1)} %pad_maximum_fusion.5), channel_id=1, source_target_pairs={{0,128},{128,0},{1,129},{129,1},{2,130},{130,2},{3,131},{131,3},{4... | collective-permute-start | bytes 393224 | tf_op jit(solution)/shard_map/ppermute | solution.py:179
  96.9 10.2 %collective-permute-start.5 = (bf16[4,2,8,8,256]{4,3,2,1,0:T(8,128)(2,1)S(1)}, bf16[4,2,8,8,256]{4,3,2,1,0:T(8,128)(2,1)S(1)}, u32[]{:S(2)}, u32[]{:S(2)}) collective-permute-start(bf16[4,2,8,8,256]{4,3,2,1,0:T(8,128)(2,1)S(1)} %pad_maximum_fusion.3), channel_id=1, source_target_pairs={{0,64},{64,0},{1,65},{65,1},{2,66},{66,2},{3,67},{67,3},{4,68},{68... | collective-permute-start | bytes 786440 | tf_op jit(solution)/shard_map/ppermute | solution.py:179
  101.7 20.9 %all-to-all-start.3 = ((f16[4,272,128]{2,1,0:T(8,128)(2,1)}), f16[4,272,128]{2,1,0:T(8,128)(2,1)S(1)}, u32[]{:S(2)}, u32[]{:S(2)}) async-start(f16[4,272,128]{2,1,0:T(8,128)(2,1)} %pad_maximum_fusion.2), calls=%async_computation.3 | async-start | bytes 557056 | tf_op jit(solution)/shard_map/all_to_all | solution.py:226
  107.2 3.8 %collective-permute-start.6 = (bf16[8,2,8,8,256]{4,3,2,1,0:T(8,128)(2,1)S(1)}, bf16[8,2,8,8,256]{4,3,2,1,0:T(8,128)(2,1)S(1)}, u32[]{:S(2)}, u32[]{:S(2)}) collective-permute-start(bf16[8,2,8,8,256]{4,3,2,1,0:T(8,128)(2,1)S(1)} %pad_maximum_fusion.1), channel_id=1, source_target_pairs={{0,32},{32,0},{1,33},{33,1},{2,34},{34,2},{3,35},{35,3},{4,36},{36... | collective-permute-start | bytes 1572872 | tf_op jit(solution)/shard_map/ppermute | solution.py:179
  124.6 17.0 %all-to-all-start.4 = ((f32[16,16,256]{2,1,0:T(8,128)}), f32[16,16,256]{2,1,0:T(8,128)S(1)}, u32[]{:S(2)}, u32[]{:S(2)}) async-start(f32[16,16,256]{2,1,0:T(8,128)} %get-tuple-element.27), calls=%async_computation.4 | async-start | bytes 524288 | tf_op jit(solution)/shard_map/all_to_all | solution.py:230
  133.6 14.6 %collective-permute-start.8 = (bf16[2,8,16,128]{3,2,1,0:T(8,128)(2,1)S(1)}, bf16[2,8,16,128]{3,2,1,0:T(8,128)(2,1)S(1)}, u32[]{:S(2)}, u32[]{:S(2)}) collective-permute-start(bf16[2,8,16,128]{3,2,1,0:T(8,128)(2,1)S(1)} %get-tuple-element.26), channel_id=1, source_target_pairs={{0,1},{1,0},{2,3},{3,2},{4,5},{5,4},{6,7},{7,6},{8,9},{9,8},{10,11... | collective-permute-start | bytes 196616 | tf_op jit(solution)/shard_map/ppermute | solution.py:231
  141.7 14.3 %collective-permute-start.7 = (f32[16,256]{1,0:T(8,128)S(1)}, f32[16,256]{1,0:T(8,128)S(1)}, u32[]{:S(2)}, u32[]{:S(2)}) collective-permute-start(f32[16,256]{1,0:T(8,128)S(1)} %reduce_sum.29.part), channel_id=1, source_target_pairs={{0,16},{16,0},{1,17},{17,1},{2,18},{18,2},{3,19},{19,3},{4,20},{20... | collective-permute-start | bytes 49160 | tf_op jit(solution)/shard_map/ppermute | solution.py:233
  156.7 12.2 %all-to-all-start.5 = ((f32[16,16,256]{2,1,0:T(8,128)}), f32[16,16,256]{2,1,0:T(8,128)S(1)}, u32[]{:S(2)}, u32[]{:S(2)}) async-start(f32[16,16,256]{2,1,0:T(8,128)} %shard_map.63), calls=%async_computation.5 | async-start | bytes 524288 | tf_op jit(solution)/shard_map/all_to_all | solution.py:237

commit v7 on v6

--- a/solution.py
+++ b/solution.py
@@ -66,29 +66,22 @@
     form = (((0,), (0,)), ((), ()))
     largest = jnp.zeros((8, 128), F32)
     for k in range(8):
-        total = None
+        left, right_re, right_im = [], [], []
         for source, blocks in ((core, own), (1 - core, sib)):
             down, right = block_at(k, ids[0] - core + source, st, ids)
-            left = []
-            right_re, right_im = [], []
             for panel, half in ((near, zh), (far, 1 - zh)):
                 rows = pl.ds(pl.multiple_of(down + 128 * half, 128), 128)
                 lanes = pl.ds(pl.multiple_of(right, 256), 256)
                 right_re.append(blocks[0, rows, lanes])
                 right_im.append(blocks[1, rows, lanes])
-            for p in range(2):
-                parts = [panel[source, :, p, k].reshape(128, 128) for panel in (near, far)]
-                left.append(jnp.concatenate(parts, axis=0))
-            re = jnp.concatenate(right_re, axis=0)
-            im = jnp.concatenate(right_im, axis=0)
-            one = lax.dot_general(
-                left[0], jnp.concatenate([re, im], axis=1), form, preferred_element_type=F32
-            )
-            two = lax.dot_general(
-                left[1], jnp.concatenate([-im, re], axis=1), form, preferred_element_type=F32
-            )
-            both = one + two
-            total = both if total is None else total + both
+                parts = [panel[source, :, p, k].reshape(128, 128) for p in range(2)]
+                left.append(jnp.concatenate(parts, axis=1))
+        left = jnp.concatenate(left, axis=0)
+        right_re = jnp.concatenate(right_re, axis=0)
+        right_im = jnp.concatenate(right_im, axis=0)
+        one = lax.dot_general(left, right_re, form, preferred_element_type=F32)
+        two = lax.dot_general(left, right_im, form, preferred_element_type=F32)
+        total = jnp.concatenate([one[:128] - two[128:], one[128:] + two[:128]], axis=1)
         total = jnp.where(present(k, st, ids), total, 0.0)
         size = jnp.max(jnp.abs(total).reshape(16, 8, 512), axis=0)
         for lane in range(4):
@@ -127,7 +120,7 @@
             upper = (-summed[p, k]).astype(BF)
             half[p, k] = upper
             left.append(upper)
-        left = jnp.concatenate(left, axis=1)
+        left = jnp.concatenate(left, axis=0)
         panel = []
         for p in range(2):
             part = []
@@ -136,11 +129,10 @@
                 at = (far % 2) * 8 + (far // 2 % 2) * 4 + (far // 4 % 2) * 2 + far // 8
                 part.append(below[at, p, k].astype(F32))
             panel.append(jnp.concatenate(part, axis=0).astype(BF))
-        re, im = panel
-        right_re = jnp.concatenate([re, -im], axis=0)
-        right_im = jnp.concatenate([im, re], axis=0)
-        out[k] = jnp.dot(left, right_re, preferred_element_type=F32)
-        out[8 + k] = jnp.dot(left, right_im, preferred_element_type=F32)
+        one = jnp.dot(left, panel[0], preferred_element_type=F32)
+        two = jnp.dot(left, panel[1], preferred_element_type=F32)
+        out[k] = one[:16] - two[16:]
+        out[8 + k] = two[:16] + one[16:]
 
 
 def diag_terms(ids, summed, below):
@@ -207,7 +199,6 @@
                     moves.append((q * 32 + 16 * h + m, (m ^ flip) * 32 + 2 * q + h))
         below.append(lax.ppermute(own, ROW + COL, moves))
     below = jnp.stack(below)
-    far, below = tie((far, below))
 
     near = near.reshape(2, 16, 2, 8, 8, 128)
     far = far.reshape(2, 16, 2, 8, 8, 128)

time: 171 us -> 170 us (level)
  starting transfers between devices: 97.3 us -> 88.6 us
  waiting for transfers between devices: 54.1 us -> 62 us
    ppermute x2, waiting for transfers between devices: 4.36 us -> 12.6 us  [shards(): below.append(lax.ppermute(own, ROW + COL, moves))]
    all_to_all x1, starting transfers between devices: 9.51 us -> 3.51 us  [shards(): lax.all_to_all(parts.astype(F16), ('zc', 'h'), 0, 0, tiled=True).astype(F32)]
    ppermute x2, starting transfers between devices: 16.8 us -> 13 us  [shards(): below.append(lax.ppermute(own, ROW + COL, moves))]
    all_to_all x1, waiting for transfers between devices: 11.5 us -> 14.5 us  [shards(): got = lax.all_to_all(parts, ('za', 'zb'), 0, 0, tiled=True).astype(F32)]
    all_to_all x1, starting transfers between devices: 3.46 us -> 6.16 us  [shards(): got = lax.all_to_all(parts, ('za', 'zb'), 0, 0, tiled=True).astype(F32)]
    all_to_all x1, starting transfers between devices: 9.01 us -> 6.43 us  [shards(): terms = lax.all_to_all(terms, PLANE, 0, 0, tiled=True)]
    ppermute x3, waiting for transfers between devices: 13.3 us -> 11 us  [doubled(): return jnp.concatenate([value, lax.ppermute(value, axis, PAIR)], axis=0)]
where the time goes in v7:
time: 170 us; the launch traced here: 169 us
  starting transfers between devices  88.6 us (52%)
  waiting for transfers between devices  62 us (36%)
  Pallas kernels  10.3 us (6%)
  other arithmetic  5.19 us (3%)
  local copies, waits for them, and re-layouts  1.7 us (1%)
    all_to_all x2, starting transfers between devices, shards(): lax.all_to_all(lanes.reshape(32, 2, 8, 8, 128), group, 0, 0, tiled=True)  17 us
    all_to_all x1, waiting for transfers between devices, shards(): got = lax.all_to_all(parts, ('za', 'zb'), 0, 0, tiled=True).astype(F32)  14.5 us
    ppermute x1, starting transfers between devices, shards(): other = lax.ppermute(own, 'zh', PAIR)  13.9 us
    ppermute x2, starting transfers between devices, shards(): below.append(lax.ppermute(own, ROW + COL, moves))  13 us
    ppermute x2, waiting for transfers between devices, shards(): below.append(lax.ppermute(own, ROW + COL, moves))  12.6 us
    ppermute x3, starting transfers between devices, doubled(): return jnp.concatenate([value, lax.ppermute(value, axis, PAIR)], axis=0)  12.5 us
    ppermute x3, waiting for transfers between devices, doubled(): return jnp.concatenate([value, lax.ppermute(value, axis, PAIR)], axis=0)  11 us
    ppermute x1, starting transfers between devices, shards(): other, partner = tie((lax.ppermute(part, 'zh', PAIR), partner))  7.4 us
  transfers between devices with their start and end apart: 15, of which 10 were waited for; matrix products, arithmetic and copies ran while one was open for 1% of the time, Pallas kernels for 1%

profile of v7, /device:TPU:2, one launch (start us, length us, event | category | flops | bytes accessed | tf_op | source)
XLA Modules:
  0.0 168.8 jit_solution(5343850293218390986)
XLA Ops:
  0.7 0.9 copy-done.1
  1.5 1.3 shard_map.59
  2.8 9.5 %all-to-all-start = ((bf16[32,2,8,8,128]{4,3,2,1,0:T(8,128)(2,1)}), bf16[32,2,8,8,128]{4,3,2,1,0:T(8,128)(2,1)S(1)}, u32[]{:S(2)}, u32[]{:S(2)}) async-start(bf16[32,2,8,8,128]{4,3,2,1,0:T(8,128)(2,1)} %bitcast.8), calls=%async_computation | async-start | bytes 2097152 | tf_op jit(solution)/shard_map/all_to_all | solution.py:185
  12.4 13.9 %collective-permute-start = (bf16[2,8,8,256]{3,2,1,0:T(8,128)(2,1)S(1)}, bf16[2,8,8,256]{3,2,1,0:T(8,128)(2,1)S(1)}, u32[]{:S(2)}, u32[]{:S(2)}) collective-permute-start(bf16[2,8,8,256]{3,2,1,0:T(8,128)(2,1)S(1)} %bitcast.27), channel_id=1, source_target_pairs={{0,16},{16,0},{1,17},{17,1},{2,18},{18,2},{3,19},{19,3},{4,20},{20... | collective-permute-start | bytes 196616 | tf_op jit(solution)/shard_map/ppermute | solution.py:183
  26.2 2.7 %collective-permute-done.panel = bf16[2,8,8,256]{3,2,1,0:T(8,128)(2,1)S(1)} collective-permute-done((bf16[2,8,8,256]{3,2,1,0:T(8,128)(2,1)S(1)}, bf16[2,8,8,256]{3,2,1,0:T(8,128)(2,1)S(1)}, u32[]{:S(2)}, u32[]{:S(2)}) %collective-permute-start) | collective-permute-done | bytes 65568 | tf_op jit(solution)/shard_map/ppermute | solution.py:183
  28.9 1.9 %collective-permute-start.3 = (bf16[2,1024,512]{2,1,0:T(8,128)(2,1)}, bf16[2,1024,512]{2,1,0:T(8,128)(2,1)}, u32[]{:S(2)}, u32[]{:S(2)}) collective-permute-start(bf16[2,1024,512]{2,1,0:T(8,128)(2,1)} %own.1), channel_id=1, source_target_pairs={{0,32},{32,0},{1,33},{33,1},{2,34},{34,2},{3,35},{35,3},{4,36},{36... | collective-permute-start | bytes 6291464 | tf_op jit(solution)/shard_map/ppermute | solution.py:188
  30.8 1.3 shard_map.60
  32.1 7.5 %all-to-all-start.1 = ((bf16[32,2,8,8,128]{4,3,2,1,0:T(8,128)(2,1)}), bf16[32,2,8,8,128]{4,3,2,1,0:T(8,128)(2,1)S(1)}, u32[]{:S(2)}, u32[]{:S(2)}) async-start(bf16[32,2,8,8,128]{4,3,2,1,0:T(8,128)(2,1)} %bitcast.12), calls=%async_computation.1 | async-start | bytes 2097152 | tf_op jit(solution)/shard_map/all_to_all | solution.py:190
  39.6 8.0 %collective-permute-start.2 = (bf16[2,8,8,256]{3,2,1,0:T(8,128)(2,1)S(1)}, bf16[2,8,8,256]{3,2,1,0:T(8,128)(2,1)S(1)}, u32[]{:S(2)}, u32[]{:S(2)}) collective-permute-start(bf16[2,8,8,256]{3,2,1,0:T(8,128)(2,1)S(1)} %bitcast.28), channel_id=1, source_target_pairs={{0,256},{1,288},{2,320},{3,352},{4,384},{5,416},{6,448},{7,480},{8... | collective-permute-start | bytes 196616 | tf_op jit(solution)/shard_map/ppermute | solution.py:200
  47.6 5.0 %collective-permute-start.1 = (bf16[2,8,8,256]{3,2,1,0:T(8,128)(2,1)S(1)}, bf16[2,8,8,256]{3,2,1,0:T(8,128)(2,1)S(1)}, u32[]{:S(2)}, u32[]{:S(2)}) collective-permute-start(bf16[2,8,8,256]{3,2,1,0:T(8,128)(2,1)S(1)} %bitcast.29), channel_id=1, source_target_pairs={{0,0},{1,32},{2,64},{3,96},{4,128},{5,160},{6,192},{7,224},{8,256}... | collective-permute-start | bytes 196616 | tf_op jit(solution)/shard_map/ppermute | solution.py:200
  52.8 5.3 %collective-permute-done.2 = bf16[2,8,8,256]{3,2,1,0:T(8,128)(2,1)S(1)} collective-permute-done((bf16[2,8,8,256]{3,2,1,0:T(8,128)(2,1)S(1)}, bf16[2,8,8,256]{3,2,1,0:T(8,128)(2,1)S(1)}, u32[]{:S(2)}, u32[]{:S(2)}) %collective-permute-start.2) | collective-permute-done | bytes 65568 | tf_op jit(solution)/shard_map/ppermute | solution.py:200
  58.1 7.3 %collective-permute-done.1 = bf16[2,8,8,256]{3,2,1,0:T(8,128)(2,1)S(1)} collective-permute-done((bf16[2,8,8,256]{3,2,1,0:T(8,128)(2,1)S(1)}, bf16[2,8,8,256]{3,2,1,0:T(8,128)(2,1)S(1)}, u32[]{:S(2)}, u32[]{:S(2)}) %collective-permute-start.1) | collective-permute-done | bytes 65568 | tf_op jit(solution)/shard_map/ppermute | solution.py:200
  65.4 5.2 %shard_map.61 = f32[4,1040,128]{2,1,0:T(8,128)} custom-call(s32[8,16]{1,0:T(8,128)S(1)} %copy-done.3, s32[7]{0:T(128)S(1)} %stack.40.ids, bf16[2,16,2,8,8,128]{5,4,3,2,1,0:T(8,128)(2,1)S(1)} %bitcast.23, bf16[2,16,2,8,8,128]{5,4,3,2,1,0:T(8,128)(2,1)S(1)} %bitcast.24, bf16[2,1024,512]{2,1,0:T(8,128)(2,1)} %own.1, ...), custom_call_target="tpu_custom_call" | custom-call | tf_op jit(solution)/shard_map/pallas_call | solution.py:106
  70.6 2.7 %convert_element_type.10 = f16[4,1040,128]{2,1,0:T(8,128)(2,1)} convert(f32[4,1040,128]{2,1,0:T(8,128)} %shard_map.61) | non-fusion elementwise | flops 532480 | bytes 3194880 | tf_op jit(solution)/shard_map/convert_element_type | solution.py:208
  73.4 3.5 %all-to-all-start.2 = ((f16[4,1040,128]{2,1,0:T(8,128)(2,1)}), f16[4,1040,128]{2,1,0:T(8,128)(2,1)S(1)}, u32[]{:S(2)}, u32[]{:S(2)}) async-start(f16[4,1040,128]{2,1,0:T(8,128)(2,1)} %convert_element_type.10), calls=%async_computation.2 | async-start | bytes 2129920 | tf_op jit(solution)/shard_map/all_to_all | solution.py:208
  76.9 5.7 %collective-permute-start.4 = (bf16[2,2,8,8,256]{4,3,2,1,0:T(8,128)(2,1)S(1)}, bf16[2,2,8,8,256]{4,3,2,1,0:T(8,128)(2,1)S(1)}, u32[]{:S(2)}, u32[]{:S(2)}) collective-permute-start(bf16[2,2,8,8,256]{4,3,2,1,0:T(8,128)(2,1)S(1)} %pad_maximum_fusion.5), channel_id=1, source_target_pairs={{0,128},{128,0},{1,129},{129,1},{2,130},{130,2},{3,131},{131,3},{4... | collective-permute-start | bytes 393224 | tf_op jit(solution)/shard_map/ppermute | solution.py:171
  82.6 9.2 %collective-permute-done.4 = bf16[2,2,8,8,256]{4,3,2,1,0:T(8,128)(2,1)S(1)} collective-permute-done((bf16[2,2,8,8,256]{4,3,2,1,0:T(8,128)(2,1)S(1)}, bf16[2,2,8,8,256]{4,3,2,1,0:T(8,128)(2,1)S(1)}, u32[]{:S(2)}, u32[]{:S(2)}) %collective-permute-start.4) | collective-permute-done | bytes 131104 | tf_op jit(solution)/shard_map/ppermute | solution.py:171
  91.8 1.9 %all-to-all-done.2 = f16[4,1040,128]{2,1,0:T(8,128)(2,1)S(1)} async-done(((f16[4,1040,128]{2,1,0:T(8,128)(2,1)}), f16[4,1040,128]{2,1,0:T(8,128)(2,1)S(1)}, u32[]{:S(2)}, u32[]{:S(2)}) %all-to-all-start.2) | async-done | bytes 1064992 | tf_op jit(solution)/shard_map/all_to_all | solution.py:208
  94.2 0.8 pad_maximum_fusion.2
  95.0 4.8 %collective-permute-start.5 = (bf16[4,2,8,8,256]{4,3,2,1,0:T(8,128)(2,1)S(1)}, bf16[4,2,8,8,256]{4,3,2,1,0:T(8,128)(2,1)S(1)}, u32[]{:S(2)}, u32[]{:S(2)}) collective-permute-start(bf16[4,2,8,8,256]{4,3,2,1,0:T(8,128)(2,1)S(1)} %pad_maximum_fusion.3), channel_id=1, source_target_pairs={{0,64},{64,0},{1,65},{65,1},{2,66},{66,2},{3,67},{67,3},{4,68},{68... | collective-permute-start | bytes 786440 | tf_op jit(solution)/shard_map/ppermute | solution.py:171
  99.8 6.2 %all-to-all-start.3 = ((f16[4,272,128]{2,1,0:T(8,128)(2,1)}), f16[4,272,128]{2,1,0:T(8,128)(2,1)S(1)}, u32[]{:S(2)}, u32[]{:S(2)}) async-start(f16[4,272,128]{2,1,0:T(8,128)(2,1)} %pad_maximum_fusion.2), calls=%async_computation.3 | async-start | bytes 557056 | tf_op jit(solution)/shard_map/all_to_all | solution.py:217
  106.0 2.1 %collective-permute-start.6 = (bf16[8,2,8,8,256]{4,3,2,1,0:T(8,128)(2,1)S(1)}, bf16[8,2,8,8,256]{4,3,2,1,0:T(8,128)(2,1)S(1)}, u32[]{:S(2)}, u32[]{:S(2)}) collective-permute-start(bf16[8,2,8,8,256]{4,3,2,1,0:T(8,128)(2,1)S(1)} %pad_maximum_fusion.1), channel_id=1, source_target_pairs={{0,32},{32,0},{1,33},{33,1},{2,34},{34,2},{3,35},{35,3},{4,36},{36... | collective-permute-start | bytes 1572872 | tf_op jit(solution)/shard_map/ppermute | solution.py:171
  108.0 1.7 %collective-permute-done.6 = bf16[8,2,8,8,256]{4,3,2,1,0:T(8,128)(2,1)S(1)} collective-permute-done((bf16[8,2,8,8,256]{4,3,2,1,0:T(8,128)(2,1)S(1)}, bf16[8,2,8,8,256]{4,3,2,1,0:T(8,128)(2,1)S(1)}, u32[]{:S(2)}, u32[]{:S(2)}) %collective-permute-start.6) | collective-permute-done | bytes 524320 | tf_op jit(solution)/shard_map/ppermute | solution.py:171
  109.9 14.5 %all-to-all-done.3 = f16[4,272,128]{2,1,0:T(8,128)(2,1)S(1)} async-done(((f16[4,272,128]{2,1,0:T(8,128)(2,1)}), f16[4,272,128]{2,1,0:T(8,128)(2,1)S(1)}, u32[]{:S(2)}, u32[]{:S(2)}) %all-to-all-start.3) | async-done | bytes 278560 | tf_op jit(solution)/shard_map/all_to_all | solution.py:217
  124.5 1.8 %shard_map.62 = (bf16[2,8,16,128]{3,2,1,0:T(8,128)(2,1)S(1)}, f32[16,16,256]{2,1,0:T(8,128)}) custom-call(s32[7]{0:T(128)S(1)} %stack.40.ids, f32[2,8,16,128]{3,2,1,0:T(8,128)S(1)} %bitcast.25, bf16[16,2,8,8,256]{4,3,2,1,0:T(8,128)(2,1)S(1)} %pad_maximum_fusion.below), custom_call_target="tpu_custom_call" | custom-call | tf_op jit(solution)/shard_map/pallas_call | solution.py:139
  126.3 6.4 %all-to-all-start.4 = ((f32[16,16,256]{2,1,0:T(8,128)}), f32[16,16,256]{2,1,0:T(8,128)S(1)}, u32[]{:S(2)}, u32[]{:S(2)}) async-start(f32[16,16,256]{2,1,0:T(8,128)} %get-tuple-element.23), calls=%async_computation.4 | async-start | bytes 524288 | tf_op jit(solution)/shard_map/all_to_all | solution.py:221
  132.7 2.0 %collective-permute-start.8 = (bf16[2,8,16,128]{3,2,1,0:T(8,128)(2,1)S(1)}, bf16[2,8,16,128]{3,2,1,0:T(8,128)(2,1)S(1)}, u32[]{:S(2)}, u32[]{:S(2)}) collective-permute-start(bf16[2,8,16,128]{3,2,1,0:T(8,128)(2,1)S(1)} %get-tuple-element.22), channel_id=1, source_target_pairs={{0,1},{1,0},{2,3},{3,2},{4,5},{5,4},{6,7},{7,6},{8,9},{9,8},{10,11... | collective-permute-start | bytes 196616 | tf_op jit(solution)/shard_map/ppermute | solution.py:222
  134.7 6.0 %all-to-all-done.4 = f32[16,16,256]{2,1,0:T(8,128)S(1)} async-done(((f32[16,16,256]{2,1,0:T(8,128)}), f32[16,16,256]{2,1,0:T(8,128)S(1)}, u32[]{:S(2)}, u32[]{:S(2)}) %all-to-all-start.4) | async-done | bytes 262176 | tf_op jit(solution)/shard_map/all_to_all | solution.py:221
  140.8 7.4 %collective-permute-start.7 = (f32[16,256]{1,0:T(8,128)S(1)}, f32[16,256]{1,0:T(8,128)S(1)}, u32[]{:S(2)}, u32[]{:S(2)}) collective-permute-start(f32[16,256]{1,0:T(8,128)S(1)} %reduce_sum.29.part), channel_id=1, source_target_pairs={{0,16},{16,0},{1,17},{17,1},{2,18},{18,2},{3,19},{19,3},{4,20},{20... | collective-permute-start | bytes 49160 | tf_op jit(solution)/shard_map/ppermute | solution.py:224
  148.4 6.7 %collective-permute-done.7.other = f32[16,256]{1,0:T(8,128)S(1)} collective-permute-done((f32[16,256]{1,0:T(8,128)S(1)}, f32[16,256]{1,0:T(8,128)S(1)}, u32[]{:S(2)}, u32[]{:S(2)}) %collective-permute-start.7) | collective-permute-done | bytes 16416 | tf_op jit(solution)/shard_map/ppermute | solution.py:224
  155.9 4.8 %all-to-all-start.5 = ((f32[16,16,256]{2,1,0:T(8,128)}), f32[16,16,256]{2,1,0:T(8,128)S(1)}, u32[]{:S(2)}, u32[]{:S(2)}) async-start(f32[16,16,256]{2,1,0:T(8,128)} %shard_map.63), calls=%async_computation.5 | async-start | bytes 524288 | tf_op jit(solution)/shard_map/all_to_all | solution.py:228
  161.5 6.6 %all-to-all-done.5 = f32[16,16,256]{2,1,0:T(8,128)S(1)} async-done(((f32[16,16,256]{2,1,0:T(8,128)}), f32[16,16,256]{2,1,0:T(8,128)S(1)}, u32[]{:S(2)}, u32[]{:S(2)}) %all-to-all-start.5) | async-done | bytes 262176 | tf_op jit(solution)/shard_map/all_to_all | solution.py:228
  (35 shorter events, 3.3 us)
Async XLA Ops:
  0.6 147.6 %copy-start = (f32[2,8,16,256]{3,2,1,0:T(8,128)S(1)}, f32[2,8,16,256]{3,2,1,0:T(8,128)}, u32[]{:S(2)}) copy-start(f32[2,8,16,256]{3,2,1,0:T(8,128)} %param.6) | copy-start | bytes 786436
  0.6 0.9 copy-start.1
  1.5 10.8 %copy-start.2 = (bf16[2,8,1,8,256]{4,3,2,1,0:T(8,128)(2,1)S(1)}, bf16[2,8,1,8,256]{4,3,2,1,0:T(8,128)(2,1)}, u32[]{:S(2)}) copy-start(bf16[2,8,1,8,256]{4,3,2,1,0:T(8,128)(2,1)} %param.5) | copy-start | bytes 196612
  2.8 26.1 %all-to-all-start = ((bf16[32,2,8,8,128]{4,3,2,1,0:T(8,128)(2,1)}), bf16[32,2,8,8,128]{4,3,2,1,0:T(8,128)(2,1)S(1)}, u32[]{:S(2)}, u32[]{:S(2)}) async-start(bf16[32,2,8,8,128]{4,3,2,1,0:T(8,128)(2,1)} %bitcast.8), calls=%async_computation | async-start | bytes 2097152 | tf_op jit(solution)/shard_map/all_to_all | solution.py:185
  12.3 53.1 %copy-start.3 = (s32[8,16]{1,0:T(8,128)S(1)}, s32[8,16]{1,0:T(8,128)}, u32[]{:S(2)}) copy-start(s32[8,16]{1,0:T(8,128)} %st.1) | copy-start | bytes 1540
  12.4 16.6 %collective-permute-start = (bf16[2,8,8,256]{3,2,1,0:T(8,128)(2,1)S(1)}, bf16[2,8,8,256]{3,2,1,0:T(8,128)(2,1)S(1)}, u32[]{:S(2)}, u32[]{:S(2)}) collective-permute-start(bf16[2,8,8,256]{3,2,1,0:T(8,128)(2,1)S(1)} %bitcast.27), channel_id=1, source_target_pairs={{0,16},{16,0},{1,17},{17,1},{2,18},{18,2},{3,19},{19,3},{4,20},{20... | collective-permute-start | bytes 196616 | tf_op jit(solution)/shard_map/ppermute | solution.py:183
  28.9 36.5 %collective-permute-start.3 = (bf16[2,1024,512]{2,1,0:T(8,128)(2,1)}, bf16[2,1024,512]{2,1,0:T(8,128)(2,1)}, u32[]{:S(2)}, u32[]{:S(2)}) collective-permute-start(bf16[2,1024,512]{2,1,0:T(8,128)(2,1)} %own.1), channel_id=1, source_target_pairs={{0,32},{32,0},{1,33},{33,1},{2,34},{34,2},{3,35},{35,3},{4,36},{36... | collective-permute-start | bytes 6291464 | tf_op jit(solution)/shard_map/ppermute | solution.py:188
  32.1 33.3 %all-to-all-start.1 = ((bf16[32,2,8,8,128]{4,3,2,1,0:T(8,128)(2,1)}), bf16[32,2,8,8,128]{4,3,2,1,0:T(8,128)(2,1)S(1)}, u32[]{:S(2)}, u32[]{:S(2)}) async-start(bf16[32,2,8,8,128]{4,3,2,1,0:T(8,128)(2,1)} %bitcast.12), calls=%async_computation.1 | async-start | bytes 2097152 | tf_op jit(solution)/shard_map/all_to_all | solution.py:190
  39.6 18.4 %collective-permute-start.2 = (bf16[2,8,8,256]{3,2,1,0:T(8,128)(2,1)S(1)}, bf16[2,8,8,256]{3,2,1,0:T(8,128)(2,1)S(1)}, u32[]{:S(2)}, u32[]{:S(2)}) collective-permute-start(bf16[2,8,8,256]{3,2,1,0:T(8,128)(2,1)S(1)} %bitcast.28), channel_id=1, source_target_pairs={{0,256},{1,288},{2,320},{3,352},{4,384},{5,416},{6,448},{7,480},{8... | collective-permute-start | bytes 196616 | tf_op jit(solution)/shard_map/ppermute | solution.py:200
  47.6 17.8 %collective-permute-start.1 = (bf16[2,8,8,256]{3,2,1,0:T(8,128)(2,1)S(1)}, bf16[2,8,8,256]{3,2,1,0:T(8,128)(2,1)S(1)}, u32[]{:S(2)}, u32[]{:S(2)}) collective-permute-start(bf16[2,8,8,256]{3,2,1,0:T(8,128)(2,1)S(1)} %bitcast.29), channel_id=1, source_target_pairs={{0,0},{1,32},{2,64},{3,96},{4,128},{5,160},{6,192},{7,224},{8,256}... | collective-permute-start | bytes 196616 | tf_op jit(solution)/shard_map/ppermute | solution.py:200
  73.4 20.4 %all-to-all-start.2 = ((f16[4,1040,128]{2,1,0:T(8,128)(2,1)}), f16[4,1040,128]{2,1,0:T(8,128)(2,1)S(1)}, u32[]{:S(2)}, u32[]{:S(2)}) async-start(f16[4,1040,128]{2,1,0:T(8,128)(2,1)} %convert_element_type.10), calls=%async_computation.2 | async-start | bytes 2129920 | tf_op jit(solution)/shard_map/all_to_all | solution.py:208
  76.9 14.9 %collective-permute-start.4 = (bf16[2,2,8,8,256]{4,3,2,1,0:T(8,128)(2,1)S(1)}, bf16[2,2,8,8,256]{4,3,2,1,0:T(8,128)(2,1)S(1)}, u32[]{:S(2)}, u32[]{:S(2)}) collective-permute-start(bf16[2,2,8,8,256]{4,3,2,1,0:T(8,128)(2,1)S(1)} %pad_maximum_fusion.5), channel_id=1, source_target_pairs={{0,128},{128,0},{1,129},{129,1},{2,130},{130,2},{3,131},{131,3},{4... | collective-permute-start | bytes 393224 | tf_op jit(solution)/shard_map/ppermute | solution.py:171
  95.0 11.0 %collective-permute-start.5 = (bf16[4,2,8,8,256]{4,3,2,1,0:T(8,128)(2,1)S(1)}, bf16[4,2,8,8,256]{4,3,2,1,0:T(8,128)(2,1)S(1)}, u32[]{:S(2)}, u32[]{:S(2)}) collective-permute-start(bf16[4,2,8,8,256]{4,3,2,1,0:T(8,128)(2,1)S(1)} %pad_maximum_fusion.3), channel_id=1, source_target_pairs={{0,64},{64,0},{1,65},{65,1},{2,66},{66,2},{3,67},{67,3},{4,68},{68... | collective-permute-start | bytes 786440 | tf_op jit(solution)/shard_map/ppermute | solution.py:171
  99.8 24.7 %all-to-all-start.3 = ((f16[4,272,128]{2,1,0:T(8,128)(2,1)}), f16[4,272,128]{2,1,0:T(8,128)(2,1)S(1)}, u32[]{:S(2)}, u32[]{:S(2)}) async-start(f16[4,272,128]{2,1,0:T(8,128)(2,1)} %pad_maximum_fusion.2), calls=%async_computation.3 | async-start | bytes 557056 | tf_op jit(solution)/shard_map/all_to_all | solution.py:217
  106.0 3.8 %collective-permute-start.6 = (bf16[8,2,8,8,256]{4,3,2,1,0:T(8,128)(2,1)S(1)}, bf16[8,2,8,8,256]{4,3,2,1,0:T(8,128)(2,1)S(1)}, u32[]{:S(2)}, u32[]{:S(2)}) collective-permute-start(bf16[8,2,8,8,256]{4,3,2,1,0:T(8,128)(2,1)S(1)} %pad_maximum_fusion.1), channel_id=1, source_target_pairs={{0,32},{32,0},{1,33},{33,1},{2,34},{34,2},{3,35},{35,3},{4,36},{36... | collective-permute-start | bytes 1572872 | tf_op jit(solution)/shard_map/ppermute | solution.py:171
  126.3 14.4 %all-to-all-start.4 = ((f32[16,16,256]{2,1,0:T(8,128)}), f32[16,16,256]{2,1,0:T(8,128)S(1)}, u32[]{:S(2)}, u32[]{:S(2)}) async-start(f32[16,16,256]{2,1,0:T(8,128)} %get-tuple-element.23), calls=%async_computation.4 | async-start | bytes 524288 | tf_op jit(solution)/shard_map/all_to_all | solution.py:221
  132.7 15.7 %collective-permute-start.8 = (bf16[2,8,16,128]{3,2,1,0:T(8,128)(2,1)S(1)}, bf16[2,8,16,128]{3,2,1,0:T(8,128)(2,1)S(1)}, u32[]{:S(2)}, u32[]{:S(2)}) collective-permute-start(bf16[2,8,16,128]{3,2,1,0:T(8,128)(2,1)S(1)} %get-tuple-element.22), channel_id=1, source_target_pairs={{0,1},{1,0},{2,3},{3,2},{4,5},{5,4},{6,7},{7,6},{8,9},{9,8},{10,11... | collective-permute-start | bytes 196616 | tf_op jit(solution)/shard_map/ppermute | solution.py:222
  140.8 14.3 %collective-permute-start.7 = (f32[16,256]{1,0:T(8,128)S(1)}, f32[16,256]{1,0:T(8,128)S(1)}, u32[]{:S(2)}, u32[]{:S(2)}) collective-permute-start(f32[16,256]{1,0:T(8,128)S(1)} %reduce_sum.29.part), channel_id=1, source_target_pairs={{0,16},{16,0},{1,17},{17,1},{2,18},{18,2},{3,19},{19,3},{4,20},{20... | collective-permute-start | bytes 49160 | tf_op jit(solution)/shard_map/ppermute | solution.py:224
  155.9 12.2 %all-to-all-start.5 = ((f32[16,16,256]{2,1,0:T(8,128)}), f32[16,16,256]{2,1,0:T(8,128)S(1)}, u32[]{:S(2)}, u32[]{:S(2)}) async-start(f32[16,16,256]{2,1,0:T(8,128)} %shard_map.63), calls=%async_computation.5 | async-start | bytes 524288 | tf_op jit(solution)/shard_map/all_to_all | solution.py:228

commit v8 on v7

--- a/solution.py
+++ b/solution.py
@@ -211,7 +211,6 @@
     parts = jnp.sum(got[:, :1024] * jnp.exp2(power - most), axis=0).reshape(4, 256, 128)
     parts = jnp.concatenate([parts, jnp.broadcast_to(most, (4, 16, 128))], axis=1).astype(F16)
 
-    below, parts = tie((below, parts))
     below = doubled(below, "zc")
     below = doubled(below, "core")
     got = lax.all_to_all(parts, ("za", "zb"), 0, 0, tiled=True).astype(F32)

time: 170 us -> 170 us (level)
  starting transfers between devices: 88.6 us -> 90.7 us
  waiting for transfers between devices: 62 us -> 59.9 us
    all_to_all x1, waiting for transfers between devices: 1.93 us -> 0.01 us  [shards(): lax.all_to_all(parts.astype(F16), ('zc', 'h'), 0, 0, tiled=True).astype(F32)]
    ppermute x3, starting transfers between devices: 12.5 us -> 14.5 us  [doubled(): return jnp.concatenate([value, lax.ppermute(value, axis, PAIR)], axis=0)]
  transfers between devices with their start and end apart: 15 -> 15, of which waited for: 10 -> 9; matrix products, arithmetic and copies ran while one was open for 1% -> 1% of each run, Pallas kernels for 1% -> 1%
where the time goes in v8:
time: 170 us; the launch traced here: 169 us
  starting transfers between devices  90.7 us (53%)
  waiting for transfers between devices  59.9 us (35%)
  Pallas kernels  10.3 us (6%)
  other arithmetic  5.2 us (3%)
  local copies, waits for them, and re-layouts  1.7 us (1%)
    all_to_all x2, starting transfers between devices, shards(): lax.all_to_all(lanes.reshape(32, 2, 8, 8, 128), group, 0, 0, tiled=True)  17 us
    all_to_all x1, waiting for transfers between devices, shards(): got = lax.all_to_all(parts, ('za', 'zb'), 0, 0, tiled=True).astype(F32)  14.5 us
    ppermute x3, starting transfers between devices, doubled(): return jnp.concatenate([value, lax.ppermute(value, axis, PAIR)], axis=0)  14.5 us
    ppermute x1, starting transfers between devices, shards(): other = lax.ppermute(own, 'zh', PAIR)  13.9 us
    ppermute x2, starting transfers between devices, shards(): below.append(lax.ppermute(own, ROW + COL, moves))  13 us
    ppermute x2, waiting for transfers between devices, shards(): below.append(lax.ppermute(own, ROW + COL, moves))  12.6 us
    ppermute x3, waiting for transfers between devices, doubled(): return jnp.concatenate([value, lax.ppermute(value, axis, PAIR)], axis=0)  11 us
    ppermute x1, starting transfers between devices, shards(): other, partner = tie((lax.ppermute(part, 'zh', PAIR), partner))  7.5 us
  transfers between devices with their start and end apart: 15, of which 9 were waited for; matrix products, arithmetic and copies ran while one was open for 1% of the time, Pallas kernels for 1%

profile of v8, /device:TPU:2, one launch (start us, length us, event | category | flops | bytes accessed | tf_op | source)
XLA Modules:
  0.0 168.8 jit_solution(16547853452321369552)
XLA Ops:
  0.7 0.9 copy-done.1
  1.5 1.3 shard_map.59
  2.8 9.5 %all-to-all-start = ((bf16[32,2,8,8,128]{4,3,2,1,0:T(8,128)(2,1)}), bf16[32,2,8,8,128]{4,3,2,1,0:T(8,128)(2,1)S(1)}, u32[]{:S(2)}, u32[]{:S(2)}) async-start(bf16[32,2,8,8,128]{4,3,2,1,0:T(8,128)(2,1)} %bitcast.8), calls=%async_computation | async-start | bytes 2097152 | tf_op jit(solution)/shard_map/all_to_all | solution.py:185
  12.4 13.9 %collective-permute-start = (bf16[2,8,8,256]{3,2,1,0:T(8,128)(2,1)S(1)}, bf16[2,8,8,256]{3,2,1,0:T(8,128)(2,1)S(1)}, u32[]{:S(2)}, u32[]{:S(2)}) collective-permute-start(bf16[2,8,8,256]{3,2,1,0:T(8,128)(2,1)S(1)} %bitcast.27), channel_id=1, source_target_pairs={{0,16},{16,0},{1,17},{17,1},{2,18},{18,2},{3,19},{19,3},{4,20},{20... | collective-permute-start | bytes 196616 | tf_op jit(solution)/shard_map/ppermute | solution.py:183
  26.2 2.7 %collective-permute-done.panel = bf16[2,8,8,256]{3,2,1,0:T(8,128)(2,1)S(1)} collective-permute-done((bf16[2,8,8,256]{3,2,1,0:T(8,128)(2,1)S(1)}, bf16[2,8,8,256]{3,2,1,0:T(8,128)(2,1)S(1)}, u32[]{:S(2)}, u32[]{:S(2)}) %collective-permute-start) | collective-permute-done | bytes 65568 | tf_op jit(solution)/shard_map/ppermute | solution.py:183
  28.9 1.9 %collective-permute-start.3 = (bf16[2,1024,512]{2,1,0:T(8,128)(2,1)}, bf16[2,1024,512]{2,1,0:T(8,128)(2,1)}, u32[]{:S(2)}, u32[]{:S(2)}) collective-permute-start(bf16[2,1024,512]{2,1,0:T(8,128)(2,1)} %own.1), channel_id=1, source_target_pairs={{0,32},{32,0},{1,33},{33,1},{2,34},{34,2},{3,35},{35,3},{4,36},{36... | collective-permute-start | bytes 6291464 | tf_op jit(solution)/shard_map/ppermute | solution.py:188
  30.8 1.3 shard_map.60
  32.1 7.5 %all-to-all-start.1 = ((bf16[32,2,8,8,128]{4,3,2,1,0:T(8,128)(2,1)}), bf16[32,2,8,8,128]{4,3,2,1,0:T(8,128)(2,1)S(1)}, u32[]{:S(2)}, u32[]{:S(2)}) async-start(bf16[32,2,8,8,128]{4,3,2,1,0:T(8,128)(2,1)} %bitcast.12), calls=%async_computation.1 | async-start | bytes 2097152 | tf_op jit(solution)/shard_map/all_to_all | solution.py:190
  39.6 8.0 %collective-permute-start.2 = (bf16[2,8,8,256]{3,2,1,0:T(8,128)(2,1)S(1)}, bf16[2,8,8,256]{3,2,1,0:T(8,128)(2,1)S(1)}, u32[]{:S(2)}, u32[]{:S(2)}) collective-permute-start(bf16[2,8,8,256]{3,2,1,0:T(8,128)(2,1)S(1)} %bitcast.28), channel_id=1, source_target_pairs={{0,256},{1,288},{2,320},{3,352},{4,384},{5,416},{6,448},{7,480},{8... | collective-permute-start | bytes 196616 | tf_op jit(solution)/shard_map/ppermute | solution.py:200
  47.6 5.0 %collective-permute-start.1 = (bf16[2,8,8,256]{3,2,1,0:T(8,128)(2,1)S(1)}, bf16[2,8,8,256]{3,2,1,0:T(8,128)(2,1)S(1)}, u32[]{:S(2)}, u32[]{:S(2)}) collective-permute-start(bf16[2,8,8,256]{3,2,1,0:T(8,128)(2,1)S(1)} %bitcast.29), channel_id=1, source_target_pairs={{0,0},{1,32},{2,64},{3,96},{4,128},{5,160},{6,192},{7,224},{8,256}... | collective-permute-start | bytes 196616 | tf_op jit(solution)/shard_map/ppermute | solution.py:200
  52.8 5.3 %collective-permute-done.2 = bf16[2,8,8,256]{3,2,1,0:T(8,128)(2,1)S(1)} collective-permute-done((bf16[2,8,8,256]{3,2,1,0:T(8,128)(2,1)S(1)}, bf16[2,8,8,256]{3,2,1,0:T(8,128)(2,1)S(1)}, u32[]{:S(2)}, u32[]{:S(2)}) %collective-permute-start.2) | collective-permute-done | bytes 65568 | tf_op jit(solution)/shard_map/ppermute | solution.py:200
  58.1 7.3 %collective-permute-done.1 = bf16[2,8,8,256]{3,2,1,0:T(8,128)(2,1)S(1)} collective-permute-done((bf16[2,8,8,256]{3,2,1,0:T(8,128)(2,1)S(1)}, bf16[2,8,8,256]{3,2,1,0:T(8,128)(2,1)S(1)}, u32[]{:S(2)}, u32[]{:S(2)}) %collective-permute-start.1) | collective-permute-done | bytes 65568 | tf_op jit(solution)/shard_map/ppermute | solution.py:200
  65.4 5.2 %shard_map.61 = f32[4,1040,128]{2,1,0:T(8,128)} custom-call(s32[8,16]{1,0:T(8,128)S(1)} %copy-done.3, s32[7]{0:T(128)S(1)} %stack.40.ids, bf16[2,16,2,8,8,128]{5,4,3,2,1,0:T(8,128)(2,1)S(1)} %bitcast.23, bf16[2,16,2,8,8,128]{5,4,3,2,1,0:T(8,128)(2,1)S(1)} %bitcast.24, bf16[2,1024,512]{2,1,0:T(8,128)(2,1)} %own.1, ...), custom_call_target="tpu_custom_call" | custom-call | tf_op jit(solution)/shard_map/pallas_call | solution.py:106
  70.6 2.7 %convert_element_type.10 = f16[4,1040,128]{2,1,0:T(8,128)(2,1)} convert(f32[4,1040,128]{2,1,0:T(8,128)} %shard_map.61) | non-fusion elementwise | flops 532480 | bytes 3194880 | tf_op jit(solution)/shard_map/convert_element_type | solution.py:208
  73.4 3.5 %all-to-all-start.2 = ((f16[4,1040,128]{2,1,0:T(8,128)(2,1)}), f16[4,1040,128]{2,1,0:T(8,128)(2,1)S(1)}, u32[]{:S(2)}, u32[]{:S(2)}) async-start(f16[4,1040,128]{2,1,0:T(8,128)(2,1)} %convert_element_type.10), calls=%async_computation.2 | async-start | bytes 2129920 | tf_op jit(solution)/shard_map/all_to_all | solution.py:208
  76.9 5.7 %collective-permute-start.4 = (bf16[2,2,8,8,256]{4,3,2,1,0:T(8,128)(2,1)S(1)}, bf16[2,2,8,8,256]{4,3,2,1,0:T(8,128)(2,1)S(1)}, u32[]{:S(2)}, u32[]{:S(2)}) collective-permute-start(bf16[2,2,8,8,256]{4,3,2,1,0:T(8,128)(2,1)S(1)} %pad_maximum_fusion.5), channel_id=1, source_target_pairs={{0,128},{128,0},{1,129},{129,1},{2,130},{130,2},{3,131},{131,3},{4... | collective-permute-start | bytes 393224 | tf_op jit(solution)/shard_map/ppermute | solution.py:171
  82.6 9.2 %collective-permute-done.4 = bf16[2,2,8,8,256]{4,3,2,1,0:T(8,128)(2,1)S(1)} collective-permute-done((bf16[2,2,8,8,256]{4,3,2,1,0:T(8,128)(2,1)S(1)}, bf16[2,2,8,8,256]{4,3,2,1,0:T(8,128)(2,1)S(1)}, u32[]{:S(2)}, u32[]{:S(2)}) %collective-permute-start.4) | collective-permute-done | bytes 131104 | tf_op jit(solution)/shard_map/ppermute | solution.py:171
  91.8 6.7 %collective-permute-start.5 = (bf16[4,2,8,8,256]{4,3,2,1,0:T(8,128)(2,1)S(1)}, bf16[4,2,8,8,256]{4,3,2,1,0:T(8,128)(2,1)S(1)}, u32[]{:S(2)}, u32[]{:S(2)}) collective-permute-start(bf16[4,2,8,8,256]{4,3,2,1,0:T(8,128)(2,1)S(1)} %pad_maximum_fusion.3), channel_id=1, source_target_pairs={{0,64},{64,0},{1,65},{65,1},{2,66},{66,2},{3,67},{67,3},{4,68},{68... | collective-permute-start | bytes 786440 | tf_op jit(solution)/shard_map/ppermute | solution.py:171
  99.0 0.8 pad_maximum_fusion.2
  99.8 6.1 %all-to-all-start.3 = ((f16[4,272,128]{2,1,0:T(8,128)(2,1)}), f16[4,272,128]{2,1,0:T(8,128)(2,1)S(1)}, u32[]{:S(2)}, u32[]{:S(2)}) async-start(f16[4,272,128]{2,1,0:T(8,128)(2,1)} %pad_maximum_fusion.2), calls=%async_computation.3 | async-start | bytes 557056 | tf_op jit(solution)/shard_map/all_to_all | solution.py:216
  106.0 2.1 %collective-permute-start.6 = (bf16[8,2,8,8,256]{4,3,2,1,0:T(8,128)(2,1)S(1)}, bf16[8,2,8,8,256]{4,3,2,1,0:T(8,128)(2,1)S(1)}, u32[]{:S(2)}, u32[]{:S(2)}) collective-permute-start(bf16[8,2,8,8,256]{4,3,2,1,0:T(8,128)(2,1)S(1)} %pad_maximum_fusion.1), channel_id=1, source_target_pairs={{0,32},{32,0},{1,33},{33,1},{2,34},{34,2},{3,35},{35,3},{4,36},{36... | collective-permute-start | bytes 1572872 | tf_op jit(solution)/shard_map/ppermute | solution.py:171
  108.0 1.7 %collective-permute-done.6 = bf16[8,2,8,8,256]{4,3,2,1,0:T(8,128)(2,1)S(1)} collective-permute-done((bf16[8,2,8,8,256]{4,3,2,1,0:T(8,128)(2,1)S(1)}, bf16[8,2,8,8,256]{4,3,2,1,0:T(8,128)(2,1)S(1)}, u32[]{:S(2)}, u32[]{:S(2)}) %collective-permute-start.6) | collective-permute-done | bytes 524320 | tf_op jit(solution)/shard_map/ppermute | solution.py:171
  109.9 14.5 %all-to-all-done.3 = f16[4,272,128]{2,1,0:T(8,128)(2,1)S(1)} async-done(((f16[4,272,128]{2,1,0:T(8,128)(2,1)}), f16[4,272,128]{2,1,0:T(8,128)(2,1)S(1)}, u32[]{:S(2)}, u32[]{:S(2)}) %all-to-all-start.3) | async-done | bytes 278560 | tf_op jit(solution)/shard_map/all_to_all | solution.py:216
  124.5 1.8 %shard_map.62 = (bf16[2,8,16,128]{3,2,1,0:T(8,128)(2,1)S(1)}, f32[16,16,256]{2,1,0:T(8,128)}) custom-call(s32[7]{0:T(128)S(1)} %stack.40.ids, f32[2,8,16,128]{3,2,1,0:T(8,128)S(1)} %bitcast.25, bf16[16,2,8,8,256]{4,3,2,1,0:T(8,128)(2,1)S(1)} %pad_maximum_fusion.below), custom_call_target="tpu_custom_call" | custom-call | tf_op jit(solution)/shard_map/pallas_call | solution.py:139
  126.3 6.4 %all-to-all-start.4 = ((f32[16,16,256]{2,1,0:T(8,128)}), f32[16,16,256]{2,1,0:T(8,128)S(1)}, u32[]{:S(2)}, u32[]{:S(2)}) async-start(f32[16,16,256]{2,1,0:T(8,128)} %get-tuple-element.19), calls=%async_computation.4 | async-start | bytes 524288 | tf_op jit(solution)/shard_map/all_to_all | solution.py:220
  132.7 2.0 %collective-permute-start.8 = (bf16[2,8,16,128]{3,2,1,0:T(8,128)(2,1)S(1)}, bf16[2,8,16,128]{3,2,1,0:T(8,128)(2,1)S(1)}, u32[]{:S(2)}, u32[]{:S(2)}) collective-permute-start(bf16[2,8,16,128]{3,2,1,0:T(8,128)(2,1)S(1)} %get-tuple-element.18), channel_id=1, source_target_pairs={{0,1},{1,0},{2,3},{3,2},{4,5},{5,4},{6,7},{7,6},{8,9},{9,8},{10,11... | collective-permute-start | bytes 196616 | tf_op jit(solution)/shard_map/ppermute | solution.py:221
  134.8 5.9 %all-to-all-done.4 = f32[16,16,256]{2,1,0:T(8,128)S(1)} async-done(((f32[16,16,256]{2,1,0:T(8,128)}), f32[16,16,256]{2,1,0:T(8,128)S(1)}, u32[]{:S(2)}, u32[]{:S(2)}) %all-to-all-start.4) | async-done | bytes 262176 | tf_op jit(solution)/shard_map/all_to_all | solution.py:220
  140.7 7.5 %collective-permute-start.7 = (f32[16,256]{1,0:T(8,128)S(1)}, f32[16,256]{1,0:T(8,128)S(1)}, u32[]{:S(2)}, u32[]{:S(2)}) collective-permute-start(f32[16,256]{1,0:T(8,128)S(1)} %reduce_sum.29.part), channel_id=1, source_target_pairs={{0,16},{16,0},{1,17},{17,1},{2,18},{18,2},{3,19},{19,3},{4,20},{20... | collective-permute-start | bytes 49160 | tf_op jit(solution)/shard_map/ppermute | solution.py:223
  148.4 6.6 %collective-permute-done.7.other = f32[16,256]{1,0:T(8,128)S(1)} collective-permute-done((f32[16,256]{1,0:T(8,128)S(1)}, f32[16,256]{1,0:T(8,128)S(1)}, u32[]{:S(2)}, u32[]{:S(2)}) %collective-permute-start.7) | collective-permute-done | bytes 16416 | tf_op jit(solution)/shard_map/ppermute | solution.py:223
  155.0 0.7 shard_map.63
  155.8 4.9 %all-to-all-start.5 = ((f32[16,16,256]{2,1,0:T(8,128)}), f32[16,16,256]{2,1,0:T(8,128)S(1)}, u32[]{:S(2)}, u32[]{:S(2)}) async-start(f32[16,16,256]{2,1,0:T(8,128)} %shard_map.63), calls=%async_computation.5 | async-start | bytes 524288 | tf_op jit(solution)/shard_map/all_to_all | solution.py:227
  161.5 6.6 %all-to-all-done.5 = f32[16,16,256]{2,1,0:T(8,128)S(1)} async-done(((f32[16,16,256]{2,1,0:T(8,128)}), f32[16,16,256]{2,1,0:T(8,128)S(1)}, u32[]{:S(2)}, u32[]{:S(2)}) %all-to-all-start.5) | async-done | bytes 262176 | tf_op jit(solution)/shard_map/all_to_all | solution.py:227
  (35 shorter events, 2.6 us)
Async XLA Ops:
  0.6 147.6 %copy-start = (f32[2,8,16,256]{3,2,1,0:T(8,128)S(1)}, f32[2,8,16,256]{3,2,1,0:T(8,128)}, u32[]{:S(2)}) copy-start(f32[2,8,16,256]{3,2,1,0:T(8,128)} %param.6) | copy-start | bytes 786436
  0.6 0.9 copy-start.1
  1.5 10.8 %copy-start.2 = (bf16[2,8,1,8,256]{4,3,2,1,0:T(8,128)(2,1)S(1)}, bf16[2,8,1,8,256]{4,3,2,1,0:T(8,128)(2,1)}, u32[]{:S(2)}) copy-start(bf16[2,8,1,8,256]{4,3,2,1,0:T(8,128)(2,1)} %param.5) | copy-start | bytes 196612
  2.8 26.1 %all-to-all-start = ((bf16[32,2,8,8,128]{4,3,2,1,0:T(8,128)(2,1)}), bf16[32,2,8,8,128]{4,3,2,1,0:T(8,128)(2,1)S(1)}, u32[]{:S(2)}, u32[]{:S(2)}) async-start(bf16[32,2,8,8,128]{4,3,2,1,0:T(8,128)(2,1)} %bitcast.8), calls=%async_computation | async-start | bytes 2097152 | tf_op jit(solution)/shard_map/all_to_all | solution.py:185
  12.3 53.1 %copy-start.3 = (s32[8,16]{1,0:T(8,128)S(1)}, s32[8,16]{1,0:T(8,128)}, u32[]{:S(2)}) copy-start(s32[8,16]{1,0:T(8,128)} %st.1) | copy-start | bytes 1540
  12.4 16.6 %collective-permute-start = (bf16[2,8,8,256]{3,2,1,0:T(8,128)(2,1)S(1)}, bf16[2,8,8,256]{3,2,1,0:T(8,128)(2,1)S(1)}, u32[]{:S(2)}, u32[]{:S(2)}) collective-permute-start(bf16[2,8,8,256]{3,2,1,0:T(8,128)(2,1)S(1)} %bitcast.27), channel_id=1, source_target_pairs={{0,16},{16,0},{1,17},{17,1},{2,18},{18,2},{3,19},{19,3},{4,20},{20... | collective-permute-start | bytes 196616 | tf_op jit(solution)/shard_map/ppermute | solution.py:183
  28.9 36.5 %collective-permute-start.3 = (bf16[2,1024,512]{2,1,0:T(8,128)(2,1)}, bf16[2,1024,512]{2,1,0:T(8,128)(2,1)}, u32[]{:S(2)}, u32[]{:S(2)}) collective-permute-start(bf16[2,1024,512]{2,1,0:T(8,128)(2,1)} %own.1), channel_id=1, source_target_pairs={{0,32},{32,0},{1,33},{33,1},{2,34},{34,2},{3,35},{35,3},{4,36},{36... | collective-permute-start | bytes 6291464 | tf_op jit(solution)/shard_map/ppermute | solution.py:188
  32.1 33.3 %all-to-all-start.1 = ((bf16[32,2,8,8,128]{4,3,2,1,0:T(8,128)(2,1)}), bf16[32,2,8,8,128]{4,3,2,1,0:T(8,128)(2,1)S(1)}, u32[]{:S(2)}, u32[]{:S(2)}) async-start(bf16[32,2,8,8,128]{4,3,2,1,0:T(8,128)(2,1)} %bitcast.12), calls=%async_computation.1 | async-start | bytes 2097152 | tf_op jit(solution)/shard_map/all_to_all | solution.py:190
  39.6 18.4 %collective-permute-start.2 = (bf16[2,8,8,256]{3,2,1,0:T(8,128)(2,1)S(1)}, bf16[2,8,8,256]{3,2,1,0:T(8,128)(2,1)S(1)}, u32[]{:S(2)}, u32[]{:S(2)}) collective-permute-start(bf16[2,8,8,256]{3,2,1,0:T(8,128)(2,1)S(1)} %bitcast.28), channel_id=1, source_target_pairs={{0,256},{1,288},{2,320},{3,352},{4,384},{5,416},{6,448},{7,480},{8... | collective-permute-start | bytes 196616 | tf_op jit(solution)/shard_map/ppermute | solution.py:200
  47.6 17.8 %collective-permute-start.1 = (bf16[2,8,8,256]{3,2,1,0:T(8,128)(2,1)S(1)}, bf16[2,8,8,256]{3,2,1,0:T(8,128)(2,1)S(1)}, u32[]{:S(2)}, u32[]{:S(2)}) collective-permute-start(bf16[2,8,8,256]{3,2,1,0:T(8,128)(2,1)S(1)} %bitcast.29), channel_id=1, source_target_pairs={{0,0},{1,32},{2,64},{3,96},{4,128},{5,160},{6,192},{7,224},{8,256}... | collective-permute-start | bytes 196616 | tf_op jit(solution)/shard_map/ppermute | solution.py:200
  73.4 25.2 %all-to-all-start.2 = ((f16[4,1040,128]{2,1,0:T(8,128)(2,1)}), f16[4,1040,128]{2,1,0:T(8,128)(2,1)S(1)}, u32[]{:S(2)}, u32[]{:S(2)}) async-start(f16[4,1040,128]{2,1,0:T(8,128)(2,1)} %convert_element_type.10), calls=%async_computation.2 | async-start | bytes 2129920 | tf_op jit(solution)/shard_map/all_to_all | solution.py:208
  76.9 14.9 %collective-permute-start.4 = (bf16[2,2,8,8,256]{4,3,2,1,0:T(8,128)(2,1)S(1)}, bf16[2,2,8,8,256]{4,3,2,1,0:T(8,128)(2,1)S(1)}, u32[]{:S(2)}, u32[]{:S(2)}) collective-permute-start(bf16[2,2,8,8,256]{4,3,2,1,0:T(8,128)(2,1)S(1)} %pad_maximum_fusion.5), channel_id=1, source_target_pairs={{0,128},{128,0},{1,129},{129,1},{2,130},{130,2},{3,131},{131,3},{4... | collective-permute-start | bytes 393224 | tf_op jit(solution)/shard_map/ppermute | solution.py:171
  91.8 14.1 %collective-permute-start.5 = (bf16[4,2,8,8,256]{4,3,2,1,0:T(8,128)(2,1)S(1)}, bf16[4,2,8,8,256]{4,3,2,1,0:T(8,128)(2,1)S(1)}, u32[]{:S(2)}, u32[]{:S(2)}) collective-permute-start(bf16[4,2,8,8,256]{4,3,2,1,0:T(8,128)(2,1)S(1)} %pad_maximum_fusion.3), channel_id=1, source_target_pairs={{0,64},{64,0},{1,65},{65,1},{2,66},{66,2},{3,67},{67,3},{4,68},{68... | collective-permute-start | bytes 786440 | tf_op jit(solution)/shard_map/ppermute | solution.py:171
  99.8 24.7 %all-to-all-start.3 = ((f16[4,272,128]{2,1,0:T(8,128)(2,1)}), f16[4,272,128]{2,1,0:T(8,128)(2,1)S(1)}, u32[]{:S(2)}, u32[]{:S(2)}) async-start(f16[4,272,128]{2,1,0:T(8,128)(2,1)} %pad_maximum_fusion.2), calls=%async_computation.3 | async-start | bytes 557056 | tf_op jit(solution)/shard_map/all_to_all | solution.py:216
  106.0 3.8 %collective-permute-start.6 = (bf16[8,2,8,8,256]{4,3,2,1,0:T(8,128)(2,1)S(1)}, bf16[8,2,8,8,256]{4,3,2,1,0:T(8,128)(2,1)S(1)}, u32[]{:S(2)}, u32[]{:S(2)}) collective-permute-start(bf16[8,2,8,8,256]{4,3,2,1,0:T(8,128)(2,1)S(1)} %pad_maximum_fusion.1), channel_id=1, source_target_pairs={{0,32},{32,0},{1,33},{33,1},{2,34},{34,2},{3,35},{35,3},{4,36},{36... | collective-permute-start | bytes 1572872 | tf_op jit(solution)/shard_map/ppermute | solution.py:171
  126.3 14.4 %all-to-all-start.4 = ((f32[16,16,256]{2,1,0:T(8,128)}), f32[16,16,256]{2,1,0:T(8,128)S(1)}, u32[]{:S(2)}, u32[]{:S(2)}) async-start(f32[16,16,256]{2,1,0:T(8,128)} %get-tuple-element.19), calls=%async_computation.4 | async-start | bytes 524288 | tf_op jit(solution)/shard_map/all_to_all | solution.py:220
  132.7 15.7 %collective-permute-start.8 = (bf16[2,8,16,128]{3,2,1,0:T(8,128)(2,1)S(1)}, bf16[2,8,16,128]{3,2,1,0:T(8,128)(2,1)S(1)}, u32[]{:S(2)}, u32[]{:S(2)}) collective-permute-start(bf16[2,8,16,128]{3,2,1,0:T(8,128)(2,1)S(1)} %get-tuple-element.18), channel_id=1, source_target_pairs={{0,1},{1,0},{2,3},{3,2},{4,5},{5,4},{6,7},{7,6},{8,9},{9,8},{10,11... | collective-permute-start | bytes 196616 | tf_op jit(solution)/shard_map/ppermute | solution.py:221
  140.7 14.3 %collective-permute-start.7 = (f32[16,256]{1,0:T(8,128)S(1)}, f32[16,256]{1,0:T(8,128)S(1)}, u32[]{:S(2)}, u32[]{:S(2)}) collective-permute-start(f32[16,256]{1,0:T(8,128)S(1)} %reduce_sum.29.part), channel_id=1, source_target_pairs={{0,16},{16,0},{1,17},{17,1},{2,18},{18,2},{3,19},{19,3},{4,20},{20... | collective-permute-start | bytes 49160 | tf_op jit(solution)/shard_map/ppermute | solution.py:223
  155.8 12.3 %all-to-all-start.5 = ((f32[16,16,256]{2,1,0:T(8,128)}), f32[16,16,256]{2,1,0:T(8,128)S(1)}, u32[]{:S(2)}, u32[]{:S(2)}) async-start(f32[16,16,256]{2,1,0:T(8,128)} %shard_map.63), calls=%async_computation.5 | async-start | bytes 524288 | tf_op jit(solution)/shard_map/all_to_all | solution.py:227

commit v9 on v8

--- a/solution.py
+++ b/solution.py
@@ -203,7 +203,6 @@
     near = near.reshape(2, 16, 2, 8, 8, 128)
     far = far.reshape(2, 16, 2, 8, 8, 128)
     parts = products(structure, ids, near, far, inverse_anc, sib)
-    below, parts = tie((below, parts))
     below = doubled(below, "zb")
     got = lax.all_to_all(parts.astype(F16), ("zc", "h"), 0, 0, tiled=True).astype(F32)
     power = got[:, 1024:1025]

time: 170 us -> 182 us (1.071)
  waiting for transfers between devices: 59.9 us -> 73.9 us
    all_to_all x2, waiting for transfers between devices: 0.01 us -> 15.2 us  [shards(): lax.all_to_all(lanes.reshape(32, 2, 8, 8, 128), group, 0, 0, tiled=True)]
    ppermute x3, starting transfers between devices: 14.5 us -> 5.76 us  [doubled(): return jnp.concatenate([value, lax.ppermute(value, axis, PAIR)], axis=0)]
    ppermute x2, starting transfers between devices: 13 us -> 18.2 us  [shards(): below.append(lax.ppermute(own, ROW + COL, moves))]
    all_to_all x1, starting transfers between devices: 6.43 us -> 9.9 us  [shards(): terms = lax.all_to_all(terms, PLANE, 0, 0, tiled=True)]
    all_to_all x1, waiting for transfers between devices: 14.5 us -> 11.2 us  [shards(): got = lax.all_to_all(parts, ('za', 'zb'), 0, 0, tiled=True).astype(F32)]
    all_to_all x1, starting transfers between devices: 3.51 us -> 6.22 us  [shards(): lax.all_to_all(parts.astype(F16), ('zc', 'h'), 0, 0, tiled=True).astype(F32)]
    all_to_all x1, starting transfers between devices: 6.15 us -> 3.45 us  [shards(): got = lax.all_to_all(parts, ('za', 'zb'), 0, 0, tiled=True).astype(F32)]
  transfers between devices with their start and end apart: 15 -> 15, of which waited for: 9 -> 11; matrix products, arithmetic and copies ran while one was open for 1% -> 1% of each run, Pallas kernels for 1% -> 1%
where the time goes in v9:
time: 182 us; the launch traced here: 181 us
  starting transfers between devices  89.1 us (49%)
  waiting for transfers between devices  73.9 us (41%)
  Pallas kernels  10.4 us (6%)
  other arithmetic  5.1 us (3%)
    ppermute x2, starting transfers between devices, shards(): below.append(lax.ppermute(own, ROW + COL, moves))  18.2 us
    all_to_all x2, starting transfers between devices, shards(): lax.all_to_all(lanes.reshape(32, 2, 8, 8, 128), group, 0, 0, tiled=True)  17 us
    all_to_all x2, waiting for transfers between devices, shards(): lax.all_to_all(lanes.reshape(32, 2, 8, 8, 128), group, 0, 0, tiled=True)  15.2 us
    ppermute x1, starting transfers between devices, shards(): other = lax.ppermute(own, 'zh', PAIR)  13.9 us
    ppermute x2, waiting for transfers between devices, shards(): below.append(lax.ppermute(own, ROW + COL, moves))  13.3 us
    all_to_all x1, waiting for transfers between devices, shards(): got = lax.all_to_all(parts, ('za', 'zb'), 0, 0, tiled=True).astype(F32)  11.2 us
    ppermute x3, waiting for transfers between devices, doubled(): return jnp.concatenate([value, lax.ppermute(value, axis, PAIR)], axis=0)  11.1 us
    all_to_all x1, starting transfers between devices, shards(): terms = lax.all_to_all(terms, PLANE, 0, 0, tiled=True)  9.9 us
  transfers between devices with their start and end apart: 15, of which 11 were waited for; matrix products, arithmetic and copies ran while one was open for 1% of the time, Pallas kernels for 1%

profile of v9, /device:TPU:2, one launch (start us, length us, event | category | flops | bytes accessed | tf_op | source)
XLA Modules:
  0.0 181.2 jit_solution(15978335465438628823)
XLA Ops:
  0.7 0.9 copy-done.1
  1.5 1.3 shard_map.59
  2.8 9.5 %all-to-all-start = ((bf16[32,2,8,8,128]{4,3,2,1,0:T(8,128)(2,1)}), bf16[32,2,8,8,128]{4,3,2,1,0:T(8,128)(2,1)S(1)}, u32[]{:S(2)}, u32[]{:S(2)}) async-start(bf16[32,2,8,8,128]{4,3,2,1,0:T(8,128)(2,1)} %bitcast.8), calls=%async_computation | async-start | bytes 2097152 | tf_op jit(solution)/shard_map/all_to_all | solution.py:185
  12.4 13.9 %collective-permute-start = (bf16[2,8,8,256]{3,2,1,0:T(8,128)(2,1)S(1)}, bf16[2,8,8,256]{3,2,1,0:T(8,128)(2,1)S(1)}, u32[]{:S(2)}, u32[]{:S(2)}) collective-permute-start(bf16[2,8,8,256]{3,2,1,0:T(8,128)(2,1)S(1)} %bitcast.29), channel_id=1, source_target_pairs={{0,16},{16,0},{1,17},{17,1},{2,18},{18,2},{3,19},{19,3},{4,20},{20... | collective-permute-start | bytes 196616 | tf_op jit(solution)/shard_map/ppermute | solution.py:183
  26.2 2.7 %collective-permute-done.panel = bf16[2,8,8,256]{3,2,1,0:T(8,128)(2,1)S(1)} collective-permute-done((bf16[2,8,8,256]{3,2,1,0:T(8,128)(2,1)S(1)}, bf16[2,8,8,256]{3,2,1,0:T(8,128)(2,1)S(1)}, u32[]{:S(2)}, u32[]{:S(2)}) %collective-permute-start) | collective-permute-done | bytes 65568 | tf_op jit(solution)/shard_map/ppermute | solution.py:183
  28.9 1.9 %collective-permute-start.1 = (bf16[2,1024,512]{2,1,0:T(8,128)(2,1)}, bf16[2,1024,512]{2,1,0:T(8,128)(2,1)}, u32[]{:S(2)}, u32[]{:S(2)}) collective-permute-start(bf16[2,1024,512]{2,1,0:T(8,128)(2,1)} %own.1), channel_id=1, source_target_pairs={{0,32},{32,0},{1,33},{33,1},{2,34},{34,2},{3,35},{35,3},{4,36},{36... | collective-permute-start | bytes 6291464 | tf_op jit(solution)/shard_map/ppermute | solution.py:188
  30.8 1.3 shard_map.60
  32.1 7.5 %all-to-all-start.1 = ((bf16[32,2,8,8,128]{4,3,2,1,0:T(8,128)(2,1)}), bf16[32,2,8,8,128]{4,3,2,1,0:T(8,128)(2,1)S(1)}, u32[]{:S(2)}, u32[]{:S(2)}) async-start(bf16[32,2,8,8,128]{4,3,2,1,0:T(8,128)(2,1)} %bitcast.10), calls=%async_computation.1 | async-start | bytes 2097152 | tf_op jit(solution)/shard_map/all_to_all | solution.py:190
  39.8 15.2 %all-to-all-done.1 = bf16[32,2,8,8,128]{4,3,2,1,0:T(8,128)(2,1)S(1)} async-done(((bf16[32,2,8,8,128]{4,3,2,1,0:T(8,128)(2,1)}), bf16[32,2,8,8,128]{4,3,2,1,0:T(8,128)(2,1)S(1)}, u32[]{:S(2)}, u32[]{:S(2)}) %all-to-all-start.1) | async-done | bytes 1048608 | tf_op jit(solution)/shard_map/all_to_all | solution.py:190
  55.0 5.2 %shard_map.61 = f32[4,1040,128]{2,1,0:T(8,128)} custom-call(s32[8,16]{1,0:T(8,128)S(1)} %copy-done.3, s32[7]{0:T(128)S(1)} %stack.40.ids, bf16[2,16,2,8,8,128]{5,4,3,2,1,0:T(8,128)(2,1)S(1)} %bitcast.25, bf16[2,16,2,8,8,128]{5,4,3,2,1,0:T(8,128)(2,1)S(1)} %bitcast.26, bf16[2,1024,512]{2,1,0:T(8,128)(2,1)} %own.1, ...), custom_call_target="tpu_custom_call" | custom-call | tf_op jit(solution)/shard_map/pallas_call | solution.py:106
  60.2 2.7 %convert_element_type.10 = f16[4,1040,128]{2,1,0:T(8,128)(2,1)} convert(f32[4,1040,128]{2,1,0:T(8,128)} %shard_map.61) | non-fusion elementwise | flops 532480 | bytes 3194880 | tf_op jit(solution)/shard_map/convert_element_type | solution.py:207
  62.9 6.2 %all-to-all-start.2 = ((f16[4,1040,128]{2,1,0:T(8,128)(2,1)}), f16[4,1040,128]{2,1,0:T(8,128)(2,1)S(1)}, u32[]{:S(2)}, u32[]{:S(2)}) async-start(f16[4,1040,128]{2,1,0:T(8,128)(2,1)} %convert_element_type.10), calls=%async_computation.2 | async-start | bytes 2129920 | tf_op jit(solution)/shard_map/all_to_all | solution.py:207
  69.1 1.9 %collective-permute-start.2 = (bf16[2,8,8,256]{3,2,1,0:T(8,128)(2,1)S(1)}, bf16[2,8,8,256]{3,2,1,0:T(8,128)(2,1)S(1)}, u32[]{:S(2)}, u32[]{:S(2)}) collective-permute-start(bf16[2,8,8,256]{3,2,1,0:T(8,128)(2,1)S(1)} %bitcast.30), channel_id=1, source_target_pairs={{0,0},{1,32},{2,64},{3,96},{4,128},{5,160},{6,192},{7,224},{8,256}... | collective-permute-start | bytes 196616 | tf_op jit(solution)/shard_map/ppermute | solution.py:200
  71.1 16.3 %collective-permute-start.3 = (bf16[2,8,8,256]{3,2,1,0:T(8,128)(2,1)S(1)}, bf16[2,8,8,256]{3,2,1,0:T(8,128)(2,1)S(1)}, u32[]{:S(2)}, u32[]{:S(2)}) collective-permute-start(bf16[2,8,8,256]{3,2,1,0:T(8,128)(2,1)S(1)} %bitcast.31), channel_id=1, source_target_pairs={{0,256},{1,288},{2,320},{3,352},{4,384},{5,416},{6,448},{7,480},{8... | collective-permute-start | bytes 196616 | tf_op jit(solution)/shard_map/ppermute | solution.py:200
  87.4 7.1 %collective-permute-done.2 = bf16[2,8,8,256]{3,2,1,0:T(8,128)(2,1)S(1)} collective-permute-done((bf16[2,8,8,256]{3,2,1,0:T(8,128)(2,1)S(1)}, bf16[2,8,8,256]{3,2,1,0:T(8,128)(2,1)S(1)}, u32[]{:S(2)}, u32[]{:S(2)}) %collective-permute-start.2) | collective-permute-done | bytes 65568 | tf_op jit(solution)/shard_map/ppermute | solution.py:200
  94.5 6.2 %collective-permute-done.3 = bf16[2,8,8,256]{3,2,1,0:T(8,128)(2,1)S(1)} collective-permute-done((bf16[2,8,8,256]{3,2,1,0:T(8,128)(2,1)S(1)}, bf16[2,8,8,256]{3,2,1,0:T(8,128)(2,1)S(1)}, u32[]{:S(2)}, u32[]{:S(2)}) %collective-permute-start.3) | collective-permute-done | bytes 65568 | tf_op jit(solution)/shard_map/ppermute | solution.py:200
  100.8 1.9 %collective-permute-start.4 = (bf16[2,2,8,8,256]{4,3,2,1,0:T(8,128)(2,1)S(1)}, bf16[2,2,8,8,256]{4,3,2,1,0:T(8,128)(2,1)S(1)}, u32[]{:S(2)}, u32[]{:S(2)}) collective-permute-start(bf16[2,2,8,8,256]{4,3,2,1,0:T(8,128)(2,1)S(1)} %pad_maximum_fusion.4), channel_id=1, source_target_pairs={{0,128},{128,0},{1,129},{129,1},{2,130},{130,2},{3,131},{131,3},{4... | collective-permute-start | bytes 393224 | tf_op jit(solution)/shard_map/ppermute | solution.py:171
  102.7 6.4 %collective-permute-done.4 = bf16[2,2,8,8,256]{4,3,2,1,0:T(8,128)(2,1)S(1)} collective-permute-done((bf16[2,2,8,8,256]{4,3,2,1,0:T(8,128)(2,1)S(1)}, bf16[2,2,8,8,256]{4,3,2,1,0:T(8,128)(2,1)S(1)}, u32[]{:S(2)}, u32[]{:S(2)}) %collective-permute-start.4) | collective-permute-done | bytes 131104 | tf_op jit(solution)/shard_map/ppermute | solution.py:171
  109.2 1.9 %collective-permute-start.5 = (bf16[4,2,8,8,256]{4,3,2,1,0:T(8,128)(2,1)S(1)}, bf16[4,2,8,8,256]{4,3,2,1,0:T(8,128)(2,1)S(1)}, u32[]{:S(2)}, u32[]{:S(2)}) collective-permute-start(bf16[4,2,8,8,256]{4,3,2,1,0:T(8,128)(2,1)S(1)} %pad_maximum_fusion.2), channel_id=1, source_target_pairs={{0,64},{64,0},{1,65},{65,1},{2,66},{66,2},{3,67},{67,3},{4,68},{68... | collective-permute-start | bytes 786440 | tf_op jit(solution)/shard_map/ppermute | solution.py:171
  112.3 3.4 %all-to-all-start.3 = ((f16[4,272,128]{2,1,0:T(8,128)(2,1)}), f16[4,272,128]{2,1,0:T(8,128)(2,1)S(1)}, u32[]{:S(2)}, u32[]{:S(2)}) async-start(f16[4,272,128]{2,1,0:T(8,128)(2,1)} %pad_maximum_fusion.1), calls=%async_computation.3 | async-start | bytes 557056 | tf_op jit(solution)/shard_map/all_to_all | solution.py:215
  115.7 2.9 %collective-permute-done.5 = bf16[4,2,8,8,256]{4,3,2,1,0:T(8,128)(2,1)S(1)} collective-permute-done((bf16[4,2,8,8,256]{4,3,2,1,0:T(8,128)(2,1)S(1)}, bf16[4,2,8,8,256]{4,3,2,1,0:T(8,128)(2,1)S(1)}, u32[]{:S(2)}, u32[]{:S(2)}) %collective-permute-start.5) | collective-permute-done | bytes 262176 | tf_op jit(solution)/shard_map/ppermute | solution.py:171
  118.7 1.9 %collective-permute-start.6 = (bf16[8,2,8,8,256]{4,3,2,1,0:T(8,128)(2,1)S(1)}, bf16[8,2,8,8,256]{4,3,2,1,0:T(8,128)(2,1)S(1)}, u32[]{:S(2)}, u32[]{:S(2)}) collective-permute-start(bf16[8,2,8,8,256]{4,3,2,1,0:T(8,128)(2,1)S(1)} %pad_maximum_fusion), channel_id=1, source_target_pairs={{0,32},{32,0},{1,33},{33,1},{2,34},{34,2},{3,35},{35,3},{4,36},{36... | collective-permute-start | bytes 1572872 | tf_op jit(solution)/shard_map/ppermute | solution.py:171
  120.7 1.8 collective-permute-done.6
  122.5 11.2 %all-to-all-done.3 = f16[4,272,128]{2,1,0:T(8,128)(2,1)S(1)} async-done(((f16[4,272,128]{2,1,0:T(8,128)(2,1)}), f16[4,272,128]{2,1,0:T(8,128)(2,1)S(1)}, u32[]{:S(2)}, u32[]{:S(2)}) %all-to-all-start.3) | async-done | bytes 278560 | tf_op jit(solution)/shard_map/all_to_all | solution.py:215
  133.8 1.8 shard_map.62
  135.6 9.9 %all-to-all-start.4 = ((f32[16,16,256]{2,1,0:T(8,128)}), f32[16,16,256]{2,1,0:T(8,128)S(1)}, u32[]{:S(2)}, u32[]{:S(2)}) async-start(f32[16,16,256]{2,1,0:T(8,128)} %get-tuple-element.15), calls=%async_computation.4 | async-start | bytes 524288 | tf_op jit(solution)/shard_map/all_to_all | solution.py:219
  145.5 2.0 %collective-permute-start.8 = (bf16[2,8,16,128]{3,2,1,0:T(8,128)(2,1)S(1)}, bf16[2,8,16,128]{3,2,1,0:T(8,128)(2,1)S(1)}, u32[]{:S(2)}, u32[]{:S(2)}) collective-permute-start(bf16[2,8,16,128]{3,2,1,0:T(8,128)(2,1)S(1)} %get-tuple-element.14), channel_id=1, source_target_pairs={{0,1},{1,0},{2,3},{3,2},{4,5},{5,4},{6,7},{7,6},{8,9},{9,8},{10,11... | collective-permute-start | bytes 196616 | tf_op jit(solution)/shard_map/ppermute | solution.py:220
  147.5 6.0 %all-to-all-done.4 = f32[16,16,256]{2,1,0:T(8,128)S(1)} async-done(((f32[16,16,256]{2,1,0:T(8,128)}), f32[16,16,256]{2,1,0:T(8,128)S(1)}, u32[]{:S(2)}, u32[]{:S(2)}) %all-to-all-start.4) | async-done | bytes 262176 | tf_op jit(solution)/shard_map/all_to_all | solution.py:219
  153.6 6.3 %collective-permute-start.7 = (f32[16,256]{1,0:T(8,128)S(1)}, f32[16,256]{1,0:T(8,128)S(1)}, u32[]{:S(2)}, u32[]{:S(2)}) collective-permute-start(f32[16,256]{1,0:T(8,128)S(1)} %reduce_sum.29.part), channel_id=1, source_target_pairs={{0,16},{16,0},{1,17},{17,1},{2,18},{18,2},{3,19},{19,3},{4,20},{20... | collective-permute-start | bytes 49160 | tf_op jit(solution)/shard_map/ppermute | solution.py:222
  160.2 7.8 %collective-permute-done.7.other = f32[16,256]{1,0:T(8,128)S(1)} collective-permute-done((f32[16,256]{1,0:T(8,128)S(1)}, f32[16,256]{1,0:T(8,128)S(1)}, u32[]{:S(2)}, u32[]{:S(2)}) %collective-permute-start.7) | collective-permute-done | bytes 16416 | tf_op jit(solution)/shard_map/ppermute | solution.py:222
  168.7 4.4 %all-to-all-start.5 = ((f32[16,16,256]{2,1,0:T(8,128)}), f32[16,16,256]{2,1,0:T(8,128)S(1)}, u32[]{:S(2)}, u32[]{:S(2)}) async-start(f32[16,16,256]{2,1,0:T(8,128)} %shard_map.63), calls=%async_computation.5 | async-start | bytes 524288 | tf_op jit(solution)/shard_map/all_to_all | solution.py:226
  173.9 6.6 %all-to-all-done.5 = f32[16,16,256]{2,1,0:T(8,128)S(1)} async-done(((f32[16,16,256]{2,1,0:T(8,128)}), f32[16,16,256]{2,1,0:T(8,128)S(1)}, u32[]{:S(2)}, u32[]{:S(2)}) %all-to-all-start.5) | async-done | bytes 262176 | tf_op jit(solution)/shard_map/all_to_all | solution.py:226
  (39 shorter events, 4.0 us)
Async XLA Ops:
  0.6 159.3 %copy-start = (f32[2,8,16,256]{3,2,1,0:T(8,128)S(1)}, f32[2,8,16,256]{3,2,1,0:T(8,128)}, u32[]{:S(2)}) copy-start(f32[2,8,16,256]{3,2,1,0:T(8,128)} %param.6) | copy-start | bytes 786436
  0.6 0.9 copy-start.1
  1.5 10.8 %copy-start.2 = (bf16[2,8,1,8,256]{4,3,2,1,0:T(8,128)(2,1)S(1)}, bf16[2,8,1,8,256]{4,3,2,1,0:T(8,128)(2,1)}, u32[]{:S(2)}) copy-start(bf16[2,8,1,8,256]{4,3,2,1,0:T(8,128)(2,1)} %param.5) | copy-start | bytes 196612
  2.8 26.1 %all-to-all-start = ((bf16[32,2,8,8,128]{4,3,2,1,0:T(8,128)(2,1)}), bf16[32,2,8,8,128]{4,3,2,1,0:T(8,128)(2,1)S(1)}, u32[]{:S(2)}, u32[]{:S(2)}) async-start(bf16[32,2,8,8,128]{4,3,2,1,0:T(8,128)(2,1)} %bitcast.8), calls=%async_computation | async-start | bytes 2097152 | tf_op jit(solution)/shard_map/all_to_all | solution.py:185
  12.3 42.6 %copy-start.3 = (s32[8,16]{1,0:T(8,128)S(1)}, s32[8,16]{1,0:T(8,128)}, u32[]{:S(2)}) copy-start(s32[8,16]{1,0:T(8,128)} %st.1) | copy-start | bytes 1540
  12.4 16.6 %collective-permute-start = (bf16[2,8,8,256]{3,2,1,0:T(8,128)(2,1)S(1)}, bf16[2,8,8,256]{3,2,1,0:T(8,128)(2,1)S(1)}, u32[]{:S(2)}, u32[]{:S(2)}) collective-permute-start(bf16[2,8,8,256]{3,2,1,0:T(8,128)(2,1)S(1)} %bitcast.29), channel_id=1, source_target_pairs={{0,16},{16,0},{1,17},{17,1},{2,18},{18,2},{3,19},{19,3},{4,20},{20... | collective-permute-start | bytes 196616 | tf_op jit(solution)/shard_map/ppermute | solution.py:183
  28.9 26.1 %collective-permute-start.1 = (bf16[2,1024,512]{2,1,0:T(8,128)(2,1)}, bf16[2,1024,512]{2,1,0:T(8,128)(2,1)}, u32[]{:S(2)}, u32[]{:S(2)}) collective-permute-start(bf16[2,1024,512]{2,1,0:T(8,128)(2,1)} %own.1), channel_id=1, source_target_pairs={{0,32},{32,0},{1,33},{33,1},{2,34},{34,2},{3,35},{35,3},{4,36},{36... | collective-permute-start | bytes 6291464 | tf_op jit(solution)/shard_map/ppermute | solution.py:188
  32.1 22.8 %all-to-all-start.1 = ((bf16[32,2,8,8,128]{4,3,2,1,0:T(8,128)(2,1)}), bf16[32,2,8,8,128]{4,3,2,1,0:T(8,128)(2,1)S(1)}, u32[]{:S(2)}, u32[]{:S(2)}) async-start(bf16[32,2,8,8,128]{4,3,2,1,0:T(8,128)(2,1)} %bitcast.10), calls=%async_computation.1 | async-start | bytes 2097152 | tf_op jit(solution)/shard_map/all_to_all | solution.py:190
  62.9 48.2 %all-to-all-start.2 = ((f16[4,1040,128]{2,1,0:T(8,128)(2,1)}), f16[4,1040,128]{2,1,0:T(8,128)(2,1)S(1)}, u32[]{:S(2)}, u32[]{:S(2)}) async-start(f16[4,1040,128]{2,1,0:T(8,128)(2,1)} %convert_element_type.10), calls=%async_computation.2 | async-start | bytes 2129920 | tf_op jit(solution)/shard_map/all_to_all | solution.py:207
  69.1 25.4 %collective-permute-start.2 = (bf16[2,8,8,256]{3,2,1,0:T(8,128)(2,1)S(1)}, bf16[2,8,8,256]{3,2,1,0:T(8,128)(2,1)S(1)}, u32[]{:S(2)}, u32[]{:S(2)}) collective-permute-start(bf16[2,8,8,256]{3,2,1,0:T(8,128)(2,1)S(1)} %bitcast.30), channel_id=1, source_target_pairs={{0,0},{1,32},{2,64},{3,96},{4,128},{5,160},{6,192},{7,224},{8,256}... | collective-permute-start | bytes 196616 | tf_op jit(solution)/shard_map/ppermute | solution.py:200
  71.1 29.7 %collective-permute-start.3 = (bf16[2,8,8,256]{3,2,1,0:T(8,128)(2,1)S(1)}, bf16[2,8,8,256]{3,2,1,0:T(8,128)(2,1)S(1)}, u32[]{:S(2)}, u32[]{:S(2)}) collective-permute-start(bf16[2,8,8,256]{3,2,1,0:T(8,128)(2,1)S(1)} %bitcast.31), channel_id=1, source_target_pairs={{0,256},{1,288},{2,320},{3,352},{4,384},{5,416},{6,448},{7,480},{8... | collective-permute-start | bytes 196616 | tf_op jit(solution)/shard_map/ppermute | solution.py:200
  100.8 8.4 %collective-permute-start.4 = (bf16[2,2,8,8,256]{4,3,2,1,0:T(8,128)(2,1)S(1)}, bf16[2,2,8,8,256]{4,3,2,1,0:T(8,128)(2,1)S(1)}, u32[]{:S(2)}, u32[]{:S(2)}) collective-permute-start(bf16[2,2,8,8,256]{4,3,2,1,0:T(8,128)(2,1)S(1)} %pad_maximum_fusion.4), channel_id=1, source_target_pairs={{0,128},{128,0},{1,129},{129,1},{2,130},{130,2},{3,131},{131,3},{4... | collective-permute-start | bytes 393224 | tf_op jit(solution)/shard_map/ppermute | solution.py:171
  109.2 9.5 %collective-permute-start.5 = (bf16[4,2,8,8,256]{4,3,2,1,0:T(8,128)(2,1)S(1)}, bf16[4,2,8,8,256]{4,3,2,1,0:T(8,128)(2,1)S(1)}, u32[]{:S(2)}, u32[]{:S(2)}) collective-permute-start(bf16[4,2,8,8,256]{4,3,2,1,0:T(8,128)(2,1)S(1)} %pad_maximum_fusion.2), channel_id=1, source_target_pairs={{0,64},{64,0},{1,65},{65,1},{2,66},{66,2},{3,67},{67,3},{4,68},{68... | collective-permute-start | bytes 786440 | tf_op jit(solution)/shard_map/ppermute | solution.py:171
  112.3 21.4 %all-to-all-start.3 = ((f16[4,272,128]{2,1,0:T(8,128)(2,1)}), f16[4,272,128]{2,1,0:T(8,128)(2,1)S(1)}, u32[]{:S(2)}, u32[]{:S(2)}) async-start(f16[4,272,128]{2,1,0:T(8,128)(2,1)} %pad_maximum_fusion.1), calls=%async_computation.3 | async-start | bytes 557056 | tf_op jit(solution)/shard_map/all_to_all | solution.py:215
  118.7 3.8 %collective-permute-start.6 = (bf16[8,2,8,8,256]{4,3,2,1,0:T(8,128)(2,1)S(1)}, bf16[8,2,8,8,256]{4,3,2,1,0:T(8,128)(2,1)S(1)}, u32[]{:S(2)}, u32[]{:S(2)}) collective-permute-start(bf16[8,2,8,8,256]{4,3,2,1,0:T(8,128)(2,1)S(1)} %pad_maximum_fusion), channel_id=1, source_target_pairs={{0,32},{32,0},{1,33},{33,1},{2,34},{34,2},{3,35},{35,3},{4,36},{36... | collective-permute-start | bytes 1572872 | tf_op jit(solution)/shard_map/ppermute | solution.py:171
  135.6 18.0 %all-to-all-start.4 = ((f32[16,16,256]{2,1,0:T(8,128)}), f32[16,16,256]{2,1,0:T(8,128)S(1)}, u32[]{:S(2)}, u32[]{:S(2)}) async-start(f32[16,16,256]{2,1,0:T(8,128)} %get-tuple-element.15), calls=%async_computation.4 | async-start | bytes 524288 | tf_op jit(solution)/shard_map/all_to_all | solution.py:219
  145.5 14.7 %collective-permute-start.8 = (bf16[2,8,16,128]{3,2,1,0:T(8,128)(2,1)S(1)}, bf16[2,8,16,128]{3,2,1,0:T(8,128)(2,1)S(1)}, u32[]{:S(2)}, u32[]{:S(2)}) collective-permute-start(bf16[2,8,16,128]{3,2,1,0:T(8,128)(2,1)S(1)} %get-tuple-element.14), channel_id=1, source_target_pairs={{0,1},{1,0},{2,3},{3,2},{4,5},{5,4},{6,7},{7,6},{8,9},{9,8},{10,11... | collective-permute-start | bytes 196616 | tf_op jit(solution)/shard_map/ppermute | solution.py:220
  153.6 14.3 %collective-permute-start.7 = (f32[16,256]{1,0:T(8,128)S(1)}, f32[16,256]{1,0:T(8,128)S(1)}, u32[]{:S(2)}, u32[]{:S(2)}) collective-permute-start(f32[16,256]{1,0:T(8,128)S(1)} %reduce_sum.29.part), channel_id=1, source_target_pairs={{0,16},{16,0},{1,17},{17,1},{2,18},{18,2},{3,19},{19,3},{4,20},{20... | collective-permute-start | bytes 49160 | tf_op jit(solution)/shard_map/ppermute | solution.py:222
  168.7 11.8 %all-to-all-start.5 = ((f32[16,16,256]{2,1,0:T(8,128)}), f32[16,16,256]{2,1,0:T(8,128)S(1)}, u32[]{:S(2)}, u32[]{:S(2)}) async-start(f32[16,16,256]{2,1,0:T(8,128)} %shard_map.63), calls=%async_computation.5 | async-start | bytes 524288 | tf_op jit(solution)/shard_map/all_to_all | solution.py:226
